TPU v7x, 32 devices: a whole 2x2x4 slice. The times are simulated.
32 devices in a mesh: groups: 2 (over y), lists: 4 (over z), sub: 4 (over x, core).
Axes of the slice: x: 2, y: 2, z: 4, core: 2. Of those that a mesh axis runs over, the one named last changes fastest.
Arguments:
- passages: bfloat16 [4096, 1024], P(('groups', 'lists', 'sub')), parts along dimension 0, may hold values from -6 to 6
- rotation: bfloat16 [1024, 1024], replicated, may hold values from -0.1875 to 0.1875
- centroids: bfloat16 [65536, 1024], P('lists', 'sub'), may hold values from -6 to 6
- list_slot: int32 [131072], P('groups'), parts along dimension 0, may hold values from 0 to 65535, as said below
- list_ids: int32 [4096], P(('groups', 'lists', 'sub')), parts along dimension 0, may hold values from 0 to 65535, as said below
- codes: int32 [4096, 128], P(('groups', 'lists', 'sub')), parts along dimension 0, may hold values from 0 to 255
- codebook: bfloat16 [128, 2048], P('sub'), may hold values from -6 to 6
Outputs:
- recon_error: bfloat16 [4096, 1024], P(('groups', 'lists', 'sub')), parts along dimension 0
- new_codebook: float32 [256, 2048], P(('groups', 'sub'), 'lists'), parts along dimension 0
There are 2 independent parts, one for each index of `groups`. A program takes and returns all parts, laid end to end along the dimension named above; an argument that names none is the same for every part. Nothing has to cross between parts.
Inputs may be any that keep to these rules, and one draw needn't show every extreme that they name: `list_slot`: A permutation: every table row holds exactly one list. The owner of passage r is list_slot[list_ids[r]] // 16384. In each aligned block of 128 passages (the passages of one device) no owner gets more than 64; one owner, the same for every block of a slab, gets exactly 64 in every block, and a second owner, drawn per block, gets exactly 64 too.
All inputs are finite; a program needn't handle non-finite values.
Results may differ from a plain program's by a relative error of at most 0.0046.
Values may be sent and summed in bfloat16 or wider, within the bound.
No kernel may reach another device: no remote copies, remote signals or barrier semaphores. Data moves between devices by JAX's collectives and lax.ppermute only.
A program may use at most 128 MiB of HBM per device.

v0:
```python
import jax
import jax.numpy as jnp
from jax import lax
from jax.sharding import PartitionSpec as P


def bucket_places(owner_ids, owner_count, capacity):
    matched = (owner_ids[:, None] == jnp.arange(owner_count, dtype=jnp.int32)[None, :]).astype(
        jnp.int32
    )
    before = jnp.sum(matched * (jnp.cumsum(matched, axis=0) - 1), axis=1)
    return owner_ids * capacity + before


def block_rows_for(row_count, sub_count):
    target = max(8, 8192 // sub_count)
    best = 1
    for size in range(1, min(row_count, target) + 1):
        if row_count % size == 0:
            best = size
    return best


def code_block(rotated_cols, centre_cols, code_cols, live_rows, book_rows):
    row_count, col_width = rotated_cols.shape
    sub_count = code_cols.shape[1]
    sub_width = col_width // sub_count
    word_count = book_rows.shape[1] // sub_width
    residual = (rotated_cols.astype(jnp.float32) - centre_cols.astype(jnp.float32)).astype(
        jnp.bfloat16
    )
    with_ones = jnp.concatenate(
        [
            residual.reshape(row_count, sub_count, sub_width),
            jnp.ones((row_count, sub_count, 1), jnp.bfloat16),
        ],
        axis=2,
    )
    word_ids = jnp.arange(word_count, dtype=jnp.int32)
    step_rows = block_rows_for(row_count, sub_count)
    live_flags = live_rows.astype(jnp.bfloat16)

    def one_block(index, totals):
        start = index * step_rows
        chosen = lax.dynamic_slice_in_dim(code_cols, start, step_rows, 0)
        weights = lax.dynamic_slice_in_dim(live_flags, start, step_rows, 0)
        indicator = (chosen[:, :, None] == word_ids[None, None, :]).astype(jnp.bfloat16) * weights[
            :, None, None
        ]
        values = lax.dynamic_slice_in_dim(with_ones, start, step_rows, 0)
        return totals + jnp.einsum(
            "rmk,rmd->mkd", indicator, values, preferred_element_type=jnp.float32
        )

    totals = lax.fori_loop(
        0,
        row_count // step_rows,
        one_block,
        jnp.zeros((sub_count, word_count, sub_width + 1), jnp.float32),
    )
    code_sums = totals[:, :, :sub_width].reshape(sub_count, word_count * sub_width)
    code_tally = totals[:, :, sub_width]
    word_table = book_rows.astype(jnp.float32).reshape(sub_count, word_count, sub_width)
    picked = word_table[jnp.arange(sub_count, dtype=jnp.int32)[None, :], code_cols]
    rebuilt = (centre_cols.astype(jnp.float32) + picked.reshape(row_count, col_width)).astype(
        jnp.bfloat16
    )
    return (code_sums, code_tally, rebuilt)


def refresh_book(code_sums, code_tally, codebook):
    code_sums, code_tally = (
        lax.psum_scatter(code_sums, "lists", scatter_dimension=1, tiled=True),
        lax.psum_scatter(code_tally, "lists", scatter_dimension=1, tiled=True),
    )
    shard_width = code_sums.shape[1]
    prior_words = lax.dynamic_slice_in_dim(
        codebook, lax.axis_index("lists") * shard_width, shard_width, 1
    ).astype(jnp.float32)
    word_depth = shard_width // code_tally.shape[1]
    return (code_sums + prior_words) / (jnp.repeat(code_tally, word_depth, axis=1) + 1.0)


def body(passages, rotation, centroids, list_slot, list_ids, codes, codebook):
    lists_count = lax.axis_size("lists")
    sub_count = lax.axis_size("sub")
    row_count, model_width = passages.shape
    capacity = 2 * row_count // lists_count
    bucket_total = lists_count * capacity
    lists_held = centroids.shape[0]
    first_list = lax.axis_index("lists") * lists_held
    rotated = jnp.dot(passages, rotation, preferred_element_type=jnp.float32).astype(jnp.bfloat16)
    table_rows = list_slot[list_ids]
    owner_ids = table_rows // lists_held
    places = bucket_places(owner_ids, lists_count, capacity)
    sent_tables = jnp.full((bucket_total,), -1, jnp.int32).at[places].set(table_rows)
    sent_rows = jnp.zeros((bucket_total, model_width), jnp.bfloat16).at[places].set(rotated)
    sent_codes = jnp.zeros((bucket_total, codes.shape[1]), jnp.int32).at[places].set(codes)
    owned_rows, owned_codes, owned_tables = (
        lax.all_to_all(
            sent_rows.reshape(lists_count, capacity, model_width),
            "lists",
            split_axis=0,
            concat_axis=0,
            tiled=True,
        ),
        lax.all_to_all(
            sent_codes.reshape(lists_count, capacity, codes.shape[1]),
            "lists",
            split_axis=0,
            concat_axis=0,
            tiled=True,
        ),
        lax.all_to_all(
            sent_tables.reshape(lists_count, capacity),
            "lists",
            split_axis=0,
            concat_axis=0,
            tiled=True,
        ),
    )
    owned_rows = owned_rows.reshape(bucket_total, model_width)
    owned_codes = owned_codes.reshape(bucket_total, codes.shape[1])
    spread_tables = jnp.broadcast_to(
        owned_tables.reshape(bucket_total, 1), (bucket_total, sub_count)
    )
    block_rows, block_codes, block_tables = (
        lax.all_to_all(owned_rows, "sub", split_axis=1, concat_axis=0, tiled=True),
        lax.all_to_all(owned_codes, "sub", split_axis=1, concat_axis=0, tiled=True),
        lax.all_to_all(spread_tables, "sub", split_axis=1, concat_axis=0, tiled=True),
    )
    block_tables = block_tables[:, 0]
    live_rows = block_tables >= 0
    centre_cols = centroids[jnp.clip(block_tables - first_list, 0, lists_held - 1)]
    code_sums, code_tally, rebuilt = code_block(
        block_rows, centre_cols, block_codes, live_rows, codebook
    )
    owner_rebuilt = lax.all_to_all(rebuilt, "sub", split_axis=0, concat_axis=1, tiled=True)
    returned = lax.all_to_all(
        owner_rebuilt.reshape(lists_count, capacity, model_width),
        "lists",
        split_axis=0,
        concat_axis=0,
        tiled=True,
    )
    rebuilt_rows = returned.reshape(bucket_total, model_width)[places]
    restored = lax.dot_general(
        rebuilt_rows, rotation, (((1,), (1,)), ((), ())), preferred_element_type=jnp.float32
    )
    recon_error = (passages.astype(jnp.float32) - restored).astype(jnp.bfloat16)
    return (recon_error, refresh_book(code_sums, code_tally, codebook))


def solution(mesh):
    return jax.shard_map(
        body,
        mesh=mesh,
        in_specs=(
            P(("groups", "lists", "sub"), None),
            P(),
            P("lists", "sub"),
            P("groups"),
            P(("groups", "lists", "sub")),
            P(("groups", "lists", "sub"), None),
            P("sub", None),
        ),
        out_specs=(P(("groups", "lists", "sub"), None), P(("groups", "sub"), "lists")),
        check_vma=False,
    )
```

profile of v0, /device:TPU:0, one launch (start us, length us, event | category | flops | bytes accessed | tf_op | source)
XLA Modules:
  0.0 666.7 jit_solution(9026332688059564791)
XLA Ops:
  7.2 0.8 compare_select_fusion.3
  8.0 1.9 gather_fusion
  10.0 0.2 reduce_window_sum.11
  10.2 0.2 select_reduce_fusion
  10.3 1.0 scatter_custom_fusion
  11.3 0.7 all_to_all.59
  12.0 6.3 all-to-all-start
  18.3 1.8 scatter_custom_fusion.1
  20.1 3.7 all-to-all-done
  23.8 3.3 all-to-all-start.2
  27.1 0.5 broadcast.254
  27.6 0.7 reduce.5
  28.4 4.6 all-to-all-done.2
  33.0 0.6 broadcast_in_dim.52
  33.6 3.2 all-to-all-start.1
  36.9 1.4 convolution_convert_fusion
  38.3 1.1 copy.33
  39.4 4.3 copy.37
  43.7 2.0 scatter_custom_fusion.2
  45.7 0.1 copy.34
  45.8 0.9 all_to_all.63
  46.7 3.3 all-to-all-start.3
  50.1 4.6 all-to-all-done.3
  54.6 4.1 all-to-all-start.6
  58.8 7.9 %gather_fusion.1 = bf16[1024,256]{1,0:T(8,128)(2,1)S(1)} fusion(bf16[16384,256]{1,0:T(8,128)(2,1)} %param.11, s32[1024]{0:T(1024)S(1)} %broadcast_clamp_fusion), kind=kCustom, calls=%fused_computation.1 | custom fusion | bytes 1052672 | tf_op jit(solution)/shard_map/gather | solution.py:134
  66.8 1.1 convert_element_type.77
  68.0 0.2 copy.36
  68.2 0.2 reshape.238
  68.4 475.9 %gather_fusion.2 = f32[32768,8]{1,0:T(8,128)} fusion(f32[32,256,8]{2,1,0:T(8,128)} %copy.37, s32[32768]{0:T(1024)S(1)} %reshape.238), kind=kCustom, calls=%fused_computation.2 | custom fusion | bytes 2359296 | tf_op jit(solution)/shard_map/gather | solution.py:64
  544.3 13.5 %reshape.211 = f32[4,256,256]{2,1,0:T(8,128)} reshape(f32[32768,8]{1,0:T(8,128)} %gather_fusion.2) | data formatting | bytes 2097152 | tf_op jit(solution)/shard_map/reshape | solution.py:65
  557.8 2.4 add_convert_fusion
  560.3 3.5 all-to-all-start.4
  563.8 2.2 all_to_all.72
  566.0 1.9 copy.40
  567.9 4.7 all-to-all-done.4
  572.6 0.8 copy-done.1
  573.4 3.5 all-to-all-start.7
  576.9 1.2 copy.42
  578.1 1.4 copy.38
  579.5 1.2 reshape.212
  580.7 5.0 all-to-all-done.7
  585.7 4.7 all-to-all-start.5
  590.3 1.1 convert_bitcast_fusion
  591.4 2.6 copy.41
  594.1 2.8 reshape.220
  596.8 1.7 fusion.15
  598.5 1.1 concatenate.7
  599.6 9.4 %while.14 = (s32[]{:T(128)}, f32[32,256,9]{1,2,0:T(8,128)S(1)}, s32[1024,32]{0,1:T(8,128)S(1)}, bf16[1024]{0:T(1024)(128)(2,1)S(1)}, bf16[1024,32,9]{0,2,1:T(8,1...) while((s32[]{:T(128)}, f32[32,256,9]{1,2,0:T(8,128)S(1)}, s32[1024,32]{0,1:T(8,128)S(1)}, ...), condition=%wide.region_6.7_spmd.clone, body=%wide.region_5.6_spmd.clone.sunk | while | flops 42090504 | bytes 951969 | solution.py:55
  599.7 2.3 fusion.38
  602.1 2.3 fusion.38
  604.4 2.3 fusion.38
  606.8 2.3 fusion.38
  609.0 0.2 copy.45
  609.2 0.8 copy.48
  610.1 0.8 constant_dynamic-slice_fusion.1
  610.8 1.4 copy.43
  612.2 0.1 copy.50
  612.4 18.0 %reduce-scatter.7.cloned.1.call-done = f32[64,32]{1,0:T(8,128)} async-done(((f32[256,32]{1,0:T(8,128)}), f32[64,32]{1,0:T(8,128)}) %reduce-scatter.7.cloned.1.call-update) | async-done | bytes 8208
  630.4 0.8 copy.49
  631.3 0.9 gather_fusion.3
  632.2 2.5 fusion.14
  634.6 23.5 %reduce-scatter.5.cloned.1.call-done = f32[32,512]{0,1:T(8,128)} async-done(((f32[32,2048]{0,1:T(8,128)}), f32[32,512]{0,1:T(8,128)}) %reduce-scatter.5.cloned.1.call-update) | async-done | bytes 65552 | tf_op jit(solution)/shard_map/reduce_scatter | solution.py:73
  658.1 1.0 bitcast_divide_fusion
  659.1 0.7 copy.47
  (40 shorter events, 1.0 us)
Async XLA Ops:
  7.2 29.7 %copy-start = (bf16[1024,1024]{1,0:T(8,128)(2,1)S(1)}, bf16[1024,1024]{1,0:T(8,128)(2,1)}, u32[]{:S(2)}) copy-start(bf16[1024,1024]{1,0:T(8,128)(2,1)} %param.10) | copy-start | bytes 6291460
  12.0 11.8 %all-to-all-start = ((s32[4,1,64]{2,1,0:T(1,128)}), s32[4,1,64]{2,1,0:T(1,128)S(1)}, u32[]{:S(2)}, u32[]{:S(2)}) async-start(s32[4,1,64]{2,1,0:T(1,128)} %all_to_all.59), calls=%async_computation | async-start | bytes 4096 | tf_op jit(solution)/shard_map/all_to_all | solution.py:114
  23.8 9.2 %all-to-all-start.2 = ((s32[4,64,128]{2,1,0:T(8,128)}), s32[4,64,128]{2,1,0:T(8,128)S(1)}, u32[]{:S(2)}, u32[]{:S(2)}) async-start(s32[4,64,128]{2,1,0:T(8,128)} %bitcast.9), calls=%async_computation.2 | async-start | bytes 262144 | tf_op jit(solution)/shard_map/all_to_all | solution.py:107
  33.6 13.1 %all-to-all-start.1 = ((s32[256,4,1]{0,2,1:T(1,128)}), s32[256,4,1]{0,2,1:T(1,128)S(1)}, u32[]{:S(2)}, u32[]{:S(2)}) async-start(s32[256,4,1]{0,2,1:T(1,128)} %broadcast_in_dim.52), calls=%async_computation.1 | async-start | bytes 8192 | tf_op jit(solution)/shard_map/all_to_all | solution.py:130
  46.7 7.9 %all-to-all-start.3 = ((s32[256,4,32]{0,2,1:T(8,128)}), s32[256,4,32]{0,2,1:T(8,128)S(1)}, u32[]{:S(2)}, u32[]{:S(2)}) async-start(s32[256,4,32]{0,2,1:T(8,128)} %all_to_all.63), calls=%async_computation.3 | async-start | bytes 262144 | tf_op jit(solution)/shard_map/all_to_all | solution.py:129
  54.6 505.6 %all-to-all-start.6 = ((bf16[4,64,1024]{2,1,0:T(8,128)(2,1)}), bf16[4,64,1024]{2,1,0:T(8,128)(2,1)}, u32[]{:S(2)}, u32[]{:S(2)}) async-start(bf16[4,64,1024]{2,1,0:T(8,128)(2,1)} %bitcast.14), calls=%async_computation.6 | async-start | bytes 1048576 | tf_op jit(solution)/shard_map/all_to_all | solution.py:100
  560.3 12.3 %all-to-all-start.4 = ((bf16[4,256,256]{2,1,0:T(8,128)(2,1)}), bf16[4,256,256]{2,1,0:T(8,128)(2,1)S(1)}, u32[]{:S(2)}, u32[]{:S(2)}) async-start(bf16[4,256,256]{2,1,0:T(8,128)(2,1)} %add_convert_fusion), calls=%async_computation.4 | async-start | bytes 1048576 | tf_op jit(solution)/shard_map/all_to_all | solution.py:138
  572.6 0.8 copy-start.1
  573.4 12.3 %all-to-all-start.7 = ((bf16[256,4,256]{2,0,1:T(8,128)(2,1)}), bf16[256,4,256]{2,0,1:T(8,128)(2,1)S(1)}, u32[]{:S(2)}, u32[]{:S(2)}) async-start(bf16[256,4,256]{2,0,1:T(8,128)(2,1)} %copy.40), calls=%async_computation.7 | async-start | bytes 1048576 | tf_op jit(solution)/shard_map/all_to_all | solution.py:128
  585.7 45.6 %all-to-all-start.5 = ((bf16[4,64,1024]{2,1,0:T(8,128)(2,1)}), bf16[4,64,1024]{2,1,0:T(8,128)(2,1)S(1)}, u32[]{:S(2)}, u32[]{:S(2)}) async-start(bf16[4,64,1024]{2,1,0:T(8,128)(2,1)} %reshape.212), calls=%async_computation.5 | async-start | bytes 1048576 | tf_op jit(solution)/shard_map/all_to_all | solution.py:139
  590.3 40.0 %reduce-scatter.7.cloned.1.call-start = ((), (), s32[]{:S(2)}) async-start(), calls=%async_computation.11 | async-start | bytes 163840
  591.4 8.2 %copy-start.2 = (f32[32,256,9]{1,2,0:T(8,128)S(1)}, f32[32,256,9]{1,2,0:T(8,128)}, u32[]{:S(2)}) copy-start(f32[32,256,9]{1,2,0:T(8,128)} %custom-call.2) | copy-start | bytes 884740
  610.0 48.1 %reduce-scatter.5.cloned.1.call-start = ((), (), s32[]{:S(2)}) async-start(), calls=%async_computation.10 | async-start | bytes 1310720 | tf_op jit(solution)/shard_map/reduce_scatter | solution.py:73
Sparse Core Ops, SparseCore 0:
  610.1 20.1 reduce-scatter.6
  632.8 25.3 reduce-scatter.4
where the time goes:
time: 671 us; the launch traced here: 667 us
  local copies, waits for them, and re-layouts  534 us (80%)
  waiting for transfers between devices  64 us (10%)
  starting transfers between devices  32 us (5%)
  between operations  14.3 us (2%)
  matrix products  12.9 us (2%)
  other arithmetic  9.29 us (1%)
    gather x1, local copies, waits for them, and re-layouts, code_block(): word_table[jnp.arange(sub_count, dtype=jnp.int32)[None, :], code_cols]  476 us
    reduce_scatter x1, waiting for transfers between devices, refresh_book(): lax.psum_scatter(code_sums, 'lists', scatter_dimension=1, tiled=True)  23.5 us
    unnamed x3, waiting for transfers between devices  18 us
    reshape x1, local copies, waits for them, and re-layouts, code_block(): picked.reshape(row_count, col_width)  13.5 us
  transfers between devices with their start and end apart: 10, of which 7 were waited for; matrix products, arithmetic and copies ran while one was open for 82% of the time, Pallas kernels for 0%

commit v1 on v0

v1 whole, which is shorter than its diff:
```python
import functools

import jax
import jax.numpy as jnp
from jax import lax
from jax.experimental import pallas as pl
from jax.experimental.pallas import tpu as pltpu
from jax.sharding import PartitionSpec as P

BF16 = jnp.bfloat16
F32 = jnp.float32
VMEM_LIMIT = 48 * 1024 * 1024
DIRECT_LISTS = 4


def call(kernel, out_shape, flops, nbytes, *args):
    whole = lambda: pl.BlockSpec(memory_space=pltpu.VMEM)
    return pl.pallas_call(
        kernel,
        out_shape=out_shape,
        in_specs=[whole() for _ in args],
        out_specs=jax.tree.map(lambda _: whole(), out_shape),
        compiler_params=pltpu.CompilerParams(vmem_limit_bytes=VMEM_LIMIT),
        cost_estimate=pl.CostEstimate(flops=flops, bytes_accessed=nbytes, transcendentals=0),
    )(*args)


def strict_before(width):
    row = lax.broadcasted_iota(jnp.int32, (width, width), 0)
    col = lax.broadcasted_iota(jnp.int32, (width, width), 1)
    return (row < col).astype(F32).astype(BF16)


def rotate_kernel(subs, passages_ref, rotation_ref, codes_ref, out_ref):
    rows, model = passages_ref.shape
    width = model // subs
    spaces = codes_ref.shape[1] // subs
    halves = width // rows
    tail = spaces // halves
    codes_t = jnp.transpose(codes_ref[...].astype(F32)).astype(BF16)
    for at in range(subs):
        out_ref[at, :rows, :] = jnp.dot(
            passages_ref[...],
            rotation_ref[:, at * width : (at + 1) * width],
            preferred_element_type=F32,
        ).astype(BF16)
        for half in range(halves):
            start = at * spaces + half * tail
            out_ref[at, rows:, half * rows : (half + 1) * rows] = codes_t[start : start + tail]


def slots_kernel(held, lists, direct, rows_ref, *outs):
    blocks, rows = rows_ref.shape
    me = lax.axis_index("lists")
    subs = blocks // lists
    cap = outs[0].shape[1]
    local = rows_ref[...] - me * held
    mine = jnp.logical_and(local >= 0, local < held)
    flags = mine.astype(F32)
    rank = jnp.dot(flags.astype(BF16), strict_before(rows), preferred_element_type=F32)
    rank = jnp.where(mine, rank, -1.0)
    local = jnp.where(mine, local, 0)
    high = (local // 128).astype(F32)
    low = (local % 128).astype(F32)
    slot = lax.broadcasted_iota(jnp.int32, (cap, rows), 0).astype(F32)
    for block in range(blocks):
        chosen = (slot == rank[block : block + 1, :]).astype(F32).astype(BF16)
        pair = jnp.concatenate(
            [
                jnp.broadcast_to(high[block : block + 1, :], (8, rows)),
                jnp.broadcast_to(low[block : block + 1, :], (8, rows)),
            ],
            axis=0,
        ).astype(BF16)
        found = lax.dot_general(
            pair, chosen, (((1,), (1,)), ((), ())), preferred_element_type=F32
        )
        row = (found[0:1, :] * 128.0 + found[8:9, :]).astype(jnp.int32)
        if direct:
            place = (block // subs) ^ me
            for step in range(lists):

                @pl.when(place == step)
                def _():
                    outs[step][block % subs : block % subs + 1, :] = row
        else:
            outs[0][block : block + 1, :] = row


def lookup_kernel(held, lists, direct, cap, rows_ref, message_ref, words_ref, picked_ref, slot_ref, codes_ref, tally_ref):
    subs, _, width = message_ref.shape
    rows = rows_ref.shape[1]
    spaces = codes_ref.shape[0]
    depth = width // spaces
    words = words_ref.shape[1]
    halves = width // rows
    tail = spaces // halves
    me = lax.axis_index("lists")
    tables = rows_ref[pl.ds(pl.multiple_of(me * subs, subs), subs), :]
    owners = tables // held
    rank = jnp.zeros((subs, rows), F32)
    flags = [(owners == at).astype(F32) for at in range(lists)]
    stacked = jnp.concatenate(flags, axis=0)
    before = jnp.dot(stacked.astype(BF16), strict_before(rows), preferred_element_type=F32)
    for at in range(lists):
        rank = rank + flags[at] * before[at * subs : (at + 1) * subs]
    place = (owners ^ me) if direct else owners
    slot = place.astype(F32) * cap + rank
    slot_ref[...] = jnp.transpose(jnp.concatenate([slot] * (rows // subs), axis=0))
    for at in range(subs):
        for half in range(halves):
            codes_ref[half * tail : (half + 1) * tail, at * rows : (at + 1) * rows] = message_ref[
                at, rows:, half * rows : (half + 1) * rows
            ].astype(F32)
    parts = []
    for space in range(spaces):
        line = codes_ref[space : space + 1, :].astype(jnp.int32)
        table = words_ref[space * depth : (space + 1) * depth, :]
        cells = []
        for at in range(subs):
            index = jnp.broadcast_to(line[:, at * rows : (at + 1) * rows], (depth, rows))
            value = None
            for piece in range(words // 128):
                got = jnp.take_along_axis(
                    table[:, piece * 128 : (piece + 1) * 128], index & 127, axis=1
                )
                value = got if value is None else jnp.where(index >= piece * 128, got, value)
            cells.append(value)
        parts.append(jnp.concatenate(cells, axis=1))
    picked_ref[...] = jnp.transpose(jnp.concatenate(parts, axis=0)).astype(BF16)
    tally = jnp.zeros((words, 128), F32)
    word = lax.broadcasted_iota(jnp.int32, (words, subs * rows), 0).astype(F32)
    lane = lax.broadcasted_iota(jnp.int32, (subs * rows, 128), 1)
    for space in range(spaces):
        hot = (word == codes_ref[space : space + 1, :]).astype(F32).astype(BF16)
        tally = tally + jnp.dot(
            hot, (lane == space).astype(F32).astype(BF16), preferred_element_type=F32
        )
    tally_ref[...] = tally.astype(BF16)


def place_kernel(own, slot_ref, message_ref, picked_ref, *refs):
    pieces, (rebuilt_ref, residual_ref) = refs[:-2], refs[-2:]
    subs, _, width = message_ref.shape
    rows = slot_ref.shape[0]
    total = sum(piece.shape[1] for piece in pieces)
    column = lax.broadcasted_iota(jnp.int32, (rows, total), 1).astype(F32)
    for at in range(subs):
        chosen = (column == slot_ref[:, at : at + 1]).astype(F32).astype(BF16)
        centre = jnp.zeros((rows, width), F32)
        start = 0
        stacked = jnp.concatenate([piece[at] for piece in pieces], axis=0)
        centre = jnp.dot(chosen, stacked, preferred_element_type=F32)
        span = slice(at * rows, (at + 1) * rows)
        rebuilt_ref[at] = (centre + picked_ref[span, :].astype(F32)).astype(BF16)
        residual_ref[span, :] = (message_ref[at, :rows, :].astype(F32) - centre).astype(BF16)


def sums_kernel(lists, codes_ref, residual_ref, tally_ref, out_ref):
    spaces, rows = codes_ref.shape
    width = residual_ref.shape[1]
    words = tally_ref.shape[0]
    depth = width // spaces
    share = words // lists
    word = lax.broadcasted_iota(jnp.int32, (words, rows), 0).astype(F32)
    owner = lax.broadcasted_iota(jnp.int32, (rows, width), 1) // depth
    residual = residual_ref[...]
    total = jnp.zeros((words, width), F32)
    for space in range(spaces):
        hot = (word == codes_ref[space : space + 1, :]).astype(F32).astype(BF16)
        part = jnp.where(owner == space, residual, jnp.zeros_like(residual))
        total = total + jnp.dot(hot, part, preferred_element_type=F32)
    total = total.astype(BF16)
    tally = tally_ref[...]
    for at in range(lists):
        out_ref[at, :, :width] = total[at * share : (at + 1) * share]
        out_ref[at, :, width:] = tally[at * share : (at + 1) * share]


def refine_kernel(spaces, direct, codebook_ref, *refs):
    pieces, (out_ref, turned_ref) = refs[:-2], refs[-2:]
    total = None
    for piece in pieces:
        if direct:
            value = piece[...].astype(F32)
        else:
            value = jnp.sum(piece[...].astype(F32), axis=0)
        total = value if total is None else total + value
    share = total.shape[0]
    width = total.shape[1] - 128
    depth = width // spaces
    span = share * depth
    turned = jnp.transpose(total)
    turned_ref[...] = turned[:width, :]
    tally = turned[width : width + spaces, :]
    word = lax.broadcasted_iota(jnp.int32, (share, span), 0)
    cell = lax.broadcasted_iota(jnp.int32, (share, span), 1)

    def spread(value, table):
        high = value.astype(BF16)
        rest = value - high.astype(F32)
        low = rest.astype(BF16)
        return jnp.dot(high, table, preferred_element_type=F32) + jnp.dot(
            low, table, preferred_element_type=F32
        )

    sums = jnp.zeros((spaces, span), F32)
    for at in range(depth):
        table = (cell == word * depth + at).astype(F32).astype(BF16)
        sums = sums + spread(turned_ref[pl.ds(at, spaces, stride=depth), :], table)
    counts = spread(tally, (cell // depth == word).astype(F32).astype(BF16))
    me = lax.axis_index("lists")
    if span % 128 == 0:
        prior = codebook_ref[:, pl.ds(pl.multiple_of(me * span, span), span)].astype(F32)
    else:
        prior = jnp.zeros((spaces, span), F32)
        for at in range(codebook_ref.shape[1] // span):
            block = codebook_ref[:, at * span : (at + 1) * span].astype(F32)
            prior = prior + jnp.where(me == at, block, 0.0)
    out_ref[...] = (sums + prior) / (counts + 1.0)


def restore_kernel(direct, passages_ref, rotation_ref, *refs):
    pieces, out_ref = refs[:-1], refs[-1]
    me = lax.axis_index("sub")
    if direct:
        blocks = [piece[...] for piece in pieces]
    else:
        blocks = [pieces[0][at] for at in range(pieces[0].shape[0])]
    width = blocks[0].shape[1]
    total = None
    for at, block in enumerate(blocks):
        start = (me ^ at) * width if direct else at * width
        if direct:
            start = pl.multiple_of(start, width)
        value = lax.dot_general(
            block,
            rotation_ref[:, pl.ds(start, width)],
            (((1,), (1,)), ((), ())),
            preferred_element_type=F32,
        )
        total = value if total is None else total + value
    out_ref[...] = (passages_ref[...].astype(F32) - total).astype(BF16)


def swap(value, axis, step):
    count = lax.axis_size(axis)
    return lax.ppermute(value, axis, [(at, at ^ step) for at in range(count)])


def pick(value, index):
    return lax.dynamic_index_in_dim(value, index, 0, keepdims=False)


def body(passages, rotation, centroids, list_slot, list_ids, codes, codebook):
    lists = lax.axis_size("lists")
    subs = lax.axis_size("sub")
    rows, model = passages.shape
    held, width = centroids.shape
    cap = 2 * rows // lists
    spaces = codebook.shape[0]
    depth = width // spaces
    words = codebook.shape[1] // depth
    share = words // lists
    direct = lists <= DIRECT_LISTS
    me_list = lax.axis_index("lists")
    me_sub = lax.axis_index("sub")
    shape = jax.ShapeDtypeStruct

    tables = list_slot.at[list_ids].get(mode="promise_in_bounds")
    tables = lax.all_to_all(
        jnp.broadcast_to(tables[None, None, :], (lists * subs, 1, rows)),
        ("lists", "sub"),
        split_axis=0,
        concat_axis=0,
        tiled=True,
    ).reshape(lists * subs, rows)

    halves = width // rows
    message = call(
        functools.partial(rotate_kernel, subs),
        shape((subs, rows + spaces // halves, width), BF16),
        2 * rows * model * model,
        2 * model * model + 4 * rows * model,
        passages,
        rotation,
        codes,
    )
    message = lax.all_to_all(message, "sub", split_axis=0, concat_axis=0, tiled=True)

    idx = call(
        functools.partial(slots_kernel, held, lists, direct),
        [shape((subs, cap), jnp.int32)] * lists if direct else [shape((lists * subs, cap), jnp.int32)],
        10_000_000,
        100_000,
        tables,
    )
    fetch = lambda at: centroids.at[at].get(mode="promise_in_bounds")
    if direct:
        pieces = [fetch(idx[0])] + [
            swap(fetch(idx[step]), "lists", step) for step in range(1, lists)
        ]
    else:
        found = lax.all_to_all(
            fetch(idx[0]).reshape(lists, subs * cap, width), "lists", 0, 0, tiled=True
        )
        found = found.reshape(lists, subs, cap, width)
        pieces = [jnp.swapaxes(found, 0, 1).reshape(subs, lists * cap, width)]

    word_table = (
        codebook.astype(F32).reshape(spaces, words, depth).transpose(0, 2, 1).reshape(width, words)
    )
    picked, slot, codes_t, tally = call(
        functools.partial(lookup_kernel, held, lists, direct, cap),
        [
            shape((subs * rows, width), BF16),
            shape((rows, rows), F32),
            shape((spaces, subs * rows), F32),
            shape((words, 128), BF16),
        ],
        1_000_000_000,
        2_000_000,
        tables,
        message,
        word_table,
    )
    rebuilt, residual = call(
        functools.partial(place_kernel, me_list),
        [shape((subs, rows, width), BF16), shape((subs * rows, width), BF16)],
        300_000_000,
        2_000_000,
        slot,
        message,
        picked,
        *pieces,
    )
    if subs <= DIRECT_LISTS:
        rebuilt = [pick(rebuilt, me_sub)] + [
            swap(pick(rebuilt, me_sub ^ step), "sub", step) for step in range(1, subs)
        ]
    else:
        rebuilt = [lax.all_to_all(rebuilt, "sub", 0, 0, tiled=True)]
    sums = call(
        functools.partial(sums_kernel, lists),
        shape((lists, share, width + 128), BF16),
        2_000_000_000,
        1_000_000,
        codes_t,
        residual,
        tally,
    )
    if direct:
        sums = [pick(sums, me_list)] + [
            swap(pick(sums, me_list ^ step), "lists", step) for step in range(1, lists)
        ]
    else:
        sums = [lax.all_to_all(sums, "lists", 0, 0, tiled=True)]
    recon_error = call(
        functools.partial(restore_kernel, subs <= DIRECT_LISTS),
        shape((rows, model), BF16),
        2 * rows * model * model,
        2 * model * model + 4 * rows * model,
        passages,
        rotation,
        *rebuilt,
    )
    new_codebook = pl.pallas_call(
        functools.partial(refine_kernel, spaces, direct),
        out_shape=shape((spaces, share * depth), F32),
        in_specs=[pl.BlockSpec(memory_space=pltpu.VMEM)] * (1 + len(sums)),
        out_specs=pl.BlockSpec(memory_space=pltpu.VMEM),
        scratch_shapes=[pltpu.VMEM((width, share), F32)],
        compiler_params=pltpu.CompilerParams(vmem_limit_bytes=VMEM_LIMIT),
        cost_estimate=pl.CostEstimate(flops=100_000_000, bytes_accessed=500_000, transcendentals=0),
    )(codebook, *sums)
    return (recon_error, new_codebook)


def solution(mesh):
    return jax.shard_map(
        body,
        mesh=mesh,
        in_specs=(
            P(("groups", "lists", "sub"), None),
            P(),
            P("lists", "sub"),
            P("groups"),
            P(("groups", "lists", "sub")),
            P(("groups", "lists", "sub"), None),
            P("sub", None),
        ),
        out_specs=(P(("groups", "lists", "sub"), None), P(("groups", "sub"), "lists")),
        check_vma=False,
    )
```

time: 671 us -> 73 us (0.11)
  local copies, waits for them, and re-layouts: 534 us -> 31.1 us
  waiting for transfers between devices: 64 us -> 4.81 us
  between operations: 14.3 us -> 0.87 us
  matrix products: 12.9 us -> 0 us
  Pallas kernels: 0 us -> 12.1 us
  starting transfers between devices: 32 us -> 22.8 us
  other arithmetic: 9.29 us -> 0.75 us
    gather x4 -> x5, local copies, waits for them, and re-layouts: 487 us -> 25 us  [the longest x4 23.8 us: body(): fetch = lambda at: centroids.at[at].get(mode='promise_in_bounds')]
    reduce_scatter x1 -> x0, waiting for transfers between devices: 23.5 us -> none  [refresh_book(): lax.psum_scatter(code_sums, 'lists', scatter_dimension=1, tiled=True)]
    all_to_all x8 -> x2, waiting for transfers between devices: 22.5 us -> 0.2 us  [the longest x1 0.2 us: body(): lax.all_to_all(jnp.broadcast_to(tables[None, None, :], (lists * subs, 1,...]
    all_to_all x8 -> x2, starting transfers between devices: 32 us -> 10.8 us  [the longest x1 7.36 us: body(): lax.all_to_all(jnp.broadcast_to(tables[None, None, :], (lists * subs, 1,...]
    reshape x4 -> x2, local copies, waits for them, and re-layouts: 20.2 us -> 1.5 us  [body(): codebook.astype(F32).reshape(spaces, words, depth).transpose(0, 2, 1)]
    unnamed x3 -> x0, waiting for transfers between devices: 18 us -> none
    dot_general x6 -> x0, matrix products: 12.9 us -> none  [the longest x4 9.01 us: one_block(): jnp.einsum('rmk,rmd->mkd', indicator, values, preferred_element_type=jnp....]
    pallas_call x0 -> x7, Pallas kernels: none -> 12.1 us  [the longest x6 11 us: call(): pl.pallas_call(kernel, out_shape=out_shape, in_specs=[whole() for _ in ar...]
  transfers between devices with their start and end apart: 10 -> 11, of which waited for: 7 -> 3; matrix products, arithmetic and copies ran while one was open for 82% -> 35% of each run, Pallas kernels for 0% -> 10%
where the time goes in v1:
time: 73 us; the launch traced here: 72.5 us
  local copies, waits for them, and re-layouts  31.1 us (43%)
  starting transfers between devices  22.8 us (31%)
  Pallas kernels  12.1 us (17%)
  waiting for transfers between devices  4.81 us (7%)
  between operations  0.87 us (1%)
  other arithmetic  0.75 us (1%)
    gather x4, local copies, waits for them, and re-layouts, body(): fetch = lambda at: centroids.at[at].get(mode='promise_in_bounds')  23.8 us
    ppermute x9, starting transfers between devices, swap(): return lax.ppermute(value, axis, [(at, at ^ step) for at in range(count)])  12 us
    pallas_call x6, Pallas kernels, call(): pl.pallas_call(kernel, out_shape=out_shape, in_specs=[whole() for _ in ar...  11 us
    all_to_all x1, starting transfers between devices, body(): lax.all_to_all(jnp.broadcast_to(tables[None, None, :], (lists * subs, 1,...  7.36 us
    ppermute x9, waiting for transfers between devices, swap(): return lax.ppermute(value, axis, [(at, at ^ step) for at in range(count)])  4.61 us
    unnamed x14, local copies, waits for them, and re-layouts  3.64 us
    all_to_all x1, starting transfers between devices, body(): lax.all_to_all(message, 'sub', split_axis=0, concat_axis=0, tiled=True)  3.45 us
    reshape x2, local copies, waits for them, and re-layouts, body(): codebook.astype(F32).reshape(spaces, words, depth).transpose(0, 2, 1)  1.5 us
  transfers between devices with their start and end apart: 11, of which 3 were waited for; matrix products, arithmetic and copies ran while one was open for 35% of the time, Pallas kernels for 10%

profile of v1, /device:TPU:0, one launch (start us, length us, event | category | flops | bytes accessed | tf_op | source)
XLA Modules:
  0.0 72.5 jit_solution(7400038825037568579)
XLA Ops:
  0.6 0.0 copy-start
  0.6 0.7 compare_select_fusion.4
  1.4 0.2 copy-done
  1.6 1.1 %gather_fusion = s32[128]{0:T(128)S(1)} fusion(s32[65536]{0:T(1024)S(1)} %copy-done, s32[1024]{0:T(1024)S(1)} %pad_clamp_fusion.4), kind=kCustom, calls=%fused_computation | custom fusion | bytes 1536 | tf_op jit(solution)/shard_map/gather | solution.py:270
  2.8 0.6 broadcast_in_dim.22
  3.4 7.4 %all-to-all-start = ((s32[16,1,128]{2,1,0:T(1,128)}), s32[16,1,128]{2,1,0:T(1,128)S(1)}, u32[]{:S(2)}, u32[]{:S(2)}) async-start(s32[16,1,128]{2,1,0:T(1,128)} %broadcast_in_dim.22), calls=%async_computation | async-start | bytes 16384 | tf_op jit(solution)/shard_map/all_to_all | solution.py:271
  10.8 1.1 %copy.12 = f32[32,2048]{0,1:T(8,128)S(1)} copy(bf16[32,2048]{1,0:T(8,128)(2,1)} %codebook_ref.1) | data formatting | bytes 393216 | tf_op jit(solution)/shard_map/reshape | solution.py:311
  11.9 0.4 copy.13
  12.3 0.0 copy-start.1
  12.3 1.6 %copy-done.1 = bf16[1024,1024]{1,0:T(8,128)(2,1)S(1)} copy-done((bf16[1024,1024]{1,0:T(8,128)(2,1)S(1)}, bf16[1024,1024]{1,0:T(8,128)(2,1)}, u32[]{:S(2)}) %copy-start.1) | copy-done | bytes 2097176
  13.9 0.0 copy-start.3
  13.9 0.9 %copy-done.3 = bf16[128,1024]{1,0:T(8,128)(2,1)S(1)} copy-done((bf16[128,1024]{1,0:T(8,128)(2,1)S(1)}, bf16[128,1024]{1,0:T(8,128)(2,1)}, u32[]{:S(2)}) %copy-start.3) | copy-done | bytes 262168
  14.8 0.0 copy-start.6
  14.9 0.8 %copy-done.6 = s32[128,128]{1,0:T(8,128)S(1)} copy-done((s32[128,128]{1,0:T(8,128)S(1)}, s32[128,128]{1,0:T(8,128)}, u32[]{:S(2)}) %copy-start.6) | copy-done | bytes 65560
  15.7 1.2 %shard_map.86 = bf16[4,144,256]{2,1,0:T(8,128)(2,1)} custom-call(bf16[128,1024]{1,0:T(8,128)(2,1)S(1)} %copy-done.3, bf16[1024,1024]{1,0:T(8,128)(2,1)S(1)} %copy-done.1, s32[128,128]{1,0:T(8,128)S(1)} %copy-done.6), custom_call_target="tpu_custom_call" | custom-call | flops 268435456 | bytes 2621440 | tf_op jit(solution)/shard_map/pallas_call | solution.py:18
  16.9 0.2 all-to-all-done
  17.1 3.5 %all-to-all-start.1 = ((bf16[4,144,256]{2,1,0:T(8,128)(2,1)}), bf16[4,144,256]{2,1,0:T(8,128)(2,1)S(1)}, u32[]{:S(2)}, u32[]{:S(2)}) async-start(bf16[4,144,256]{2,1,0:T(8,128)(2,1)} %shard_map.86), calls=%async_computation.1 | async-start | bytes 589824 | tf_op jit(solution)/shard_map/all_to_all | solution.py:289
  20.5 2.3 %shard_map.88 = (s32[4,64]{1,0:T(4,128)S(1)}, s32[4,64]{1,0:T(4,128)S(1)}, s32[4,64]{1,0:T(4,128)S(1)}, s32[4,64]{1,0:T(4,128)S(1)}) custom-call(s32[16,128]{1,0:T(8,128)S(1)} %bitcast.27), custom_call_target="tpu_custom_call" | custom-call | flops 10000000 | bytes 100000 | tf_op jit(solution)/shard_map/pallas_call | solution.py:18
  22.8 0.1 reshape.38
  22.9 0.1 reshape.46
  23.0 6.1 %gather_fusion.2 = bf16[256,256]{1,0:T(8,128)(2,1)} fusion(bf16[16384,256]{1,0:T(8,128)(2,1)} %param.9, s32[1024]{0:T(1024)S(1)} %pad_clamp_fusion.2), kind=kCustom, calls=%fused_computation.2 | custom fusion | bytes 263168 | tf_op jit(solution)/shard_map/gather | solution.py:298
  29.1 1.7 %collective-permute-start = (bf16[4,64,256]{2,1,0:T(8,128)(2,1)}, bf16[4,64,256]{2,1,0:T(8,128)(2,1)}, u32[]{:S(2)}, u32[]{:S(2)}) collective-permute-start(bf16[4,64,256]{2,1,0:T(8,128)(2,1)} %bitcast.5), channel_id=1, source_target_pairs={{0,4},{4,0},{8,12},{12,8},{1,5},{5,1},{9,13},{13,9},{2,6},{6,2},{1... | collective-permute-start | bytes 393224 | tf_op jit(solution)/shard_map/ppermute | solution.py:248
  30.8 0.0 copy-start.5
  30.8 0.1 reshape.54
  30.9 0.0 copy-start.2
  30.9 0.0 copy-start.4
  30.9 6.2 %gather_fusion.3 = bf16[256,256]{1,0:T(8,128)(2,1)} fusion(bf16[16384,256]{1,0:T(8,128)(2,1)} %param.9, s32[1024]{0:T(1024)S(1)} %pad_clamp_fusion.1), kind=kCustom, calls=%fused_computation.3 | custom fusion | bytes 263168 | tf_op jit(solution)/shard_map/gather | solution.py:298
  37.1 2.4 %collective-permute-start.1 = (bf16[4,64,256]{2,1,0:T(8,128)(2,1)}, bf16[4,64,256]{2,1,0:T(8,128)(2,1)}, u32[]{:S(2)}, u32[]{:S(2)}) collective-permute-start(bf16[4,64,256]{2,1,0:T(8,128)(2,1)} %bitcast.6), channel_id=1, source_target_pairs={{0,8},{4,12},{8,0},{12,4},{1,9},{5,13},{9,1},{13,5},{2,10},{6,14},... | collective-permute-start | bytes 393224 | tf_op jit(solution)/shard_map/ppermute | solution.py:248
  39.5 0.1 reshape.62
  39.6 6.1 %gather_fusion.4 = bf16[256,256]{1,0:T(8,128)(2,1)} fusion(bf16[16384,256]{1,0:T(8,128)(2,1)} %param.9, s32[1024]{0:T(1024)S(1)} %pad_clamp_fusion), kind=kCustom, calls=%fused_computation.4 | custom fusion | bytes 263168 | tf_op jit(solution)/shard_map/gather | solution.py:298
  45.7 0.3 collective-permute-start.2
  46.0 5.4 %gather_fusion.1 = bf16[256,256]{1,0:T(8,128)(2,1)S(1)} fusion(bf16[16384,256]{1,0:T(8,128)(2,1)} %param.9, s32[1024]{0:T(1024)S(1)} %pad_clamp_fusion.3), kind=kCustom, calls=%fused_computation.1 | custom fusion | bytes 263168 | tf_op jit(solution)/shard_map/gather | solution.py:298
  51.4 0.0 all-to-all-done.1.message_ref
  51.4 2.4 %shard_map.87 = (bf16[512,256]{1,0:T(8,128)(2,1)S(1)}, f32[128,128]{1,0:T(8,128)S(1)}, f32[32,512]{1,0:T(8,128)S(1)}, bf16[256,128]{1,0:T(8,128)(2,1)S(1)}) custom-call(s32[16,128]{1,0:T(8,128)S(1)} %bitcast.28, bf16[4,144,256]{2,1,0:T(8,128)(2,1)S(1)} %all-to-all-done.1.message_ref, f32[256,256]{1,0:T(8,128)S(1)} %bitcast.26), custom_call_target="tpu_custom_call" | custom-call | flops 1000000000 | bytes 2000000 | tf_op jit(solution)/shard_map/pallas_call | solution.py:18
  53.8 0.0 collective-permute-done.refs_1_
  53.8 0.0 collective-permute-done.1.refs_2_
  53.8 0.0 collective-permute-done.2.refs_3_
  53.8 1.3 %shard_map.89 = (bf16[4,128,256]{2,1,0:T(8,128)(2,1)S(1)}, bf16[512,256]{1,0:T(8,128)(2,1)S(1)}) custom-call(f32[128,128]{1,0:T(8,128)S(1)} %get-tuple-element.12.slot_ref, bf16[4,144,256]{2,1,0:T(8,128)(2,1)S(1)} %all-to-all-done.1.message_ref, bf16[512,256]{1,0:T(8,128)(2,1)S(1)} %get-tuple-element.13.picked_ref, bf16[4,64,256]{2,1,0:T(8,128)(2,1)S(1)} %bitcast.25, ...), custom_call_target="tpu_custom_call" | custom-call | flops 300000000 | bytes 2000000 | tf_op jit(solution)/shard_map/pallas_call | solution.py:18
  55.2 2.3 %shard_map.91 = bf16[4,64,384]{2,1,0:T(8,128)(2,1)S(1)} custom-call(f32[32,512]{1,0:T(8,128)S(1)} %get-tuple-element.19.codes_ref, bf16[512,256]{1,0:T(8,128)(2,1)S(1)} %get-tuple-element.20.residual_ref, bf16[256,128]{1,0:T(8,128)(2,1)S(1)} %get-tuple-element.21.tally_ref), custom_call_target="tpu_custom_call" | custom-call | flops 2000000000 | bytes 1000000 | tf_op jit(solution)/shard_map/pallas_call | solution.py:18
  57.6 0.9 %collective-permute-start.6 = (bf16[64,384]{1,0:T(8,128)(2,1)S(1)}, bf16[64,384]{1,0:T(8,128)(2,1)S(1)}, u32[]{:S(2)}, u32[]{:S(2)}) collective-permute-start(bf16[64,384]{1,0:T(8,128)(2,1)S(1)} %get-tuple-element.28), channel_id=1, source_target_pairs={{0,4},{4,0},{8,12},{12,8},{1,5},{5,1},{9,13},{13,9},{2,6},{6,2},{1... | collective-permute-start | bytes 147464 | tf_op jit(solution)/shard_map/ppermute | solution.py:248
  58.4 0.1 collective-permute-start.3
  58.5 2.0 %collective-permute-start.4 = (bf16[128,256]{1,0:T(8,128)(2,1)S(1)}, bf16[128,256]{1,0:T(8,128)(2,1)S(1)}, u32[]{:S(2)}, u32[]{:S(2)}) collective-permute-start(bf16[128,256]{1,0:T(8,128)(2,1)S(1)} %get-tuple-element.23), channel_id=1, source_target_pairs={{0,2},{1,3},{2,0},{3,1},{4,6},{5,7},{6,4},{7,5},{8,10},{9,11},{10,... | collective-permute-start | bytes 196616 | tf_op jit(solution)/shard_map/ppermute | solution.py:248
  60.6 0.1 collective-permute-start.5
  60.6 3.3 %collective-permute-start.7 = (bf16[64,384]{1,0:T(8,128)(2,1)S(1)}, bf16[64,384]{1,0:T(8,128)(2,1)S(1)}, u32[]{:S(2)}, u32[]{:S(2)}) collective-permute-start(bf16[64,384]{1,0:T(8,128)(2,1)S(1)} %get-tuple-element.27), channel_id=1, source_target_pairs={{0,8},{4,12},{8,0},{12,4},{1,9},{5,13},{9,1},{13,5},{2,10},{6,14},... | collective-permute-start | bytes 147464 | tf_op jit(solution)/shard_map/ppermute | solution.py:248
  63.9 0.0 collective-permute-done.6.refs_1_
  63.9 1.3 %collective-permute-start.8 = (bf16[64,384]{1,0:T(8,128)(2,1)S(1)}, bf16[64,384]{1,0:T(8,128)(2,1)S(1)}, u32[]{:S(2)}, u32[]{:S(2)}) collective-permute-start(bf16[64,384]{1,0:T(8,128)(2,1)S(1)} %get-tuple-element.26), channel_id=1, source_target_pairs={{0,12},{4,8},{8,4},{12,0},{1,13},{5,9},{9,5},{13,1},{2,14},{6,10},... | collective-permute-start | bytes 147464 | tf_op jit(solution)/shard_map/ppermute | solution.py:248
  65.2 1.9 %collective-permute-done.7.refs_2_ = bf16[64,384]{1,0:T(8,128)(2,1)S(1)} collective-permute-done((bf16[64,384]{1,0:T(8,128)(2,1)S(1)}, bf16[64,384]{1,0:T(8,128)(2,1)S(1)}, u32[]{:S(2)}, u32[]{:S(2)}) %collective-permute-start.7) | collective-permute-done | bytes 49184 | tf_op jit(solution)/shard_map/ppermute | solution.py:248
  67.1 2.7 %collective-permute-done.8.refs_3_ = bf16[64,384]{1,0:T(8,128)(2,1)S(1)} collective-permute-done((bf16[64,384]{1,0:T(8,128)(2,1)S(1)}, bf16[64,384]{1,0:T(8,128)(2,1)S(1)}, u32[]{:S(2)}, u32[]{:S(2)}) %collective-permute-start.8) | collective-permute-done | bytes 49184 | tf_op jit(solution)/shard_map/ppermute | solution.py:248
  69.8 0.0 copy-done.5
  69.8 1.1 %shard_map.92 = f32[32,512]{1,0:T(8,128)} custom-call(bf16[32,2048]{1,0:T(8,128)(2,1)S(1)} %copy-done.5, bf16[64,384]{1,0:T(8,128)(2,1)S(1)} %get-tuple-element.29.refs_0_, bf16[64,384]{1,0:T(8,128)(2,1)S(1)} %collective-permute-done.6.refs_1_, bf16[64,384]{1,0:T(8,128)(2,1)S(1)} %collective-permute-done.7.refs_2_, ...), custom_call_target="tpu_custom_call" | custom-call | flops 100000000 | bytes 500000 | tf_op jit(solution)/shard_map/pallas_call | solution.py:367
  70.9 0.0 collective-permute-done.3.refs_1_
  70.9 0.0 collective-permute-done.4.refs_2_
  70.9 0.0 collective-permute-done.5.refs_3_
  70.9 0.0 copy-done.2
  70.9 0.0 copy-done.4
  70.9 1.5 %shard_map.90 = bf16[128,1024]{1,0:T(8,128)(2,1)} custom-call(bf16[128,1024]{1,0:T(8,128)(2,1)S(1)} %copy-done.4, bf16[1024,1024]{1,0:T(8,128)(2,1)S(1)} %copy-done.2, bf16[128,256]{1,0:T(8,128)(2,1)S(1)} %get-tuple-element.25.refs_0_, bf16[128,256]{1,0:T(8,128)(2,1)S(1)} %collective-permute-done.3.refs_1_, ...), custom_call_target="tpu_custom_call" | custom-call | flops 268435456 | bytes 2621440 | tf_op jit(solution)/shard_map/pallas_call | solution.py:18
  (9 shorter events, 0.1 us)
Async XLA Ops:
  0.6 1.0 %copy-start = (s32[65536]{0:T(1024)S(1)}, s32[65536]{0:T(1024)}, u32[]{:S(2)}) copy-start(s32[65536]{0:T(1024)} %param.10) | copy-start | bytes 786436
  3.4 13.7 %all-to-all-start = ((s32[16,1,128]{2,1,0:T(1,128)}), s32[16,1,128]{2,1,0:T(1,128)S(1)}, u32[]{:S(2)}, u32[]{:S(2)}) async-start(s32[16,1,128]{2,1,0:T(1,128)} %broadcast_in_dim.22), calls=%async_computation | async-start | bytes 16384 | tf_op jit(solution)/shard_map/all_to_all | solution.py:271
  12.3 1.6 %copy-start.1 = (bf16[1024,1024]{1,0:T(8,128)(2,1)S(1)}, bf16[1024,1024]{1,0:T(8,128)(2,1)}, u32[]{:S(2)}) copy-start(bf16[1024,1024]{1,0:T(8,128)(2,1)} %rotation_ref.3) | copy-start | bytes 6291460
  13.9 0.9 %copy-start.3 = (bf16[128,1024]{1,0:T(8,128)(2,1)S(1)}, bf16[128,1024]{1,0:T(8,128)(2,1)}, u32[]{:S(2)}) copy-start(bf16[128,1024]{1,0:T(8,128)(2,1)} %passages_ref.3) | copy-start | bytes 786436
  14.8 0.8 %copy-start.6 = (s32[128,128]{1,0:T(8,128)S(1)}, s32[128,128]{1,0:T(8,128)}, u32[]{:S(2)}) copy-start(s32[128,128]{1,0:T(8,128)} %codes_ref.1) | copy-start | bytes 196612
  17.1 34.4 %all-to-all-start.1 = ((bf16[4,144,256]{2,1,0:T(8,128)(2,1)}), bf16[4,144,256]{2,1,0:T(8,128)(2,1)S(1)}, u32[]{:S(2)}, u32[]{:S(2)}) async-start(bf16[4,144,256]{2,1,0:T(8,128)(2,1)} %shard_map.86), calls=%async_computation.1 | async-start | bytes 589824 | tf_op jit(solution)/shard_map/all_to_all | solution.py:289
  29.1 24.7 %collective-permute-start = (bf16[4,64,256]{2,1,0:T(8,128)(2,1)}, bf16[4,64,256]{2,1,0:T(8,128)(2,1)}, u32[]{:S(2)}, u32[]{:S(2)}) collective-permute-start(bf16[4,64,256]{2,1,0:T(8,128)(2,1)} %bitcast.5), channel_id=1, source_target_pairs={{0,4},{4,0},{8,12},{12,8},{1,5},{5,1},{9,13},{13,9},{2,6},{6,2},{1... | collective-permute-start | bytes 393224 | tf_op jit(solution)/shard_map/ppermute | solution.py:248
  30.8 39.0 %copy-start.5 = (bf16[32,2048]{1,0:T(8,128)(2,1)S(1)}, bf16[32,2048]{1,0:T(8,128)(2,1)}, u32[]{:S(2)}) copy-start(bf16[32,2048]{1,0:T(8,128)(2,1)} %codebook_ref.1) | copy-start | bytes 393220
  30.9 40.0 %copy-start.2 = (bf16[1024,1024]{1,0:T(8,128)(2,1)S(1)}, bf16[1024,1024]{1,0:T(8,128)(2,1)}, u32[]{:S(2)}) copy-start(bf16[1024,1024]{1,0:T(8,128)(2,1)} %rotation_ref.3) | copy-start | bytes 6291460
  30.9 40.0 %copy-start.4 = (bf16[128,1024]{1,0:T(8,128)(2,1)S(1)}, bf16[128,1024]{1,0:T(8,128)(2,1)}, u32[]{:S(2)}) copy-start(bf16[128,1024]{1,0:T(8,128)(2,1)} %passages_ref.3) | copy-start | bytes 786436
  37.1 16.7 %collective-permute-start.1 = (bf16[4,64,256]{2,1,0:T(8,128)(2,1)}, bf16[4,64,256]{2,1,0:T(8,128)(2,1)}, u32[]{:S(2)}, u32[]{:S(2)}) collective-permute-start(bf16[4,64,256]{2,1,0:T(8,128)(2,1)} %bitcast.6), channel_id=1, source_target_pairs={{0,8},{4,12},{8,0},{12,4},{1,9},{5,13},{9,1},{13,5},{2,10},{6,14},... | collective-permute-start | bytes 393224 | tf_op jit(solution)/shard_map/ppermute | solution.py:248
  45.7 8.2 %collective-permute-start.2 = (bf16[4,64,256]{2,1,0:T(8,128)(2,1)}, bf16[4,64,256]{2,1,0:T(8,128)(2,1)}, u32[]{:S(2)}, u32[]{:S(2)}) collective-permute-start(bf16[4,64,256]{2,1,0:T(8,128)(2,1)} %bitcast.7), channel_id=1, source_target_pairs={{0,12},{4,8},{8,4},{12,0},{1,13},{5,9},{9,5},{13,1},{2,14},{6,10},... | collective-permute-start | bytes 393224 | tf_op jit(solution)/shard_map/ppermute | solution.py:248
  57.6 6.4 %collective-permute-start.6 = (bf16[64,384]{1,0:T(8,128)(2,1)S(1)}, bf16[64,384]{1,0:T(8,128)(2,1)S(1)}, u32[]{:S(2)}, u32[]{:S(2)}) collective-permute-start(bf16[64,384]{1,0:T(8,128)(2,1)S(1)} %get-tuple-element.28), channel_id=1, source_target_pairs={{0,4},{4,0},{8,12},{12,8},{1,5},{5,1},{9,13},{13,9},{2,6},{6,2},{1... | collective-permute-start | bytes 147464 | tf_op jit(solution)/shard_map/ppermute | solution.py:248
  58.4 12.4 %collective-permute-start.3 = (bf16[128,256]{1,0:T(8,128)(2,1)S(1)}, bf16[128,256]{1,0:T(8,128)(2,1)S(1)}, u32[]{:S(2)}, u32[]{:S(2)}) collective-permute-start(bf16[128,256]{1,0:T(8,128)(2,1)S(1)} %get-tuple-element.24), channel_id=1, source_target_pairs={{0,1},{1,0},{2,3},{3,2},{4,5},{5,4},{6,7},{7,6},{8,9},{9,8},{10,11... | collective-permute-start | bytes 196616 | tf_op jit(solution)/shard_map/ppermute | solution.py:248
  58.5 12.4 %collective-permute-start.4 = (bf16[128,256]{1,0:T(8,128)(2,1)S(1)}, bf16[128,256]{1,0:T(8,128)(2,1)S(1)}, u32[]{:S(2)}, u32[]{:S(2)}) collective-permute-start(bf16[128,256]{1,0:T(8,128)(2,1)S(1)} %get-tuple-element.23), channel_id=1, source_target_pairs={{0,2},{1,3},{2,0},{3,1},{4,6},{5,7},{6,4},{7,5},{8,10},{9,11},{10,... | collective-permute-start | bytes 196616 | tf_op jit(solution)/shard_map/ppermute | solution.py:248
  60.6 10.3 %collective-permute-start.5 = (bf16[128,256]{1,0:T(8,128)(2,1)S(1)}, bf16[128,256]{1,0:T(8,128)(2,1)S(1)}, u32[]{:S(2)}, u32[]{:S(2)}) collective-permute-start(bf16[128,256]{1,0:T(8,128)(2,1)S(1)} %get-tuple-element.22), channel_id=1, source_target_pairs={{0,3},{1,2},{2,1},{3,0},{4,7},{5,6},{6,5},{7,4},{8,11},{9,10},{10,... | collective-permute-start | bytes 196616 | tf_op jit(solution)/shard_map/ppermute | solution.py:248
  60.6 6.5 %collective-permute-start.7 = (bf16[64,384]{1,0:T(8,128)(2,1)S(1)}, bf16[64,384]{1,0:T(8,128)(2,1)S(1)}, u32[]{:S(2)}, u32[]{:S(2)}) collective-permute-start(bf16[64,384]{1,0:T(8,128)(2,1)S(1)} %get-tuple-element.27), channel_id=1, source_target_pairs={{0,8},{4,12},{8,0},{12,4},{1,9},{5,13},{9,1},{13,5},{2,10},{6,14},... | collective-permute-start | bytes 147464 | tf_op jit(solution)/shard_map/ppermute | solution.py:248
  63.9 5.9 %collective-permute-start.8 = (bf16[64,384]{1,0:T(8,128)(2,1)S(1)}, bf16[64,384]{1,0:T(8,128)(2,1)S(1)}, u32[]{:S(2)}, u32[]{:S(2)}) collective-permute-start(bf16[64,384]{1,0:T(8,128)(2,1)S(1)} %get-tuple-element.26), channel_id=1, source_target_pairs={{0,12},{4,8},{8,4},{12,0},{1,13},{5,9},{9,5},{13,1},{2,14},{6,10},... | collective-permute-start | bytes 147464 | tf_op jit(solution)/shard_map/ppermute | solution.py:248

commit v2 on v1

--- a/solution.py
+++ b/solution.py
@@ -9,17 +9,18 @@
 
 BF16 = jnp.bfloat16
 F32 = jnp.float32
-VMEM_LIMIT = 48 * 1024 * 1024
-DIRECT_LISTS = 4
-
-
-def call(kernel, out_shape, flops, nbytes, *args):
+VMEM_LIMIT = 32 * 1024 * 1024
+DIRECT = 4
+
+
+def call(kernel, out_shape, flops, nbytes, *args, scratch=()):
     whole = lambda: pl.BlockSpec(memory_space=pltpu.VMEM)
     return pl.pallas_call(
         kernel,
         out_shape=out_shape,
         in_specs=[whole() for _ in args],
         out_specs=jax.tree.map(lambda _: whole(), out_shape),
+        scratch_shapes=list(scratch),
         compiler_params=pltpu.CompilerParams(vmem_limit_bytes=VMEM_LIMIT),
         cost_estimate=pl.CostEstimate(flops=flops, bytes_accessed=nbytes, transcendentals=0),
     )(*args)
@@ -31,30 +32,37 @@
     return (row < col).astype(F32).astype(BF16)
 
 
-def rotate_kernel(subs, passages_ref, rotation_ref, codes_ref, out_ref):
+def rotate_kernel(subs, direct, passages_ref, rotation_ref, codes_ref, *refs):
+    outs, turned_ref = refs[:-1], refs[-1]
     rows, model = passages_ref.shape
     width = model // subs
     spaces = codes_ref.shape[1] // subs
     halves = width // rows
     tail = spaces // halves
-    codes_t = jnp.transpose(codes_ref[...].astype(F32)).astype(BF16)
-    for at in range(subs):
-        out_ref[at, :rows, :] = jnp.dot(
-            passages_ref[...],
-            rotation_ref[:, at * width : (at + 1) * width],
-            preferred_element_type=F32,
+    me = lax.axis_index("sub")
+    turned_ref[...] = jnp.transpose(codes_ref[...].astype(F32))
+    for step in range(subs):
+        at = (me ^ step) if direct else step
+        out = outs[step] if direct else outs[0].at[step]
+        columns = pl.ds(pl.multiple_of(at * width, width), width)
+        out[:rows, :] = jnp.dot(
+            passages_ref[...], rotation_ref[:, columns], preferred_element_type=F32
         ).astype(BF16)
         for half in range(halves):
-            start = at * spaces + half * tail
-            out_ref[at, rows:, half * rows : (half + 1) * rows] = codes_t[start : start + tail]
-
-
-def slots_kernel(held, lists, direct, rows_ref, *outs):
-    blocks, rows = rows_ref.shape
+            start = pl.multiple_of(at * spaces + half * tail, tail)
+            out[rows:, half * rows : (half + 1) * rows] = turned_ref[pl.ds(start, tail), :].astype(
+                BF16
+            )
+
+
+def fetch_kernel(held, lists, count, *refs):
+    rows_refs, centroids_ref, outs = refs[:count], refs[count], refs[count + 1 : -3]
+    index_ref, scalar_ref, sem = refs[-3:]
+    blocks, cap = index_ref.shape
+    rows = rows_refs[0].shape[1]
+    group = min(cap, 16)
     me = lax.axis_index("lists")
-    subs = blocks // lists
-    cap = outs[0].shape[1]
-    local = rows_ref[...] - me * held
+    local = jnp.concatenate([ref[...] for ref in rows_refs], axis=0) - me * held
     mine = jnp.logical_and(local >= 0, local < held)
     flags = mine.astype(F32)
     rank = jnp.dot(flags.astype(BF16), strict_before(rows), preferred_element_type=F32)
@@ -76,19 +84,37 @@
             pair, chosen, (((1,), (1,)), ((), ())), preferred_element_type=F32
         )
         row = (found[0:1, :] * 128.0 + found[8:9, :]).astype(jnp.int32)
-        if direct:
-            place = (block // subs) ^ me
-            for step in range(lists):
-
-                @pl.when(place == step)
-                def _():
-                    outs[step][block % subs : block % subs + 1, :] = row
-        else:
-            outs[0][block : block + 1, :] = row
-
-
-def lookup_kernel(held, lists, direct, cap, rows_ref, message_ref, words_ref, picked_ref, slot_ref, codes_ref, tally_ref):
-    subs, _, width = message_ref.shape
+        index_ref[block : block + 1, :] = row
+    move = pltpu.make_async_copy(index_ref, scalar_ref, sem)
+    move.start()
+    within = lax.broadcasted_iota(jnp.int32, (blocks, cap), 1) % group
+    spot = (within * 16 + index_ref[...] % 16).astype(F32)
+    pad = max(128 // blocks, 1)
+    spot = jnp.transpose(jnp.concatenate([spot] * pad, axis=0))
+    lane = lax.broadcasted_iota(jnp.int32, (cap, group * 16), 1).astype(F32)
+    move.wait()
+    for block in range(blocks):
+        chosen = (lane == spot[:, block : block + 1]).astype(F32).astype(BF16)
+        for start in range(0, cap, group):
+            tiles = []
+            for at in range(start, start + group):
+                base = pl.multiple_of((scalar_ref[block, at] // 16) * 16, 16)
+                tiles.append(centroids_ref[pl.ds(base, 16), :])
+            value = jnp.dot(
+                chosen[start : start + group],
+                jnp.concatenate(tiles, axis=0),
+                preferred_element_type=F32,
+            ).astype(BF16)
+            per = blocks // len(outs)
+            outs[block // per][block % per, start : start + group, :] = value
+
+
+def lookup_kernel(held, lists, direct, cap, count, rows_ref, words_ref, *refs):
+    messages, (picked_ref, slot_ref, codes_ref, tally_ref) = refs[:count], refs[count:]
+    if not direct:
+        messages = [messages[0].at[at] for at in range(messages[0].shape[0])]
+    subs = len(messages)
+    width = messages[0].shape[1]
     rows = rows_ref.shape[1]
     spaces = codes_ref.shape[0]
     depth = width // spaces
@@ -96,7 +122,10 @@
     halves = width // rows
     tail = spaces // halves
     me = lax.axis_index("lists")
-    tables = rows_ref[pl.ds(pl.multiple_of(me * subs, subs), subs), :]
+    if direct:
+        tables = rows_ref[...]
+    else:
+        tables = rows_ref[pl.ds(pl.multiple_of(me * subs, subs), subs), :]
     owners = tables // held
     rank = jnp.zeros((subs, rows), F32)
     flags = [(owners == at).astype(F32) for at in range(lists)]
@@ -109,8 +138,8 @@
     slot_ref[...] = jnp.transpose(jnp.concatenate([slot] * (rows // subs), axis=0))
     for at in range(subs):
         for half in range(halves):
-            codes_ref[half * tail : (half + 1) * tail, at * rows : (at + 1) * rows] = message_ref[
-                at, rows:, half * rows : (half + 1) * rows
+            codes_ref[half * tail : (half + 1) * tail, at * rows : (at + 1) * rows] = messages[at][
+                rows:, half * rows : (half + 1) * rows
             ].astype(F32)
     parts = []
     for space in range(spaces):
@@ -136,27 +165,31 @@
         tally = tally + jnp.dot(
             hot, (lane == space).astype(F32).astype(BF16), preferred_element_type=F32
         )
-    tally_ref[...] = tally.astype(BF16)
-
-
-def place_kernel(own, slot_ref, message_ref, picked_ref, *refs):
-    pieces, (rebuilt_ref, residual_ref) = refs[:-2], refs[-2:]
-    subs, _, width = message_ref.shape
+    tally_ref[...] = tally
+
+
+def place_kernel(direct, count, slot_ref, picked_ref, *refs):
+    messages, refs = refs[:count], refs[count:]
+    if not direct:
+        messages = [messages[0].at[at] for at in range(messages[0].shape[0])]
+    subs = len(messages)
+    spread = subs if direct else 1
+    pieces, rebuilt, residual_ref = refs[: -1 - spread], refs[-1 - spread : -1], refs[-1]
     rows = slot_ref.shape[0]
     total = sum(piece.shape[1] for piece in pieces)
     column = lax.broadcasted_iota(jnp.int32, (rows, total), 1).astype(F32)
     for at in range(subs):
         chosen = (column == slot_ref[:, at : at + 1]).astype(F32).astype(BF16)
-        centre = jnp.zeros((rows, width), F32)
-        start = 0
         stacked = jnp.concatenate([piece[at] for piece in pieces], axis=0)
         centre = jnp.dot(chosen, stacked, preferred_element_type=F32)
         span = slice(at * rows, (at + 1) * rows)
-        rebuilt_ref[at] = (centre + picked_ref[span, :].astype(F32)).astype(BF16)
-        residual_ref[span, :] = (message_ref[at, :rows, :].astype(F32) - centre).astype(BF16)
-
-
-def sums_kernel(lists, codes_ref, residual_ref, tally_ref, out_ref):
+        out = rebuilt[at] if direct else rebuilt[0].at[at]
+        out[...] = (centre + picked_ref[span, :].astype(F32)).astype(BF16)
+        residual_ref[span, :] = (messages[at][:rows, :].astype(F32) - centre).astype(BF16)
+
+
+def sums_kernel(lists, direct, codes_ref, residual_ref, tally_ref, *refs):
+    outs, total_ref = refs[:-1], refs[-1]
     spaces, rows = codes_ref.shape
     width = residual_ref.shape[1]
     words = tally_ref.shape[0]
@@ -170,11 +203,14 @@
         hot = (word == codes_ref[space : space + 1, :]).astype(F32).astype(BF16)
         part = jnp.where(owner == space, residual, jnp.zeros_like(residual))
         total = total + jnp.dot(hot, part, preferred_element_type=F32)
-    total = total.astype(BF16)
-    tally = tally_ref[...]
-    for at in range(lists):
-        out_ref[at, :, :width] = total[at * share : (at + 1) * share]
-        out_ref[at, :, width:] = tally[at * share : (at + 1) * share]
+    total_ref[...] = total
+    me = lax.axis_index("lists")
+    for step in range(lists):
+        out = outs[step] if direct else outs[0].at[step]
+        at = (me ^ step) if direct else step
+        span = pl.ds(pl.multiple_of(at * share, share), share)
+        out[:, :width] = total_ref[span, :].astype(BF16)
+        out[:, width:] = tally_ref[span, :].astype(BF16)
 
 
 def refine_kernel(spaces, direct, codebook_ref, *refs):
@@ -248,8 +284,22 @@
     return lax.ppermute(value, axis, [(at, at ^ step) for at in range(count)])
 
 
-def pick(value, index):
-    return lax.dynamic_index_in_dim(value, index, 0, keepdims=False)
+def gather_rows(table, at):
+    return lax.gather(
+        table,
+        at[:, None],
+        lax.GatherDimensionNumbers(offset_dims=(), collapsed_slice_dims=(0,), start_index_map=(0,)),
+        slice_sizes=(1,),
+        mode=lax.GatherScatterMode.PROMISE_IN_BOUNDS,
+    )
+
+
+def exchange(values, axis):
+    return [values[0]] + [swap(values[step], axis, step) for step in range(1, len(values))]
+
+
+def all_swap(value, axis):
+    return lax.all_to_all(value, axis, split_axis=0, concat_axis=0, tiled=True)
 
 
 def body(passages, rotation, centroids, list_slot, list_ids, codes, codebook):
@@ -262,101 +312,97 @@
     depth = width // spaces
     words = codebook.shape[1] // depth
     share = words // lists
-    direct = lists <= DIRECT_LISTS
-    me_list = lax.axis_index("lists")
-    me_sub = lax.axis_index("sub")
+    direct = max(lists, subs) <= DIRECT
     shape = jax.ShapeDtypeStruct
 
-    tables = list_slot.at[list_ids].get(mode="promise_in_bounds")
-    tables = lax.all_to_all(
-        jnp.broadcast_to(tables[None, None, :], (lists * subs, 1, rows)),
-        ("lists", "sub"),
-        split_axis=0,
-        concat_axis=0,
-        tiled=True,
-    ).reshape(lists * subs, rows)
-
-    halves = width // rows
-    message = call(
-        functools.partial(rotate_kernel, subs),
-        shape((subs, rows + spaces // halves, width), BF16),
+    tables = gather_rows(list_slot, list_ids)
+    if direct:
+        tables = tables.reshape(1, rows)
+        tables = jnp.concatenate(exchange([tables] * subs, "sub"), axis=0)
+        tables = exchange([tables] * lists, "lists")
+    else:
+        tables = jnp.broadcast_to(tables[None, None, :], (lists * subs, 1, rows))
+        tables = [all_swap(tables, ("lists", "sub")).reshape(lists * subs, rows)]
+
+    pieces = call(
+        functools.partial(fetch_kernel, held, lists, len(tables)),
+        [shape((subs, cap, width), BF16)] * lists
+        if direct
+        else [shape((lists * subs, cap, width), BF16)],
+        600_000_000,
+        held * width * 2,
+        *tables,
+        centroids,
+        scratch=[
+            pltpu.VMEM((lists * subs, cap), jnp.int32),
+            pltpu.SMEM((lists * subs, cap), jnp.int32),
+            pltpu.SemaphoreType.DMA,
+        ],
+    )
+    if direct:
+        pieces = exchange(pieces, "lists")
+    else:
+        found = all_swap(pieces[0].reshape(lists, subs * cap, width), "lists")
+        found = found.reshape(lists, subs, cap, width)
+        pieces = [jnp.swapaxes(found, 0, 1).reshape(subs, lists * cap, width)]
+
+    long = rows + spaces // (width // rows)
+    messages = call(
+        functools.partial(rotate_kernel, subs, direct),
+        [shape((long, width), BF16)] * subs if direct else [shape((subs, long, width), BF16)],
         2 * rows * model * model,
         2 * model * model + 4 * rows * model,
         passages,
         rotation,
         codes,
-    )
-    message = lax.all_to_all(message, "sub", split_axis=0, concat_axis=0, tiled=True)
-
-    idx = call(
-        functools.partial(slots_kernel, held, lists, direct),
-        [shape((subs, cap), jnp.int32)] * lists if direct else [shape((lists * subs, cap), jnp.int32)],
-        10_000_000,
-        100_000,
-        tables,
-    )
-    fetch = lambda at: centroids.at[at].get(mode="promise_in_bounds")
-    if direct:
-        pieces = [fetch(idx[0])] + [
-            swap(fetch(idx[step]), "lists", step) for step in range(1, lists)
-        ]
-    else:
-        found = lax.all_to_all(
-            fetch(idx[0]).reshape(lists, subs * cap, width), "lists", 0, 0, tiled=True
-        )
-        found = found.reshape(lists, subs, cap, width)
-        pieces = [jnp.swapaxes(found, 0, 1).reshape(subs, lists * cap, width)]
+        scratch=[pltpu.VMEM((codes.shape[1], rows), F32)],
+    )
+    messages = exchange(messages, "sub") if direct else [all_swap(messages[0], "sub")]
 
     word_table = (
         codebook.astype(F32).reshape(spaces, words, depth).transpose(0, 2, 1).reshape(width, words)
     )
     picked, slot, codes_t, tally = call(
-        functools.partial(lookup_kernel, held, lists, direct, cap),
+        functools.partial(lookup_kernel, held, lists, direct, cap, len(messages)),
         [
             shape((subs * rows, width), BF16),
             shape((rows, rows), F32),
             shape((spaces, subs * rows), F32),
-            shape((words, 128), BF16),
+            shape((words, 128), F32),
         ],
         1_000_000_000,
         2_000_000,
-        tables,
-        message,
+        tables[0],
         word_table,
-    )
-    rebuilt, residual = call(
-        functools.partial(place_kernel, me_list),
-        [shape((subs, rows, width), BF16), shape((subs * rows, width), BF16)],
+        *messages,
+    )
+    *rebuilt, residual = call(
+        functools.partial(place_kernel, direct, len(messages)),
+        ([shape((rows, width), BF16)] * subs if direct else [shape((subs, rows, width), BF16)])
+        + [shape((subs * rows, width), BF16)],
         300_000_000,
         2_000_000,
         slot,
-        message,
         picked,
+        *messages,
         *pieces,
     )
-    if subs <= DIRECT_LISTS:
-        rebuilt = [pick(rebuilt, me_sub)] + [
-            swap(pick(rebuilt, me_sub ^ step), "sub", step) for step in range(1, subs)
-        ]
-    else:
-        rebuilt = [lax.all_to_all(rebuilt, "sub", 0, 0, tiled=True)]
+    rebuilt = exchange(rebuilt, "sub") if direct else [all_swap(rebuilt[0], "sub")]
     sums = call(
-        functools.partial(sums_kernel, lists),
-        shape((lists, share, width + 128), BF16),
+        functools.partial(sums_kernel, lists, direct),
+        [shape((share, width + 128), BF16)] * lists
+        if direct
+        else [shape((lists, share, width + 128), BF16)],
         2_000_000_000,
         1_000_000,
         codes_t,
         residual,
         tally,
-    )
-    if direct:
-        sums = [pick(sums, me_list)] + [
-            swap(pick(sums, me_list ^ step), "lists", step) for step in range(1, lists)
-        ]
-    else:
-        sums = [lax.all_to_all(sums, "lists", 0, 0, tiled=True)]
+        scratch=[pltpu.VMEM((words, width), F32)],
+    )
+    sums = exchange(sums, "lists") if direct else [all_swap(sums[0], "lists")]
     recon_error = call(
-        functools.partial(restore_kernel, subs <= DIRECT_LISTS),
+        functools.partial(restore_kernel, direct),
         shape((rows, model), BF16),
         2 * rows * model * model,
         2 * model * model + 4 * rows * model,
@@ -364,15 +410,15 @@
         rotation,
         *rebuilt,
     )
-    new_codebook = pl.pallas_call(
+    new_codebook = call(
         functools.partial(refine_kernel, spaces, direct),
-        out_shape=shape((spaces, share * depth), F32),
-        in_specs=[pl.BlockSpec(memory_space=pltpu.VMEM)] * (1 + len(sums)),
-        out_specs=pl.BlockSpec(memory_space=pltpu.VMEM),
-        scratch_shapes=[pltpu.VMEM((width, share), F32)],
-        compiler_params=pltpu.CompilerParams(vmem_limit_bytes=VMEM_LIMIT),
-        cost_estimate=pl.CostEstimate(flops=100_000_000, bytes_accessed=500_000, transcendentals=0),
-    )(codebook, *sums)
+        shape((spaces, share * depth), F32),
+        100_000_000,
+        500_000,
+        codebook,
+        *sums,
+        scratch=[pltpu.VMEM((width, share), F32)],
+    )
     return (recon_error, new_codebook)
 
 

time: 73 us -> 62.6 us (0.86)
  local copies, waits for them, and re-layouts: 31.1 us -> 14.8 us
  Pallas kernels: 12.1 us -> 17.7 us
  waiting for transfers between devices: 4.81 us -> 8.19 us
  starting transfers between devices: 22.8 us -> 19.9 us
    gather x5 -> x1, local copies, waits for them, and re-layouts: 25 us -> 1.15 us  [gather_rows(): lax.gather(table, at[:, None], lax.GatherDimensionNumbers(offset_dims=(),...]
    all_to_all x2 -> x0, starting transfers between devices: 10.8 us -> none  [the longest x1 7.36 us: body(): lax.all_to_all(jnp.broadcast_to(tables[None, None, :], (lists * subs, 1,...]
    ppermute x9 -> x18, starting transfers between devices: 12 us -> 19.9 us  [swap(): return lax.ppermute(value, axis, [(at, at ^ step) for at in range(count)])]
    unnamed x14 -> x26, local copies, waits for them, and re-layouts: 3.64 us -> 10.9 us
    pallas_call x6 -> x7, Pallas kernels: 11 us -> 17.7 us  [call(): pl.pallas_call(kernel, out_shape=out_shape, in_specs=[whole() for _ in ar...]
    ppermute x9 -> x18, waiting for transfers between devices: 4.61 us -> 8.19 us  [swap(): return lax.ppermute(value, axis, [(at, at ^ step) for at in range(count)])]
    reshape x2, local copies, waits for them, and re-layouts: 1.5 us -> 2.75 us  [body(): codebook.astype(F32).reshape(spaces, words, depth).transpose(0, 2, 1)]
    pallas_call x1 -> x0, Pallas kernels: 1.09 us -> none  [body(): pl.pallas_call(functools.partial(refine_kernel, spaces, direct), out_shap...]
  transfers between devices with their start and end apart: 11 -> 18, of which waited for: 3 -> 4; matrix products, arithmetic and copies ran while one was open for 35% -> 4% of each run, Pallas kernels for 10% -> 20%
where the time goes in v2:
time: 62.6 us; the launch traced here: 62.1 us
  starting transfers between devices  19.9 us (32%)
  Pallas kernels  17.7 us (28%)
  local copies, waits for them, and re-layouts  14.8 us (24%)
  waiting for transfers between devices  8.19 us (13%)
  between operations  0.82 us (1%)
  other arithmetic  0.72 us (1%)
    ppermute x18, starting transfers between devices, swap(): return lax.ppermute(value, axis, [(at, at ^ step) for at in range(count)])  19.9 us
    pallas_call x7, Pallas kernels, call(): pl.pallas_call(kernel, out_shape=out_shape, in_specs=[whole() for _ in ar...  17.7 us
    unnamed x26, local copies, waits for them, and re-layouts  10.9 us
    ppermute x18, waiting for transfers between devices, swap(): return lax.ppermute(value, axis, [(at, at ^ step) for at in range(count)])  8.19 us
    reshape x2, local copies, waits for them, and re-layouts, body(): codebook.astype(F32).reshape(spaces, words, depth).transpose(0, 2, 1)  2.75 us
  transfers between devices with their start and end apart: 18, of which 4 were waited for; matrix products, arithmetic and copies ran while one was open for 4% of the time, Pallas kernels for 20%

profile of v2, /device:TPU:0, one launch (start us, length us, event | category | flops | bytes accessed | tf_op | source)
XLA Modules:
  0.0 62.1 jit_solution(16157731406063878417)
XLA Ops:
  0.6 0.0 copy-start
  0.6 0.0 copy-start.6
  0.7 0.7 %pad_clamp_fusion = s32[1024]{0:T(1024)S(1)} fusion(s32[128]{0:T(128)} %param.11), kind=kLoop, calls=%fused_computation.1 | loop fusion | flops 1024 | bytes 4608 | tf_op jit(solution)/shard_map/gather | solution.py:288
  1.4 0.2 copy-done
  1.6 1.1 %gather_fusion = s32[128]{0:T(128)S(1)} fusion(s32[65536]{0:T(1024)S(1)} %copy-done, s32[1024]{0:T(1024)S(1)} %pad_clamp_fusion), kind=kCustom, calls=%fused_computation | custom fusion | bytes 1536 | tf_op jit(solution)/shard_map/gather | solution.py:288
  2.8 2.4 %collective-permute-start.2 = (s32[1,128]{1,0:T(1,128)S(1)}, s32[1,128]{1,0:T(1,128)S(1)}, u32[]{:S(2)}, u32[]{:S(2)}) collective-permute-start(s32[1,128]{1,0:T(1,128)S(1)} %bitcast.7), channel_id=1, source_target_pairs={{0,3},{1,2},{2,1},{3,0},{4,7},{5,6},{6,5},{7,4},{8,11},{9,10},{10,... | collective-permute-start | bytes 1544 | tf_op jit(solution)/shard_map/ppermute | solution.py:284
  5.2 0.6 %collective-permute-start.1 = (s32[1,128]{1,0:T(1,128)S(1)}, s32[1,128]{1,0:T(1,128)S(1)}, u32[]{:S(2)}, u32[]{:S(2)}) collective-permute-start(s32[1,128]{1,0:T(1,128)S(1)} %bitcast.8), channel_id=1, source_target_pairs={{0,2},{1,3},{2,0},{3,1},{4,6},{5,7},{6,4},{7,5},{8,10},{9,11},{10,... | collective-permute-start | bytes 1544 | tf_op jit(solution)/shard_map/ppermute | solution.py:284
  5.8 0.0 collective-permute-start
  5.9 1.6 %copy-done.2 = bf16[1024,1024]{1,0:T(8,128)(2,1)S(1)} copy-done((bf16[1024,1024]{1,0:T(8,128)(2,1)S(1)}, bf16[1024,1024]{1,0:T(8,128)(2,1)}, u32[]{:S(2)}) %copy-start.2) | copy-done | bytes 2097176
  7.5 0.9 %copy-done.4 = bf16[128,1024]{1,0:T(8,128)(2,1)S(1)} copy-done((bf16[128,1024]{1,0:T(8,128)(2,1)S(1)}, bf16[128,1024]{1,0:T(8,128)(2,1)}, u32[]{:S(2)}) %copy-start.4) | copy-done | bytes 262168
  8.4 0.8 %copy-done.12 = s32[128,128]{1,0:T(8,128)S(1)} copy-done((s32[128,128]{1,0:T(8,128)S(1)}, s32[128,128]{1,0:T(8,128)}, u32[]{:S(2)}) %copy-start.12) | copy-done | bytes 65560
  9.3 1.2 %shard_map.86 = (bf16[144,256]{1,0:T(8,128)(2,1)S(1)}, bf16[144,256]{1,0:T(8,128)(2,1)S(1)}, bf16[144,256]{1,0:T(8,128)(2,1)}, bf16[144,256]{1,0:T(8,128)(2,1)}) custom-call(bf16[128,1024]{1,0:T(8,128)(2,1)S(1)} %copy-done.4, bf16[1024,1024]{1,0:T(8,128)(2,1)S(1)} %copy-done.2, s32[128,128]{1,0:T(8,128)S(1)} %copy-done.12), custom_call_target="tpu_custom_call" | custom-call | flops 268435456 | bytes 2621440 | tf_op jit(solution)/shard_map/pallas_call | solution.py:18
  10.4 0.6 copy-done.7
  11.0 0.5 collective-permute-start.3
  11.5 0.0 collective-permute-done.2
  11.5 0.0 collective-permute-done.1
  11.5 0.0 collective-permute-done
  11.5 1.6 %collective-permute-start.6 = (s32[4,128]{1,0:T(4,128)S(1)}, s32[4,128]{1,0:T(4,128)S(1)}, u32[]{:S(2)}, u32[]{:S(2)}) collective-permute-start(s32[4,128]{1,0:T(4,128)S(1)} %pad_add_fusion.rows_ref.refs_0_), channel_id=1, source_target_pairs={{0,4},{4,0},{8,12},{12,8},{1,5},{5,1},{9,13},{13,9},{2,6},{6,2},{1... | collective-permute-start | bytes 6152 | tf_op jit(solution)/shard_map/ppermute | solution.py:284
  13.2 2.6 %collective-permute-start.7 = (s32[4,128]{1,0:T(4,128)S(1)}, s32[4,128]{1,0:T(4,128)S(1)}, u32[]{:S(2)}, u32[]{:S(2)}) collective-permute-start(s32[4,128]{1,0:T(4,128)S(1)} %pad_add_fusion.rows_ref.refs_0_), channel_id=1, source_target_pairs={{0,8},{4,12},{8,0},{12,4},{1,9},{5,13},{9,1},{13,5},{2,10},{6,14},... | collective-permute-start | bytes 6152 | tf_op jit(solution)/shard_map/ppermute | solution.py:284
  15.8 0.2 collective-permute-start.8
  16.0 1.4 %collective-permute-start.4 = (bf16[144,256]{1,0:T(8,128)(2,1)}, bf16[144,256]{1,0:T(8,128)(2,1)}, u32[]{:S(2)}, u32[]{:S(2)}) collective-permute-start(bf16[144,256]{1,0:T(8,128)(2,1)} %get-tuple-element.25), channel_id=1, source_target_pairs={{0,2},{1,3},{2,0},{3,1},{4,6},{5,7},{6,4},{7,5},{8,10},{9,11},{10,... | collective-permute-start | bytes 221192 | tf_op jit(solution)/shard_map/ppermute | solution.py:284
  17.4 0.0 collective-permute-done.6.refs_1_
  17.4 0.0 collective-permute-start.5
  17.4 0.3 collective-permute-done.7.refs_2_
  17.7 3.5 %collective-permute-done.8.refs_3_ = s32[4,128]{1,0:T(4,128)S(1)} collective-permute-done((s32[4,128]{1,0:T(4,128)S(1)}, s32[4,128]{1,0:T(4,128)S(1)}, u32[]{:S(2)}, u32[]{:S(2)}) %collective-permute-start.8) | collective-permute-done | bytes 2080 | tf_op jit(solution)/shard_map/ppermute | solution.py:284
  21.2 3.4 %copy-done.1 = bf16[16384,256]{1,0:T(8,128)(2,1)S(1)} copy-done((bf16[16384,256]{1,0:T(8,128)(2,1)S(1)}, bf16[16384,256]{1,0:T(8,128)(2,1)}, u32[]{:S(2)}) %copy-start.1) | copy-done | bytes 8388632
  24.5 7.0 %shard_map.88 = (bf16[4,64,256]{2,1,0:T(8,128)(2,1)S(1)}, bf16[4,64,256]{2,1,0:T(8,128)(2,1)}, bf16[4,64,256]{2,1,0:T(8,128)(2,1)}, bf16[4,64,256]{2,1,0:T(8,128)(2,1)}) custom-call(s32[4,128]{1,0:T(4,128)S(1)} %pad_add_fusion.rows_ref.refs_0_, s32[4,128]{1,0:T(4,128)S(1)} %collective-permute-done.6.refs_1_, s32[4,128]{1,0:T(4,128)S(1)} %collective-permute-done.7.refs_2_, ...), custom_call_target="tpu_custom_call" | custom-call | flops 600000000 | bytes 8388608 | tf_op jit(solution)/shard_map/pallas_call | solution.py:18
  31.5 0.0 copy-start.3
  31.5 0.0 copy-start.5
  31.5 0.1 collective-permute-start.9
  31.6 0.8 %collective-permute-start.10 = (bf16[4,64,256]{2,1,0:T(8,128)(2,1)}, bf16[4,64,256]{2,1,0:T(8,128)(2,1)S(1)}, u32[]{:S(2)}, u32[]{:S(2)}) collective-permute-start(bf16[4,64,256]{2,1,0:T(8,128)(2,1)} %get-tuple-element.31), channel_id=1, source_target_pairs={{0,8},{4,12},{8,0},{12,4},{1,9},{5,13},{9,1},{13,5},{2,10},{6,14},... | collective-permute-start | bytes 393224 | tf_op jit(solution)/shard_map/ppermute | solution.py:284
  32.4 0.0 collective-permute-done.3.refs_1_
  32.4 0.6 %copy-done.9 = bf16[144,256]{1,0:T(8,128)(2,1)} copy-done((bf16[144,256]{1,0:T(8,128)(2,1)}, bf16[144,256]{1,0:T(8,128)(2,1)S(1)}, u32[]{:S(2)}) %copy-start.9) | copy-done | bytes 73752
  33.0 3.6 %collective-permute-start.11 = (bf16[4,64,256]{2,1,0:T(8,128)(2,1)}, bf16[4,64,256]{2,1,0:T(8,128)(2,1)S(1)}, u32[]{:S(2)}, u32[]{:S(2)}) collective-permute-start(bf16[4,64,256]{2,1,0:T(8,128)(2,1)} %get-tuple-element.32), channel_id=1, source_target_pairs={{0,12},{4,8},{8,4},{12,0},{1,13},{5,9},{9,5},{13,1},{2,14},{6,10},... | collective-permute-start | bytes 393224 | tf_op jit(solution)/shard_map/ppermute | solution.py:284
  36.6 0.0 copy-done.6
  36.6 1.2 %copy.10 = f32[32,2048]{0,1:T(8,128)} copy(bf16[32,2048]{1,0:T(8,128)(2,1)S(1)} %copy-done.6) | data formatting | bytes 393216 | tf_op jit(solution)/shard_map/reshape | solution.py:363
  37.8 1.6 %copy.11 = f32[32,8,256]{2,1,0:T(8,128)S(1)} copy(f32[32,8,256]{0,1,2:T(8,128)} %bitcast.6) | data formatting | bytes 524288 | tf_op jit(solution)/shard_map/reshape | solution.py:363
  39.4 0.0 collective-permute-done.4.refs_2_
  39.4 0.0 collective-permute-done.5.refs_3_
  39.4 0.0 copy-start.8
  39.4 0.9 %copy-done.8 = bf16[144,256]{1,0:T(8,128)(2,1)S(1)} copy-done((bf16[144,256]{1,0:T(8,128)(2,1)S(1)}, bf16[144,256]{1,0:T(8,128)(2,1)}, u32[]{:S(2)}) %copy-start.8) | copy-done | bytes 73752
  40.3 0.9 %copy-done.10 = bf16[144,256]{1,0:T(8,128)(2,1)S(1)} copy-done((bf16[144,256]{1,0:T(8,128)(2,1)S(1)}, bf16[144,256]{1,0:T(8,128)(2,1)}, u32[]{:S(2)}) %copy-start.10) | copy-done | bytes 73752
  41.2 3.3 %shard_map.87 = (bf16[512,256]{1,0:T(8,128)(2,1)S(1)}, f32[128,128]{1,0:T(8,128)S(1)}, f32[32,512]{1,0:T(8,128)S(1)}, f32[256,128]{1,0:T(8,128)S(1)}) custom-call(s32[4,128]{1,0:T(4,128)S(1)} %pad_add_fusion.rows_ref.refs_0_, f32[256,256]{1,0:T(8,128)S(1)} %bitcast.5, bf16[144,256]{1,0:T(8,128)(2,1)S(1)} %copy-done.8, bf16[144,256]{1,0:T(8,128)(2,1)S(1)} %copy-done.10, ...), custom_call_target="tpu_custom_call" | custom-call | flops 1000000000 | bytes 2000000 | tf_op jit(solution)/shard_map/pallas_call | solution.py:18
  44.5 0.0 collective-permute-done.9.refs_5_
  44.5 0.0 collective-permute-done.10.refs_6_
  44.5 0.0 collective-permute-done.11.refs_7_
  44.5 0.0 copy-start.11
  44.5 0.9 %copy-done.11 = bf16[144,256]{1,0:T(8,128)(2,1)S(1)} copy-done((bf16[144,256]{1,0:T(8,128)(2,1)S(1)}, bf16[144,256]{1,0:T(8,128)(2,1)}, u32[]{:S(2)}) %copy-start.11) | copy-done | bytes 73752
  45.4 1.2 %shard_map.89 = (bf16[128,256]{1,0:T(8,128)(2,1)S(1)}, bf16[128,256]{1,0:T(8,128)(2,1)S(1)}, bf16[128,256]{1,0:T(8,128)(2,1)S(1)}, bf16[128,256]{1,0:T(8,128)(2,1)S(1)}, bf16[512,256]{1,0:T(8,128)(2,1)S(1)}) custom-call(f32[128,128]{1,0:T(8,128)S(1)} %get-tuple-element.27.slot_ref, bf16[512,256]{1,0:T(8,128)(2,1)S(1)} %get-tuple-element.28.picked_ref, ...), custom_call_target="tpu_custom_call" | custom-call | flops 300000000 | bytes 2000000 | tf_op jit(solution)/shard_map/pallas_call | solution.py:18
  46.6 2.4 %shard_map.91 = (bf16[64,384]{1,0:T(8,128)(2,1)S(1)}, bf16[64,384]{1,0:T(8,128)(2,1)S(1)}, bf16[64,384]{1,0:T(8,128)(2,1)S(1)}, bf16[64,384]{1,0:T(8,128)(2,1)S(1)}) custom-call(f32[32,512]{1,0:T(8,128)S(1)} %get-tuple-element.37.codes_ref, bf16[512,256]{1,0:T(8,128)(2,1)S(1)} %get-tuple-element.38.residual_ref, f32[256,128]{1,0:T(8,128)S(1)} %get-tuple-element.39.tally_ref), custom_call_target="tpu_custom_call" | custom-call | flops 2000000000 | bytes 1000000 | tf_op jit(solution)/shard_map/pallas_call | solution.py:18
  49.0 1.4 %collective-permute-start.15 = (bf16[64,384]{1,0:T(8,128)(2,1)S(1)}, bf16[64,384]{1,0:T(8,128)(2,1)S(1)}, u32[]{:S(2)}, u32[]{:S(2)}) collective-permute-start(bf16[64,384]{1,0:T(8,128)(2,1)S(1)} %get-tuple-element.41), channel_id=1, source_target_pairs={{0,4},{4,0},{8,12},{12,8},{1,5},{5,1},{9,13},{13,9},{2,6},{6,2},{1... | collective-permute-start | bytes 147464 | tf_op jit(solution)/shard_map/ppermute | solution.py:284
  50.4 0.0 collective-permute-start.12
  50.4 1.5 %collective-permute-start.13 = (bf16[128,256]{1,0:T(8,128)(2,1)S(1)}, bf16[128,256]{1,0:T(8,128)(2,1)S(1)}, u32[]{:S(2)}, u32[]{:S(2)}) collective-permute-start(bf16[128,256]{1,0:T(8,128)(2,1)S(1)} %get-tuple-element.35), channel_id=1, source_target_pairs={{0,2},{1,3},{2,0},{3,1},{4,6},{5,7},{6,4},{7,5},{8,10},{9,11},{10,... | collective-permute-start | bytes 196616 | tf_op jit(solution)/shard_map/ppermute | solution.py:284
  51.9 0.4 collective-permute-start.14
  52.2 0.6 %collective-permute-start.16 = (bf16[64,384]{1,0:T(8,128)(2,1)S(1)}, bf16[64,384]{1,0:T(8,128)(2,1)S(1)}, u32[]{:S(2)}, u32[]{:S(2)}) collective-permute-start(bf16[64,384]{1,0:T(8,128)(2,1)S(1)} %get-tuple-element.42), channel_id=1, source_target_pairs={{0,8},{4,12},{8,0},{12,4},{1,9},{5,13},{9,1},{13,5},{2,10},{6,14},... | collective-permute-start | bytes 147464 | tf_op jit(solution)/shard_map/ppermute | solution.py:284
  52.9 0.3 collective-permute-done.15.refs_1_
  53.1 2.2 %collective-permute-start.17 = (bf16[64,384]{1,0:T(8,128)(2,1)S(1)}, bf16[64,384]{1,0:T(8,128)(2,1)S(1)}, u32[]{:S(2)}, u32[]{:S(2)}) collective-permute-start(bf16[64,384]{1,0:T(8,128)(2,1)S(1)} %get-tuple-element.43), channel_id=1, source_target_pairs={{0,12},{4,8},{8,4},{12,0},{1,13},{5,9},{9,5},{13,1},{2,14},{6,10},... | collective-permute-start | bytes 147464 | tf_op jit(solution)/shard_map/ppermute | solution.py:284
  55.3 4.1 %collective-permute-done.16.refs_2_ = bf16[64,384]{1,0:T(8,128)(2,1)S(1)} collective-permute-done((bf16[64,384]{1,0:T(8,128)(2,1)S(1)}, bf16[64,384]{1,0:T(8,128)(2,1)S(1)}, u32[]{:S(2)}, u32[]{:S(2)}) %collective-permute-start.16) | collective-permute-done | bytes 49184 | tf_op jit(solution)/shard_map/ppermute | solution.py:284
  59.4 0.0 collective-permute-done.17.refs_3_
  59.4 1.1 %shard_map.92 = f32[32,512]{1,0:T(8,128)} custom-call(bf16[32,2048]{1,0:T(8,128)(2,1)S(1)} %copy-done.6, bf16[64,384]{1,0:T(8,128)(2,1)S(1)} %get-tuple-element.40.refs_0_, bf16[64,384]{1,0:T(8,128)(2,1)S(1)} %collective-permute-done.15.refs_1_, bf16[64,384]{1,0:T(8,128)(2,1)S(1)} %collective-permute-done.16.refs_2_, ...), custom_call_target="tpu_custom_call" | custom-call | flops 100000000 | bytes 500000 | tf_op jit(solution)/shard_map/pallas_call | solution.py:18
  60.5 0.0 collective-permute-done.12.refs_1_
  60.5 0.0 collective-permute-done.13.refs_2_
  60.5 0.0 collective-permute-done.14.refs_3_
  60.6 1.5 %shard_map.90 = bf16[128,1024]{1,0:T(8,128)(2,1)} custom-call(bf16[128,1024]{1,0:T(8,128)(2,1)S(1)} %copy-done.5, bf16[1024,1024]{1,0:T(8,128)(2,1)S(1)} %copy-done.3, bf16[128,256]{1,0:T(8,128)(2,1)S(1)} %get-tuple-element.33.refs_0_, bf16[128,256]{1,0:T(8,128)(2,1)S(1)} %collective-permute-done.12.refs_1_, ...), custom_call_target="tpu_custom_call" | custom-call | flops 268435456 | bytes 2621440 | tf_op jit(solution)/shard_map/pallas_call | solution.py:18
  (10 shorter events, 0.0 us)
Async XLA Ops:
  0.6 1.0 %copy-start = (s32[65536]{0:T(1024)S(1)}, s32[65536]{0:T(1024)}, u32[]{:S(2)}) copy-start(s32[65536]{0:T(1024)} %param.10) | copy-start | bytes 786436
  0.6 36.0 %copy-start.6 = (bf16[32,2048]{1,0:T(8,128)(2,1)S(1)}, bf16[32,2048]{1,0:T(8,128)(2,1)}, u32[]{:S(2)}) copy-start(bf16[32,2048]{1,0:T(8,128)(2,1)} %codebook_ref.1) | copy-start | bytes 393220
  2.8 8.8 %collective-permute-start.2 = (s32[1,128]{1,0:T(1,128)S(1)}, s32[1,128]{1,0:T(1,128)S(1)}, u32[]{:S(2)}, u32[]{:S(2)}) collective-permute-start(s32[1,128]{1,0:T(1,128)S(1)} %bitcast.7), channel_id=1, source_target_pairs={{0,3},{1,2},{2,1},{3,0},{4,7},{5,6},{6,5},{7,4},{8,11},{9,10},{10,... | collective-permute-start | bytes 1544 | tf_op jit(solution)/shard_map/ppermute | solution.py:284
  5.2 6.3 %collective-permute-start.1 = (s32[1,128]{1,0:T(1,128)S(1)}, s32[1,128]{1,0:T(1,128)S(1)}, u32[]{:S(2)}, u32[]{:S(2)}) collective-permute-start(s32[1,128]{1,0:T(1,128)S(1)} %bitcast.8), channel_id=1, source_target_pairs={{0,2},{1,3},{2,0},{3,1},{4,6},{5,7},{6,4},{7,5},{8,10},{9,11},{10,... | collective-permute-start | bytes 1544 | tf_op jit(solution)/shard_map/ppermute | solution.py:284
  5.8 5.7 %collective-permute-start = (s32[1,128]{1,0:T(1,128)S(1)}, s32[1,128]{1,0:T(1,128)S(1)}, u32[]{:S(2)}, u32[]{:S(2)}) collective-permute-start(s32[1,128]{1,0:T(1,128)S(1)} %bitcast.9), channel_id=1, source_target_pairs={{0,1},{1,0},{2,3},{3,2},{4,5},{5,4},{6,7},{7,6},{8,9},{9,8},{10,11... | collective-permute-start | bytes 1544 | tf_op jit(solution)/shard_map/ppermute | solution.py:284
  5.9 1.6 %copy-start.2 = (bf16[1024,1024]{1,0:T(8,128)(2,1)S(1)}, bf16[1024,1024]{1,0:T(8,128)(2,1)}, u32[]{:S(2)}) copy-start(bf16[1024,1024]{1,0:T(8,128)(2,1)} %rotation_ref.3) | copy-start | bytes 6291460
  7.5 0.9 %copy-start.4 = (bf16[128,1024]{1,0:T(8,128)(2,1)S(1)}, bf16[128,1024]{1,0:T(8,128)(2,1)}, u32[]{:S(2)}) copy-start(bf16[128,1024]{1,0:T(8,128)(2,1)} %passages_ref.3) | copy-start | bytes 786436
  8.4 0.8 %copy-start.12 = (s32[128,128]{1,0:T(8,128)S(1)}, s32[128,128]{1,0:T(8,128)}, u32[]{:S(2)}) copy-start(s32[128,128]{1,0:T(8,128)} %codes_ref.1) | copy-start | bytes 196612
  10.4 0.6 copy-start.7
  11.0 21.4 %collective-permute-start.3 = (bf16[144,256]{1,0:T(8,128)(2,1)S(1)}, bf16[144,256]{1,0:T(8,128)(2,1)S(1)}, u32[]{:S(2)}, u32[]{:S(2)}) collective-permute-start(bf16[144,256]{1,0:T(8,128)(2,1)S(1)} %get-tuple-element.24), channel_id=1, source_target_pairs={{0,1},{1,0},{2,3},{3,2},{4,5},{5,4},{6,7},{7,6},{8,9},{9,8},{10,11... | collective-permute-start | bytes 221192 | tf_op jit(solution)/shard_map/ppermute | solution.py:284
  11.5 5.8 %collective-permute-start.6 = (s32[4,128]{1,0:T(4,128)S(1)}, s32[4,128]{1,0:T(4,128)S(1)}, u32[]{:S(2)}, u32[]{:S(2)}) collective-permute-start(s32[4,128]{1,0:T(4,128)S(1)} %pad_add_fusion.rows_ref.refs_0_), channel_id=1, source_target_pairs={{0,4},{4,0},{8,12},{12,8},{1,5},{5,1},{9,13},{13,9},{2,6},{6,2},{1... | collective-permute-start | bytes 6152 | tf_op jit(solution)/shard_map/ppermute | solution.py:284
  13.2 4.5 %collective-permute-start.7 = (s32[4,128]{1,0:T(4,128)S(1)}, s32[4,128]{1,0:T(4,128)S(1)}, u32[]{:S(2)}, u32[]{:S(2)}) collective-permute-start(s32[4,128]{1,0:T(4,128)S(1)} %pad_add_fusion.rows_ref.refs_0_), channel_id=1, source_target_pairs={{0,8},{4,12},{8,0},{12,4},{1,9},{5,13},{9,1},{13,5},{2,10},{6,14},... | collective-permute-start | bytes 6152 | tf_op jit(solution)/shard_map/ppermute | solution.py:284
  15.8 5.4 %collective-permute-start.8 = (s32[4,128]{1,0:T(4,128)S(1)}, s32[4,128]{1,0:T(4,128)S(1)}, u32[]{:S(2)}, u32[]{:S(2)}) collective-permute-start(s32[4,128]{1,0:T(4,128)S(1)} %pad_add_fusion.rows_ref.refs_0_), channel_id=1, source_target_pairs={{0,12},{4,8},{8,4},{12,0},{1,13},{5,9},{9,5},{13,1},{2,14},{6,10},... | collective-permute-start | bytes 6152 | tf_op jit(solution)/shard_map/ppermute | solution.py:284
  16.0 23.4 %collective-permute-start.4 = (bf16[144,256]{1,0:T(8,128)(2,1)}, bf16[144,256]{1,0:T(8,128)(2,1)}, u32[]{:S(2)}, u32[]{:S(2)}) collective-permute-start(bf16[144,256]{1,0:T(8,128)(2,1)} %get-tuple-element.25), channel_id=1, source_target_pairs={{0,2},{1,3},{2,0},{3,1},{4,6},{5,7},{6,4},{7,5},{8,10},{9,11},{10,... | collective-permute-start | bytes 221192 | tf_op jit(solution)/shard_map/ppermute | solution.py:284
  17.4 22.0 %collective-permute-start.5 = (bf16[144,256]{1,0:T(8,128)(2,1)}, bf16[144,256]{1,0:T(8,128)(2,1)}, u32[]{:S(2)}, u32[]{:S(2)}) collective-permute-start(bf16[144,256]{1,0:T(8,128)(2,1)} %get-tuple-element.26), channel_id=1, source_target_pairs={{0,3},{1,2},{2,1},{3,0},{4,7},{5,6},{6,5},{7,4},{8,11},{9,10},{10,... | collective-permute-start | bytes 221192 | tf_op jit(solution)/shard_map/ppermute | solution.py:284
  21.2 3.4 %copy-start.1 = (bf16[16384,256]{1,0:T(8,128)(2,1)S(1)}, bf16[16384,256]{1,0:T(8,128)(2,1)}, u32[]{:S(2)}) copy-start(bf16[16384,256]{1,0:T(8,128)(2,1)} %refs_4_.1) | copy-start | bytes 25165828
  31.5 29.0 %copy-start.3 = (bf16[1024,1024]{1,0:T(8,128)(2,1)S(1)}, bf16[1024,1024]{1,0:T(8,128)(2,1)}, u32[]{:S(2)}) copy-start(bf16[1024,1024]{1,0:T(8,128)(2,1)} %rotation_ref.3) | copy-start | bytes 6291460
  31.5 29.0 %copy-start.5 = (bf16[128,1024]{1,0:T(8,128)(2,1)S(1)}, bf16[128,1024]{1,0:T(8,128)(2,1)}, u32[]{:S(2)}) copy-start(bf16[128,1024]{1,0:T(8,128)(2,1)} %passages_ref.3) | copy-start | bytes 786436
  31.5 12.9 %collective-permute-start.9 = (bf16[4,64,256]{2,1,0:T(8,128)(2,1)}, bf16[4,64,256]{2,1,0:T(8,128)(2,1)S(1)}, u32[]{:S(2)}, u32[]{:S(2)}) collective-permute-start(bf16[4,64,256]{2,1,0:T(8,128)(2,1)} %get-tuple-element.30), channel_id=1, source_target_pairs={{0,4},{4,0},{8,12},{12,8},{1,5},{5,1},{9,13},{13,9},{2,6},{6,2},{1... | collective-permute-start | bytes 393224 | tf_op jit(solution)/shard_map/ppermute | solution.py:284
  31.6 12.9 %collective-permute-start.10 = (bf16[4,64,256]{2,1,0:T(8,128)(2,1)}, bf16[4,64,256]{2,1,0:T(8,128)(2,1)S(1)}, u32[]{:S(2)}, u32[]{:S(2)}) collective-permute-start(bf16[4,64,256]{2,1,0:T(8,128)(2,1)} %get-tuple-element.31), channel_id=1, source_target_pairs={{0,8},{4,12},{8,0},{12,4},{1,9},{5,13},{9,1},{13,5},{2,10},{6,14},... | collective-permute-start | bytes 393224 | tf_op jit(solution)/shard_map/ppermute | solution.py:284
  32.4 0.6 %copy-start.9 = (bf16[144,256]{1,0:T(8,128)(2,1)}, bf16[144,256]{1,0:T(8,128)(2,1)S(1)}, u32[]{:S(2)}) copy-start(bf16[144,256]{1,0:T(8,128)(2,1)S(1)} %collective-permute-done.3.refs_1_) | copy-start | bytes 221188
  33.0 11.5 %collective-permute-start.11 = (bf16[4,64,256]{2,1,0:T(8,128)(2,1)}, bf16[4,64,256]{2,1,0:T(8,128)(2,1)S(1)}, u32[]{:S(2)}, u32[]{:S(2)}) collective-permute-start(bf16[4,64,256]{2,1,0:T(8,128)(2,1)} %get-tuple-element.32), channel_id=1, source_target_pairs={{0,12},{4,8},{8,4},{12,0},{1,13},{5,9},{9,5},{13,1},{2,14},{6,10},... | collective-permute-start | bytes 393224 | tf_op jit(solution)/shard_map/ppermute | solution.py:284
  39.4 0.9 %copy-start.8 = (bf16[144,256]{1,0:T(8,128)(2,1)S(1)}, bf16[144,256]{1,0:T(8,128)(2,1)}, u32[]{:S(2)}) copy-start(bf16[144,256]{1,0:T(8,128)(2,1)} %copy-done.7) | copy-start | bytes 221188
  40.3 0.9 %copy-start.10 = (bf16[144,256]{1,0:T(8,128)(2,1)S(1)}, bf16[144,256]{1,0:T(8,128)(2,1)}, u32[]{:S(2)}) copy-start(bf16[144,256]{1,0:T(8,128)(2,1)} %copy-done.9) | copy-start | bytes 221188
  44.5 0.9 %copy-start.11 = (bf16[144,256]{1,0:T(8,128)(2,1)S(1)}, bf16[144,256]{1,0:T(8,128)(2,1)}, u32[]{:S(2)}) copy-start(bf16[144,256]{1,0:T(8,128)(2,1)} %copy-done.9) | copy-start | bytes 221188
  49.0 4.2 %collective-permute-start.15 = (bf16[64,384]{1,0:T(8,128)(2,1)S(1)}, bf16[64,384]{1,0:T(8,128)(2,1)S(1)}, u32[]{:S(2)}, u32[]{:S(2)}) collective-permute-start(bf16[64,384]{1,0:T(8,128)(2,1)S(1)} %get-tuple-element.41), channel_id=1, source_target_pairs={{0,4},{4,0},{8,12},{12,8},{1,5},{5,1},{9,13},{13,9},{2,6},{6,2},{1... | collective-permute-start | bytes 147464 | tf_op jit(solution)/shard_map/ppermute | solution.py:284
  50.4 10.2 %collective-permute-start.12 = (bf16[128,256]{1,0:T(8,128)(2,1)S(1)}, bf16[128,256]{1,0:T(8,128)(2,1)S(1)}, u32[]{:S(2)}, u32[]{:S(2)}) collective-permute-start(bf16[128,256]{1,0:T(8,128)(2,1)S(1)} %get-tuple-element.34), channel_id=1, source_target_pairs={{0,1},{1,0},{2,3},{3,2},{4,5},{5,4},{6,7},{7,6},{8,9},{9,8},{10,11... | collective-permute-start | bytes 196616 | tf_op jit(solution)/shard_map/ppermute | solution.py:284
  50.4 10.2 %collective-permute-start.13 = (bf16[128,256]{1,0:T(8,128)(2,1)S(1)}, bf16[128,256]{1,0:T(8,128)(2,1)S(1)}, u32[]{:S(2)}, u32[]{:S(2)}) collective-permute-start(bf16[128,256]{1,0:T(8,128)(2,1)S(1)} %get-tuple-element.35), channel_id=1, source_target_pairs={{0,2},{1,3},{2,0},{3,1},{4,6},{5,7},{6,4},{7,5},{8,10},{9,11},{10,... | collective-permute-start | bytes 196616 | tf_op jit(solution)/shard_map/ppermute | solution.py:284
  51.9 8.7 %collective-permute-start.14 = (bf16[128,256]{1,0:T(8,128)(2,1)S(1)}, bf16[128,256]{1,0:T(8,128)(2,1)S(1)}, u32[]{:S(2)}, u32[]{:S(2)}) collective-permute-start(bf16[128,256]{1,0:T(8,128)(2,1)S(1)} %get-tuple-element.36), channel_id=1, source_target_pairs={{0,3},{1,2},{2,1},{3,0},{4,7},{5,6},{6,5},{7,4},{8,11},{9,10},{10,... | collective-permute-start | bytes 196616 | tf_op jit(solution)/shard_map/ppermute | solution.py:284
  52.2 7.2 %collective-permute-start.16 = (bf16[64,384]{1,0:T(8,128)(2,1)S(1)}, bf16[64,384]{1,0:T(8,128)(2,1)S(1)}, u32[]{:S(2)}, u32[]{:S(2)}) collective-permute-start(bf16[64,384]{1,0:T(8,128)(2,1)S(1)} %get-tuple-element.42), channel_id=1, source_target_pairs={{0,8},{4,12},{8,0},{12,4},{1,9},{5,13},{9,1},{13,5},{2,10},{6,14},... | collective-permute-start | bytes 147464 | tf_op jit(solution)/shard_map/ppermute | solution.py:284
  53.1 6.3 %collective-permute-start.17 = (bf16[64,384]{1,0:T(8,128)(2,1)S(1)}, bf16[64,384]{1,0:T(8,128)(2,1)S(1)}, u32[]{:S(2)}, u32[]{:S(2)}) collective-permute-start(bf16[64,384]{1,0:T(8,128)(2,1)S(1)} %get-tuple-element.43), channel_id=1, source_target_pairs={{0,12},{4,8},{8,4},{12,0},{1,13},{5,9},{9,5},{13,1},{2,14},{6,10},... | collective-permute-start | bytes 147464 | tf_op jit(solution)/shard_map/ppermute | solution.py:284

commit v3 on v2

--- a/solution.py
+++ b/solution.py
@@ -13,12 +13,13 @@
 DIRECT = 4
 
 
-def call(kernel, out_shape, flops, nbytes, *args, scratch=()):
+def call(kernel, out_shape, flops, nbytes, *args, scratch=(), loose=0):
     whole = lambda: pl.BlockSpec(memory_space=pltpu.VMEM)
     return pl.pallas_call(
         kernel,
         out_shape=out_shape,
-        in_specs=[whole() for _ in args],
+        in_specs=[whole() for _ in args[: len(args) - loose]]
+        + [pl.BlockSpec(memory_space=pl.ANY)] * loose,
         out_specs=jax.tree.map(lambda _: whole(), out_shape),
         scratch_shapes=list(scratch),
         compiler_params=pltpu.CompilerParams(vmem_limit_bytes=VMEM_LIMIT),
@@ -32,7 +33,25 @@
     return (row < col).astype(F32).astype(BF16)
 
 
-def rotate_kernel(subs, direct, passages_ref, rotation_ref, codes_ref, *refs):
+def tables_kernel(ids_ref, slots_ref, out_ref):
+    rows = ids_ref.shape[1]
+    lines = slots_ref.shape[0]
+    ids = jnp.transpose(jnp.concatenate([ids_ref[...].astype(F32)] * 128, axis=0))[:, :1]
+    ids = ids.astype(jnp.int32)
+    line = lax.broadcasted_iota(jnp.int32, (rows, lines), 1)
+    chosen = (line == (ids >> 7)).astype(F32).astype(BF16)
+    table = slots_ref[...]
+    high = (table >> 8).astype(F32).astype(BF16)
+    low = (table & 255).astype(F32).astype(BF16)
+    found = jnp.dot(chosen, high, preferred_element_type=F32) * 256.0 + jnp.dot(
+        chosen, low, preferred_element_type=F32
+    )
+    lane = lax.broadcasted_iota(jnp.int32, (rows, 128), 1)
+    found = jnp.transpose(jnp.where(lane == (ids & 127), found, 0.0))
+    out_ref[...] = jnp.sum(found, axis=0, keepdims=True).astype(jnp.int32)
+
+
+def rotate_kernel(subs, direct, passages_ref, rotation_ref, codes_ref, after_ref, *refs):
     outs, turned_ref = refs[:-1], refs[-1]
     rows, model = passages_ref.shape
     width = model // subs
@@ -68,28 +87,22 @@
     rank = jnp.dot(flags.astype(BF16), strict_before(rows), preferred_element_type=F32)
     rank = jnp.where(mine, rank, -1.0)
     local = jnp.where(mine, local, 0)
-    high = (local // 128).astype(F32)
-    low = (local % 128).astype(F32)
-    slot = lax.broadcasted_iota(jnp.int32, (cap, rows), 0).astype(F32)
+    pad = max(128 // blocks, 1)
+    rank = jnp.transpose(jnp.concatenate([rank] * pad, axis=0))
+    local = jnp.transpose(jnp.concatenate([local.astype(F32)] * pad, axis=0))
+    slot = lax.broadcasted_iota(jnp.int32, (rows, cap), 1).astype(F32)
+    index = []
     for block in range(blocks):
-        chosen = (slot == rank[block : block + 1, :]).astype(F32).astype(BF16)
-        pair = jnp.concatenate(
-            [
-                jnp.broadcast_to(high[block : block + 1, :], (8, rows)),
-                jnp.broadcast_to(low[block : block + 1, :], (8, rows)),
-            ],
-            axis=0,
-        ).astype(BF16)
-        found = lax.dot_general(
-            pair, chosen, (((1,), (1,)), ((), ())), preferred_element_type=F32
+        chosen = slot == rank[:, block : block + 1]
+        index.append(
+            jnp.sum(jnp.where(chosen, local[:, block : block + 1], 0.0), axis=0, keepdims=True)
         )
-        row = (found[0:1, :] * 128.0 + found[8:9, :]).astype(jnp.int32)
-        index_ref[block : block + 1, :] = row
+    index = jnp.concatenate(index, axis=0).astype(jnp.int32)
+    index_ref[...] = index & -16
     move = pltpu.make_async_copy(index_ref, scalar_ref, sem)
     move.start()
-    within = lax.broadcasted_iota(jnp.int32, (blocks, cap), 1) % group
-    spot = (within * 16 + index_ref[...] % 16).astype(F32)
-    pad = max(128 // blocks, 1)
+    within = lax.broadcasted_iota(jnp.int32, (blocks, cap), 1) & (group - 1)
+    spot = (within * 16 + (index & 15)).astype(F32)
     spot = jnp.transpose(jnp.concatenate([spot] * pad, axis=0))
     lane = lax.broadcasted_iota(jnp.int32, (cap, group * 16), 1).astype(F32)
     move.wait()
@@ -98,7 +111,7 @@
         for start in range(0, cap, group):
             tiles = []
             for at in range(start, start + group):
-                base = pl.multiple_of((scalar_ref[block, at] // 16) * 16, 16)
+                base = pl.multiple_of(scalar_ref[block, at], 16)
                 tiles.append(centroids_ref[pl.ds(base, 16), :])
             value = jnp.dot(
                 chosen[start : start + group],
@@ -109,8 +122,9 @@
             outs[block // per][block % per, start : start + group, :] = value
 
 
-def lookup_kernel(held, lists, direct, cap, count, rows_ref, words_ref, *refs):
-    messages, (picked_ref, slot_ref, codes_ref, tally_ref) = refs[:count], refs[count:]
+def lookup_kernel(held, lists, direct, cap, count, rows_ref, codebook_ref, *refs):
+    messages, refs = refs[:count], refs[count:]
+    picked_ref, slot_ref, codes_ref, tally_ref, turned_ref, words_ref = refs
     if not direct:
         messages = [messages[0].at[at] for at in range(messages[0].shape[0])]
     subs = len(messages)
@@ -118,7 +132,7 @@
     rows = rows_ref.shape[1]
     spaces = codes_ref.shape[0]
     depth = width // spaces
-    words = words_ref.shape[1]
+    words = words_ref.shape[0] * 128
     halves = width // rows
     tail = spaces // halves
     me = lax.axis_index("lists")
@@ -141,17 +155,27 @@
             codes_ref[half * tail : (half + 1) * tail, at * rows : (at + 1) * rows] = messages[at][
                 rows:, half * rows : (half + 1) * rows
             ].astype(F32)
+    for at in range(0, words * depth, 128):
+        block = jnp.concatenate(
+            [codebook_ref[:, at : at + 128].astype(F32)] * (128 // spaces), axis=0
+        )
+        turned_ref[at : at + 128, :] = jnp.transpose(block)
+    for at in range(depth):
+        block = jnp.transpose(turned_ref[pl.ds(at, words, stride=depth), :])
+        for piece in range(words // 128):
+            words_ref[piece, pl.ds(at, spaces, stride=depth), :] = block[
+                :spaces, piece * 128 : (piece + 1) * 128
+            ]
     parts = []
     for space in range(spaces):
         line = codes_ref[space : space + 1, :].astype(jnp.int32)
-        table = words_ref[space * depth : (space + 1) * depth, :]
         cells = []
         for at in range(subs):
             index = jnp.broadcast_to(line[:, at * rows : (at + 1) * rows], (depth, rows))
             value = None
             for piece in range(words // 128):
                 got = jnp.take_along_axis(
-                    table[:, piece * 128 : (piece + 1) * 128], index & 127, axis=1
+                    words_ref[piece, space * depth : (space + 1) * depth, :], index & 127, axis=1
                 )
                 value = got if value is None else jnp.where(index >= piece * 128, got, value)
             cells.append(value)
@@ -284,16 +308,6 @@
     return lax.ppermute(value, axis, [(at, at ^ step) for at in range(count)])
 
 
-def gather_rows(table, at):
-    return lax.gather(
-        table,
-        at[:, None],
-        lax.GatherDimensionNumbers(offset_dims=(), collapsed_slice_dims=(0,), start_index_map=(0,)),
-        slice_sizes=(1,),
-        mode=lax.GatherScatterMode.PROMISE_IN_BOUNDS,
-    )
-
-
 def exchange(values, axis):
     return [values[0]] + [swap(values[step], axis, step) for step in range(1, len(values))]
 
@@ -315,13 +329,19 @@
     direct = max(lists, subs) <= DIRECT
     shape = jax.ShapeDtypeStruct
 
-    tables = gather_rows(list_slot, list_ids)
+    tables = call(
+        tables_kernel,
+        shape((1, rows), jnp.int32),
+        40_000_000,
+        4 * list_slot.shape[0],
+        list_ids.reshape(1, rows),
+        list_slot.reshape(-1, 128),
+    )
     if direct:
-        tables = tables.reshape(1, rows)
         tables = jnp.concatenate(exchange([tables] * subs, "sub"), axis=0)
         tables = exchange([tables] * lists, "lists")
     else:
-        tables = jnp.broadcast_to(tables[None, None, :], (lists * subs, 1, rows))
+        tables = jnp.broadcast_to(tables[None], (lists * subs, 1, rows))
         tables = [all_swap(tables, ("lists", "sub")).reshape(lists * subs, rows)]
 
     pieces = call(
@@ -339,6 +359,7 @@
             pltpu.SemaphoreType.DMA,
         ],
     )
+    fetched = pieces[0]
     if direct:
         pieces = exchange(pieces, "lists")
     else:
@@ -355,13 +376,12 @@
         passages,
         rotation,
         codes,
+        fetched,
+        loose=1,
         scratch=[pltpu.VMEM((codes.shape[1], rows), F32)],
     )
     messages = exchange(messages, "sub") if direct else [all_swap(messages[0], "sub")]
 
-    word_table = (
-        codebook.astype(F32).reshape(spaces, words, depth).transpose(0, 2, 1).reshape(width, words)
-    )
     picked, slot, codes_t, tally = call(
         functools.partial(lookup_kernel, held, lists, direct, cap, len(messages)),
         [
@@ -373,8 +393,9 @@
         1_000_000_000,
         2_000_000,
         tables[0],
-        word_table,
+        codebook,
         *messages,
+        scratch=[pltpu.VMEM((words * depth, 128), F32), pltpu.VMEM((words // 128, width, 128), F32)],
     )
     *rebuilt, residual = call(
         functools.partial(place_kernel, direct, len(messages)),

time: 62.6 us -> 56.4 us (0.901)
  local copies, waits for them, and re-layouts: 14.8 us -> 5.04 us
  waiting for transfers between devices: 8.19 us -> 17 us
  Pallas kernels: 17.7 us -> 11.5 us
  starting transfers between devices: 19.9 us -> 21.9 us
  other arithmetic: 0.72 us -> 0.01 us
    ppermute x18, waiting for transfers between devices: 8.19 us -> 17 us  [swap(): return lax.ppermute(value, axis, [(at, at ^ step) for at in range(count)])]
    pallas_call x7 -> x8, Pallas kernels: 17.7 us -> 11.5 us  [call(): pl.pallas_call(kernel, out_shape=out_shape, in_specs=[whole() for _ in ar...]
    unnamed x26 -> x14, local copies, waits for them, and re-layouts: 10.9 us -> 5.04 us
    reshape x2 -> x0, local copies, waits for them, and re-layouts: 2.75 us -> none  [body(): codebook.astype(F32).reshape(spaces, words, depth).transpose(0, 2, 1)]
    ppermute x18, starting transfers between devices: 19.9 us -> 21.9 us  [swap(): return lax.ppermute(value, axis, [(at, at ^ step) for at in range(count)])]
    gather x1 -> x0, local copies, waits for them, and re-layouts: 1.15 us -> none  [gather_rows(): lax.gather(table, at[:, None], lax.GatherDimensionNumbers(offset_dims=(),...]
    gather x1 -> x0, other arithmetic: 0.71 us -> none  [gather_rows(): lax.gather(table, at[:, None], lax.GatherDimensionNumbers(offset_dims=(),...]
  transfers between devices with their start and end apart: 18 -> 18, of which waited for: 4 -> 8; matrix products, arithmetic and copies ran while one was open for 4% -> 0% of each run, Pallas kernels for 20% -> 6%
where the time goes in v3:
time: 56.4 us; the launch traced here: 56.2 us
  starting transfers between devices  21.9 us (39%)
  waiting for transfers between devices  17 us (30%)
  Pallas kernels  11.5 us (20%)
  local copies, waits for them, and re-layouts  5.04 us (9%)
  between operations  0.75 us (1%)
    ppermute x18, starting transfers between devices, swap(): return lax.ppermute(value, axis, [(at, at ^ step) for at in range(count)])  21.9 us
    ppermute x18, waiting for transfers between devices, swap(): return lax.ppermute(value, axis, [(at, at ^ step) for at in range(count)])  17 us
    pallas_call x8, Pallas kernels, call(): pl.pallas_call(kernel, out_shape=out_shape, in_specs=[whole() for _ in ar...  11.5 us
    unnamed x14, local copies, waits for them, and re-layouts  5.04 us
  transfers between devices with their start and end apart: 18, of which 8 were waited for; matrix products, arithmetic and copies ran while one was open for 0% of the time, Pallas kernels for 6%

profile of v3, /device:TPU:0, one launch (start us, length us, event | category | flops | bytes accessed | tf_op | source)
XLA Modules:
  0.0 56.2 jit_solution(7789663203166578846)
XLA Ops:
  0.6 0.0 copy-start.2
  0.6 0.0 copy-start.3
  0.6 1.0 %copy-done.3 = s32[65536]{0:T(1024)S(1)} copy-done((s32[65536]{0:T(1024)S(1)}, s32[65536]{0:T(1024)}, u32[]{:S(2)}) %copy-start.3) | copy-done | bytes 262168
  1.6 0.0 copy-start.6
  1.6 0.7 %copy-done.6 = s32[128]{0:T(128)S(1)} copy-done((s32[128]{0:T(128)S(1)}, s32[128]{0:T(128)}, u32[]{:S(2)}) %copy-start.6) | copy-done | bytes 536
  2.3 0.4 shard_map.86
  2.7 2.4 %collective-permute-start.2 = (s32[1,128]{1,0:T(1,128)S(1)}, s32[1,128]{1,0:T(1,128)S(1)}, u32[]{:S(2)}, u32[]{:S(2)}) collective-permute-start(s32[1,128]{1,0:T(1,128)S(1)} %shard_map.86), channel_id=1, source_target_pairs={{0,3},{1,2},{2,1},{3,0},{4,7},{5,6},{6,5},{7,4},{8,11},{9,10},{10,... | collective-permute-start | bytes 1544 | tf_op jit(solution)/shard_map/ppermute | solution.py:308
  5.2 0.6 %collective-permute-start.1 = (s32[1,128]{1,0:T(1,128)S(1)}, s32[1,128]{1,0:T(1,128)S(1)}, u32[]{:S(2)}, u32[]{:S(2)}) collective-permute-start(s32[1,128]{1,0:T(1,128)S(1)} %shard_map.86), channel_id=1, source_target_pairs={{0,2},{1,3},{2,0},{3,1},{4,6},{5,7},{6,4},{7,5},{8,10},{9,11},{10,... | collective-permute-start | bytes 1544 | tf_op jit(solution)/shard_map/ppermute | solution.py:308
  5.8 0.0 collective-permute-start
  5.8 0.6 %collective-permute-done.2 = s32[1,128]{1,0:T(1,128)S(1)} collective-permute-done((s32[1,128]{1,0:T(1,128)S(1)}, s32[1,128]{1,0:T(1,128)S(1)}, u32[]{:S(2)}, u32[]{:S(2)}) %collective-permute-start.2) | collective-permute-done | bytes 544 | tf_op jit(solution)/shard_map/ppermute | solution.py:308
  6.5 2.2 %collective-permute-done.1 = s32[1,128]{1,0:T(1,128)S(1)} collective-permute-done((s32[1,128]{1,0:T(1,128)S(1)}, s32[1,128]{1,0:T(1,128)S(1)}, u32[]{:S(2)}, u32[]{:S(2)}) %collective-permute-start.1) | collective-permute-done | bytes 544 | tf_op jit(solution)/shard_map/ppermute | solution.py:308
  8.7 0.0 collective-permute-done
  8.7 3.7 %collective-permute-start.5 = (s32[4,128]{1,0:T(4,128)S(1)}, s32[4,128]{1,0:T(4,128)S(1)}, u32[]{:S(2)}, u32[]{:S(2)}) collective-permute-start(s32[4,128]{1,0:T(4,128)S(1)} %pad_add_fusion.refs_0_.rows_ref), channel_id=1, source_target_pairs={{0,12},{4,8},{8,4},{12,0},{1,13},{5,9},{9,5},{13,1},{2,14},{6,10},... | collective-permute-start | bytes 6152 | tf_op jit(solution)/shard_map/ppermute | solution.py:308
  12.4 0.0 collective-permute-start.4
  12.4 0.8 %collective-permute-start.3 = (s32[4,128]{1,0:T(4,128)S(1)}, s32[4,128]{1,0:T(4,128)S(1)}, u32[]{:S(2)}, u32[]{:S(2)}) collective-permute-start(s32[4,128]{1,0:T(4,128)S(1)} %pad_add_fusion.refs_0_.rows_ref), channel_id=1, source_target_pairs={{0,4},{4,0},{8,12},{12,8},{1,5},{5,1},{9,13},{13,9},{2,6},{6,2},{1... | collective-permute-start | bytes 6152 | tf_op jit(solution)/shard_map/ppermute | solution.py:308
  13.2 1.0 %collective-permute-done.5.refs_3_ = s32[4,128]{1,0:T(4,128)S(1)} collective-permute-done((s32[4,128]{1,0:T(4,128)S(1)}, s32[4,128]{1,0:T(4,128)S(1)}, u32[]{:S(2)}, u32[]{:S(2)}) %collective-permute-start.5) | collective-permute-done | bytes 2080 | tf_op jit(solution)/shard_map/ppermute | solution.py:308
  14.2 2.7 %collective-permute-done.4.refs_2_ = s32[4,128]{1,0:T(4,128)S(1)} collective-permute-done((s32[4,128]{1,0:T(4,128)S(1)}, s32[4,128]{1,0:T(4,128)S(1)}, u32[]{:S(2)}, u32[]{:S(2)}) %collective-permute-start.4) | collective-permute-done | bytes 2080 | tf_op jit(solution)/shard_map/ppermute | solution.py:308
  16.9 0.0 collective-permute-done.3.refs_1_
  16.9 0.0 copy-start
  16.9 3.4 %copy-done = bf16[16384,256]{1,0:T(8,128)(2,1)S(1)} copy-done((bf16[16384,256]{1,0:T(8,128)(2,1)S(1)}, bf16[16384,256]{1,0:T(8,128)(2,1)}, u32[]{:S(2)}) %copy-start) | copy-done | bytes 8388632
  20.3 0.0 copy-start.1
  20.3 0.0 copy-start.5
  20.3 0.0 copy-start.4
  20.3 2.8 %shard_map.87 = (bf16[4,64,256]{2,1,0:T(8,128)(2,1)S(1)}, bf16[4,64,256]{2,1,0:T(8,128)(2,1)S(1)}, bf16[4,64,256]{2,1,0:T(8,128)(2,1)S(1)}, bf16[4,64,256]{2,1,0:T(8,128)(2,1)S(1)}) custom-call(s32[4,128]{1,0:T(4,128)S(1)} %pad_add_fusion.refs_0_.rows_ref, s32[4,128]{1,0:T(4,128)S(1)} %collective-permute-done.3.refs_1_, ...), custom_call_target="tpu_custom_call" | custom-call | flops 600000000 | bytes 8388608 | tf_op jit(solution)/shard_map/pallas_call | solution.py:18
  23.1 0.0 copy-done.2
  23.1 0.0 copy-done.1
  23.1 0.0 copy-done.5
  23.1 0.5 shard_map.88
  23.6 0.1 collective-permute-start.6
  23.7 0.7 %collective-permute-start.7 = (bf16[144,256]{1,0:T(8,128)(2,1)S(1)}, bf16[144,256]{1,0:T(8,128)(2,1)S(1)}, u32[]{:S(2)}, u32[]{:S(2)}) collective-permute-start(bf16[144,256]{1,0:T(8,128)(2,1)S(1)} %get-tuple-element.26), channel_id=1, source_target_pairs={{0,2},{1,3},{2,0},{3,1},{4,6},{5,7},{6,4},{7,5},{8,10},{9,11},{10,... | collective-permute-start | bytes 221192 | tf_op jit(solution)/shard_map/ppermute | solution.py:308
  24.4 1.2 %collective-permute-start.8 = (bf16[144,256]{1,0:T(8,128)(2,1)S(1)}, bf16[144,256]{1,0:T(8,128)(2,1)S(1)}, u32[]{:S(2)}, u32[]{:S(2)}) collective-permute-start(bf16[144,256]{1,0:T(8,128)(2,1)S(1)} %get-tuple-element.27), channel_id=1, source_target_pairs={{0,3},{1,2},{2,1},{3,0},{4,7},{5,6},{6,5},{7,4},{8,11},{9,10},{10,... | collective-permute-start | bytes 221192 | tf_op jit(solution)/shard_map/ppermute | solution.py:308
  25.6 0.0 collective-permute-start.9
  25.6 2.0 %collective-permute-start.10 = (bf16[4,64,256]{2,1,0:T(8,128)(2,1)S(1)}, bf16[4,64,256]{2,1,0:T(8,128)(2,1)S(1)}, u32[]{:S(2)}, u32[]{:S(2)}) collective-permute-start(bf16[4,64,256]{2,1,0:T(8,128)(2,1)S(1)} %get-tuple-element.31), channel_id=1, source_target_pairs={{0,8},{4,12},{8,0},{12,4},{1,9},{5,13},{9,1},{13,5},{2,10},{6,14},... | collective-permute-start | bytes 393224 | tf_op jit(solution)/shard_map/ppermute | solution.py:308
  27.6 0.0 collective-permute-done.6.refs_1_
  27.6 2.4 %collective-permute-start.11 = (bf16[4,64,256]{2,1,0:T(8,128)(2,1)S(1)}, bf16[4,64,256]{2,1,0:T(8,128)(2,1)S(1)}, u32[]{:S(2)}, u32[]{:S(2)}) collective-permute-start(bf16[4,64,256]{2,1,0:T(8,128)(2,1)S(1)} %get-tuple-element.32), channel_id=1, source_target_pairs={{0,12},{4,8},{8,4},{12,0},{1,13},{5,9},{9,5},{13,1},{2,14},{6,10},... | collective-permute-start | bytes 393224 | tf_op jit(solution)/shard_map/ppermute | solution.py:308
  30.0 0.0 collective-permute-done.7.refs_2_
  30.0 0.0 collective-permute-done.8.refs_3_
  30.0 0.0 copy-done.4
  30.0 2.4 %shard_map.89 = (bf16[512,256]{1,0:T(8,128)(2,1)S(1)}, f32[128,128]{1,0:T(8,128)S(1)}, f32[32,512]{1,0:T(8,128)S(1)}, f32[256,128]{1,0:T(8,128)S(1)}) custom-call(s32[4,128]{1,0:T(4,128)S(1)} %pad_add_fusion.refs_0_.rows_ref, bf16[32,2048]{1,0:T(8,128)(2,1)S(1)} %copy-done.4, bf16[144,256]{1,0:T(8,128)(2,1)S(1)} %get-tuple-element.24.refs_0_, ...), custom_call_target="tpu_custom_call" | custom-call | flops 1000000000 | bytes 2000000 | tf_op jit(solution)/shard_map/pallas_call | solution.py:18
  32.4 1.7 %collective-permute-done.9.refs_5_ = bf16[4,64,256]{2,1,0:T(8,128)(2,1)S(1)} collective-permute-done((bf16[4,64,256]{2,1,0:T(8,128)(2,1)S(1)}, bf16[4,64,256]{2,1,0:T(8,128)(2,1)S(1)}, u32[]{:S(2)}, u32[]{:S(2)}) %collective-permute-start.9) | collective-permute-done | bytes 131104 | tf_op jit(solution)/shard_map/ppermute | solution.py:308
  34.1 0.0 collective-permute-done.10.refs_6_
  34.1 4.4 %collective-permute-done.11.refs_7_ = bf16[4,64,256]{2,1,0:T(8,128)(2,1)S(1)} collective-permute-done((bf16[4,64,256]{2,1,0:T(8,128)(2,1)S(1)}, bf16[4,64,256]{2,1,0:T(8,128)(2,1)S(1)}, u32[]{:S(2)}, u32[]{:S(2)}) %collective-permute-start.11) | collective-permute-done | bytes 131104 | tf_op jit(solution)/shard_map/ppermute | solution.py:308
  38.5 0.3 shard_map.90
  38.8 2.4 %shard_map.92 = (bf16[64,384]{1,0:T(8,128)(2,1)S(1)}, bf16[64,384]{1,0:T(8,128)(2,1)S(1)}, bf16[64,384]{1,0:T(8,128)(2,1)S(1)}, bf16[64,384]{1,0:T(8,128)(2,1)S(1)}) custom-call(f32[32,512]{1,0:T(8,128)S(1)} %get-tuple-element.37.codes_ref, bf16[512,256]{1,0:T(8,128)(2,1)S(1)} %get-tuple-element.38.residual_ref, f32[256,128]{1,0:T(8,128)S(1)} %get-tuple-element.39.tally_ref), custom_call_target="tpu_custom_call" | custom-call | flops 2000000000 | bytes 1000000 | tf_op jit(solution)/shard_map/pallas_call | solution.py:18
  41.2 2.8 %collective-permute-start.15 = (bf16[64,384]{1,0:T(8,128)(2,1)S(1)}, bf16[64,384]{1,0:T(8,128)(2,1)S(1)}, u32[]{:S(2)}, u32[]{:S(2)}) collective-permute-start(bf16[64,384]{1,0:T(8,128)(2,1)S(1)} %get-tuple-element.41), channel_id=1, source_target_pairs={{0,4},{4,0},{8,12},{12,8},{1,5},{5,1},{9,13},{13,9},{2,6},{6,2},{1... | collective-permute-start | bytes 147464 | tf_op jit(solution)/shard_map/ppermute | solution.py:308
  44.0 0.0 collective-permute-start.12
  44.0 0.6 %collective-permute-start.13 = (bf16[128,256]{1,0:T(8,128)(2,1)S(1)}, bf16[128,256]{1,0:T(8,128)(2,1)S(1)}, u32[]{:S(2)}, u32[]{:S(2)}) collective-permute-start(bf16[128,256]{1,0:T(8,128)(2,1)S(1)} %get-tuple-element.35), channel_id=1, source_target_pairs={{0,2},{1,3},{2,0},{3,1},{4,6},{5,7},{6,4},{7,5},{8,10},{9,11},{10,... | collective-permute-start | bytes 196616 | tf_op jit(solution)/shard_map/ppermute | solution.py:308
  44.6 1.2 %collective-permute-start.14 = (bf16[128,256]{1,0:T(8,128)(2,1)S(1)}, bf16[128,256]{1,0:T(8,128)(2,1)S(1)}, u32[]{:S(2)}, u32[]{:S(2)}) collective-permute-start(bf16[128,256]{1,0:T(8,128)(2,1)S(1)} %get-tuple-element.36), channel_id=1, source_target_pairs={{0,3},{1,2},{2,1},{3,0},{4,7},{5,6},{6,5},{7,4},{8,11},{9,10},{10,... | collective-permute-start | bytes 196616 | tf_op jit(solution)/shard_map/ppermute | solution.py:308
  45.9 1.8 %collective-permute-start.16 = (bf16[64,384]{1,0:T(8,128)(2,1)S(1)}, bf16[64,384]{1,0:T(8,128)(2,1)S(1)}, u32[]{:S(2)}, u32[]{:S(2)}) collective-permute-start(bf16[64,384]{1,0:T(8,128)(2,1)S(1)} %get-tuple-element.42), channel_id=1, source_target_pairs={{0,8},{4,12},{8,0},{12,4},{1,9},{5,13},{9,1},{13,5},{2,10},{6,14},... | collective-permute-start | bytes 147464 | tf_op jit(solution)/shard_map/ppermute | solution.py:308
  47.6 0.0 collective-permute-done.15.refs_1_
  47.6 1.6 %collective-permute-start.17 = (bf16[64,384]{1,0:T(8,128)(2,1)S(1)}, bf16[64,384]{1,0:T(8,128)(2,1)S(1)}, u32[]{:S(2)}, u32[]{:S(2)}) collective-permute-start(bf16[64,384]{1,0:T(8,128)(2,1)S(1)} %get-tuple-element.43), channel_id=1, source_target_pairs={{0,12},{4,8},{8,4},{12,0},{1,13},{5,9},{9,5},{13,1},{2,14},{6,10},... | collective-permute-start | bytes 147464 | tf_op jit(solution)/shard_map/ppermute | solution.py:308
  49.2 2.6 %collective-permute-done.16.refs_2_ = bf16[64,384]{1,0:T(8,128)(2,1)S(1)} collective-permute-done((bf16[64,384]{1,0:T(8,128)(2,1)S(1)}, bf16[64,384]{1,0:T(8,128)(2,1)S(1)}, u32[]{:S(2)}, u32[]{:S(2)}) %collective-permute-start.16) | collective-permute-done | bytes 49184 | tf_op jit(solution)/shard_map/ppermute | solution.py:308
  51.8 1.8 %collective-permute-done.17.refs_3_ = bf16[64,384]{1,0:T(8,128)(2,1)S(1)} collective-permute-done((bf16[64,384]{1,0:T(8,128)(2,1)S(1)}, bf16[64,384]{1,0:T(8,128)(2,1)S(1)}, u32[]{:S(2)}, u32[]{:S(2)}) %collective-permute-start.17) | collective-permute-done | bytes 49184 | tf_op jit(solution)/shard_map/ppermute | solution.py:308
  53.6 1.1 %shard_map.93 = f32[32,512]{1,0:T(8,128)} custom-call(bf16[32,2048]{1,0:T(8,128)(2,1)S(1)} %copy-done.4, bf16[64,384]{1,0:T(8,128)(2,1)S(1)} %get-tuple-element.40.refs_0_, bf16[64,384]{1,0:T(8,128)(2,1)S(1)} %collective-permute-done.15.refs_1_, bf16[64,384]{1,0:T(8,128)(2,1)S(1)} %collective-permute-done.16.refs_2_, ...), custom_call_target="tpu_custom_call" | custom-call | flops 100000000 | bytes 500000 | tf_op jit(solution)/shard_map/pallas_call | solution.py:18
  54.7 0.0 collective-permute-done.12.refs_1_
  54.7 0.0 collective-permute-done.13.refs_2_
  54.7 0.0 collective-permute-done.14.refs_3_
  54.7 1.5 %shard_map.91 = bf16[128,1024]{1,0:T(8,128)(2,1)} custom-call(bf16[128,1024]{1,0:T(8,128)(2,1)S(1)} %copy-done.2, bf16[1024,1024]{1,0:T(8,128)(2,1)S(1)} %copy-done.1, bf16[128,256]{1,0:T(8,128)(2,1)S(1)} %get-tuple-element.33.refs_0_, bf16[128,256]{1,0:T(8,128)(2,1)S(1)} %collective-permute-done.12.refs_1_, ...), custom_call_target="tpu_custom_call" | custom-call | flops 268435456 | bytes 2621440 | tf_op jit(solution)/shard_map/pallas_call | solution.py:18
  (1 shorter events, 0.0 us)
Async XLA Ops:
  0.6 22.5 %copy-start.2 = (bf16[128,1024]{1,0:T(8,128)(2,1)S(1)}, bf16[128,1024]{1,0:T(8,128)(2,1)}, u32[]{:S(2)}) copy-start(bf16[128,1024]{1,0:T(8,128)(2,1)} %passages_ref.3) | copy-start | bytes 786436
  0.6 1.0 %copy-start.3 = (s32[65536]{0:T(1024)S(1)}, s32[65536]{0:T(1024)}, u32[]{:S(2)}) copy-start(s32[65536]{0:T(1024)} %param.10) | copy-start | bytes 786436
  1.6 0.7 %copy-start.6 = (s32[128]{0:T(128)S(1)}, s32[128]{0:T(128)}, u32[]{:S(2)}) copy-start(s32[128]{0:T(128)} %param.11) | copy-start | bytes 1540
  2.7 3.7 %collective-permute-start.2 = (s32[1,128]{1,0:T(1,128)S(1)}, s32[1,128]{1,0:T(1,128)S(1)}, u32[]{:S(2)}, u32[]{:S(2)}) collective-permute-start(s32[1,128]{1,0:T(1,128)S(1)} %shard_map.86), channel_id=1, source_target_pairs={{0,3},{1,2},{2,1},{3,0},{4,7},{5,6},{6,5},{7,4},{8,11},{9,10},{10,... | collective-permute-start | bytes 1544 | tf_op jit(solution)/shard_map/ppermute | solution.py:308
  5.2 3.5 %collective-permute-start.1 = (s32[1,128]{1,0:T(1,128)S(1)}, s32[1,128]{1,0:T(1,128)S(1)}, u32[]{:S(2)}, u32[]{:S(2)}) collective-permute-start(s32[1,128]{1,0:T(1,128)S(1)} %shard_map.86), channel_id=1, source_target_pairs={{0,2},{1,3},{2,0},{3,1},{4,6},{5,7},{6,4},{7,5},{8,10},{9,11},{10,... | collective-permute-start | bytes 1544 | tf_op jit(solution)/shard_map/ppermute | solution.py:308
  5.8 2.9 %collective-permute-start = (s32[1,128]{1,0:T(1,128)S(1)}, s32[1,128]{1,0:T(1,128)S(1)}, u32[]{:S(2)}, u32[]{:S(2)}) collective-permute-start(s32[1,128]{1,0:T(1,128)S(1)} %shard_map.86), channel_id=1, source_target_pairs={{0,1},{1,0},{2,3},{3,2},{4,5},{5,4},{6,7},{7,6},{8,9},{9,8},{10,11... | collective-permute-start | bytes 1544 | tf_op jit(solution)/shard_map/ppermute | solution.py:308
  8.7 5.4 %collective-permute-start.5 = (s32[4,128]{1,0:T(4,128)S(1)}, s32[4,128]{1,0:T(4,128)S(1)}, u32[]{:S(2)}, u32[]{:S(2)}) collective-permute-start(s32[4,128]{1,0:T(4,128)S(1)} %pad_add_fusion.refs_0_.rows_ref), channel_id=1, source_target_pairs={{0,12},{4,8},{8,4},{12,0},{1,13},{5,9},{9,5},{13,1},{2,14},{6,10},... | collective-permute-start | bytes 6152 | tf_op jit(solution)/shard_map/ppermute | solution.py:308
  12.4 4.5 %collective-permute-start.4 = (s32[4,128]{1,0:T(4,128)S(1)}, s32[4,128]{1,0:T(4,128)S(1)}, u32[]{:S(2)}, u32[]{:S(2)}) collective-permute-start(s32[4,128]{1,0:T(4,128)S(1)} %pad_add_fusion.refs_0_.rows_ref), channel_id=1, source_target_pairs={{0,8},{4,12},{8,0},{12,4},{1,9},{5,13},{9,1},{13,5},{2,10},{6,14},... | collective-permute-start | bytes 6152 | tf_op jit(solution)/shard_map/ppermute | solution.py:308
  12.4 4.5 %collective-permute-start.3 = (s32[4,128]{1,0:T(4,128)S(1)}, s32[4,128]{1,0:T(4,128)S(1)}, u32[]{:S(2)}, u32[]{:S(2)}) collective-permute-start(s32[4,128]{1,0:T(4,128)S(1)} %pad_add_fusion.refs_0_.rows_ref), channel_id=1, source_target_pairs={{0,4},{4,0},{8,12},{12,8},{1,5},{5,1},{9,13},{13,9},{2,6},{6,2},{1... | collective-permute-start | bytes 6152 | tf_op jit(solution)/shard_map/ppermute | solution.py:308
  16.9 3.4 %copy-start = (bf16[16384,256]{1,0:T(8,128)(2,1)S(1)}, bf16[16384,256]{1,0:T(8,128)(2,1)}, u32[]{:S(2)}) copy-start(bf16[16384,256]{1,0:T(8,128)(2,1)} %refs_4_.1) | copy-start | bytes 25165828
  20.3 2.9 %copy-start.1 = (bf16[1024,1024]{1,0:T(8,128)(2,1)S(1)}, bf16[1024,1024]{1,0:T(8,128)(2,1)}, u32[]{:S(2)}) copy-start(bf16[1024,1024]{1,0:T(8,128)(2,1)} %rotation_ref.3) | copy-start | bytes 6291460
  20.3 2.9 %copy-start.5 = (s32[128,128]{1,0:T(8,128)S(1)}, s32[128,128]{1,0:T(8,128)}, u32[]{:S(2)}) copy-start(s32[128,128]{1,0:T(8,128)} %codes_ref.1) | copy-start | bytes 196612
  20.3 9.7 %copy-start.4 = (bf16[32,2048]{1,0:T(8,128)(2,1)S(1)}, bf16[32,2048]{1,0:T(8,128)(2,1)}, u32[]{:S(2)}) copy-start(bf16[32,2048]{1,0:T(8,128)(2,1)} %codebook_ref.3) | copy-start | bytes 393220
  23.6 4.0 %collective-permute-start.6 = (bf16[144,256]{1,0:T(8,128)(2,1)S(1)}, bf16[144,256]{1,0:T(8,128)(2,1)S(1)}, u32[]{:S(2)}, u32[]{:S(2)}) collective-permute-start(bf16[144,256]{1,0:T(8,128)(2,1)S(1)} %get-tuple-element.25), channel_id=1, source_target_pairs={{0,1},{1,0},{2,3},{3,2},{4,5},{5,4},{6,7},{7,6},{8,9},{9,8},{10,11... | collective-permute-start | bytes 221192 | tf_op jit(solution)/shard_map/ppermute | solution.py:308
  23.7 6.3 %collective-permute-start.7 = (bf16[144,256]{1,0:T(8,128)(2,1)S(1)}, bf16[144,256]{1,0:T(8,128)(2,1)S(1)}, u32[]{:S(2)}, u32[]{:S(2)}) collective-permute-start(bf16[144,256]{1,0:T(8,128)(2,1)S(1)} %get-tuple-element.26), channel_id=1, source_target_pairs={{0,2},{1,3},{2,0},{3,1},{4,6},{5,7},{6,4},{7,5},{8,10},{9,11},{10,... | collective-permute-start | bytes 221192 | tf_op jit(solution)/shard_map/ppermute | solution.py:308
  24.4 5.6 %collective-permute-start.8 = (bf16[144,256]{1,0:T(8,128)(2,1)S(1)}, bf16[144,256]{1,0:T(8,128)(2,1)S(1)}, u32[]{:S(2)}, u32[]{:S(2)}) collective-permute-start(bf16[144,256]{1,0:T(8,128)(2,1)S(1)} %get-tuple-element.27), channel_id=1, source_target_pairs={{0,3},{1,2},{2,1},{3,0},{4,7},{5,6},{6,5},{7,4},{8,11},{9,10},{10,... | collective-permute-start | bytes 221192 | tf_op jit(solution)/shard_map/ppermute | solution.py:308
  25.6 8.6 %collective-permute-start.9 = (bf16[4,64,256]{2,1,0:T(8,128)(2,1)S(1)}, bf16[4,64,256]{2,1,0:T(8,128)(2,1)S(1)}, u32[]{:S(2)}, u32[]{:S(2)}) collective-permute-start(bf16[4,64,256]{2,1,0:T(8,128)(2,1)S(1)} %get-tuple-element.30), channel_id=1, source_target_pairs={{0,4},{4,0},{8,12},{12,8},{1,5},{5,1},{9,13},{13,9},{2,6},{6,2},{1... | collective-permute-start | bytes 393224 | tf_op jit(solution)/shard_map/ppermute | solution.py:308
  25.6 8.6 %collective-permute-start.10 = (bf16[4,64,256]{2,1,0:T(8,128)(2,1)S(1)}, bf16[4,64,256]{2,1,0:T(8,128)(2,1)S(1)}, u32[]{:S(2)}, u32[]{:S(2)}) collective-permute-start(bf16[4,64,256]{2,1,0:T(8,128)(2,1)S(1)} %get-tuple-element.31), channel_id=1, source_target_pairs={{0,8},{4,12},{8,0},{12,4},{1,9},{5,13},{9,1},{13,5},{2,10},{6,14},... | collective-permute-start | bytes 393224 | tf_op jit(solution)/shard_map/ppermute | solution.py:308
  27.6 10.9 %collective-permute-start.11 = (bf16[4,64,256]{2,1,0:T(8,128)(2,1)S(1)}, bf16[4,64,256]{2,1,0:T(8,128)(2,1)S(1)}, u32[]{:S(2)}, u32[]{:S(2)}) collective-permute-start(bf16[4,64,256]{2,1,0:T(8,128)(2,1)S(1)} %get-tuple-element.32), channel_id=1, source_target_pairs={{0,12},{4,8},{8,4},{12,0},{1,13},{5,9},{9,5},{13,1},{2,14},{6,10},... | collective-permute-start | bytes 393224 | tf_op jit(solution)/shard_map/ppermute | solution.py:308
  41.2 6.5 %collective-permute-start.15 = (bf16[64,384]{1,0:T(8,128)(2,1)S(1)}, bf16[64,384]{1,0:T(8,128)(2,1)S(1)}, u32[]{:S(2)}, u32[]{:S(2)}) collective-permute-start(bf16[64,384]{1,0:T(8,128)(2,1)S(1)} %get-tuple-element.41), channel_id=1, source_target_pairs={{0,4},{4,0},{8,12},{12,8},{1,5},{5,1},{9,13},{13,9},{2,6},{6,2},{1... | collective-permute-start | bytes 147464 | tf_op jit(solution)/shard_map/ppermute | solution.py:308
  44.0 10.7 %collective-permute-start.12 = (bf16[128,256]{1,0:T(8,128)(2,1)S(1)}, bf16[128,256]{1,0:T(8,128)(2,1)S(1)}, u32[]{:S(2)}, u32[]{:S(2)}) collective-permute-start(bf16[128,256]{1,0:T(8,128)(2,1)S(1)} %get-tuple-element.34), channel_id=1, source_target_pairs={{0,1},{1,0},{2,3},{3,2},{4,5},{5,4},{6,7},{7,6},{8,9},{9,8},{10,11... | collective-permute-start | bytes 196616 | tf_op jit(solution)/shard_map/ppermute | solution.py:308
  44.0 10.7 %collective-permute-start.13 = (bf16[128,256]{1,0:T(8,128)(2,1)S(1)}, bf16[128,256]{1,0:T(8,128)(2,1)S(1)}, u32[]{:S(2)}, u32[]{:S(2)}) collective-permute-start(bf16[128,256]{1,0:T(8,128)(2,1)S(1)} %get-tuple-element.35), channel_id=1, source_target_pairs={{0,2},{1,3},{2,0},{3,1},{4,6},{5,7},{6,4},{7,5},{8,10},{9,11},{10,... | collective-permute-start | bytes 196616 | tf_op jit(solution)/shard_map/ppermute | solution.py:308
  44.6 10.0 %collective-permute-start.14 = (bf16[128,256]{1,0:T(8,128)(2,1)S(1)}, bf16[128,256]{1,0:T(8,128)(2,1)S(1)}, u32[]{:S(2)}, u32[]{:S(2)}) collective-permute-start(bf16[128,256]{1,0:T(8,128)(2,1)S(1)} %get-tuple-element.36), channel_id=1, source_target_pairs={{0,3},{1,2},{2,1},{3,0},{4,7},{5,6},{6,5},{7,4},{8,11},{9,10},{10,... | collective-permute-start | bytes 196616 | tf_op jit(solution)/shard_map/ppermute | solution.py:308
  45.9 6.0 %collective-permute-start.16 = (bf16[64,384]{1,0:T(8,128)(2,1)S(1)}, bf16[64,384]{1,0:T(8,128)(2,1)S(1)}, u32[]{:S(2)}, u32[]{:S(2)}) collective-permute-start(bf16[64,384]{1,0:T(8,128)(2,1)S(1)} %get-tuple-element.42), channel_id=1, source_target_pairs={{0,8},{4,12},{8,0},{12,4},{1,9},{5,13},{9,1},{13,5},{2,10},{6,14},... | collective-permute-start | bytes 147464 | tf_op jit(solution)/shard_map/ppermute | solution.py:308
  47.6 5.9 %collective-permute-start.17 = (bf16[64,384]{1,0:T(8,128)(2,1)S(1)}, bf16[64,384]{1,0:T(8,128)(2,1)S(1)}, u32[]{:S(2)}, u32[]{:S(2)}) collective-permute-start(bf16[64,384]{1,0:T(8,128)(2,1)S(1)} %get-tuple-element.43), channel_id=1, source_target_pairs={{0,12},{4,8},{8,4},{12,0},{1,13},{5,9},{9,5},{13,1},{2,14},{6,10},... | collective-permute-start | bytes 147464 | tf_op jit(solution)/shard_map/ppermute | solution.py:308

commit v4 on v3

--- a/solution.py
+++ b/solution.py
@@ -10,10 +10,11 @@
 BF16 = jnp.bfloat16
 F32 = jnp.float32
 VMEM_LIMIT = 32 * 1024 * 1024
+MERGE_FLOPS = 6_000_000_000
 DIRECT = 4
 
 
-def call(kernel, out_shape, flops, nbytes, *args, scratch=(), loose=0):
+def call(kernel, out_shape, flops, nbytes, *args, scratch=(), loose=0, limit=VMEM_LIMIT):
     whole = lambda: pl.BlockSpec(memory_space=pltpu.VMEM)
     return pl.pallas_call(
         kernel,
@@ -22,7 +23,7 @@
         + [pl.BlockSpec(memory_space=pl.ANY)] * loose,
         out_specs=jax.tree.map(lambda _: whole(), out_shape),
         scratch_shapes=list(scratch),
-        compiler_params=pltpu.CompilerParams(vmem_limit_bytes=VMEM_LIMIT),
+        compiler_params=pltpu.CompilerParams(vmem_limit_bytes=limit),
         cost_estimate=pl.CostEstimate(flops=flops, bytes_accessed=nbytes, transcendentals=0),
     )(*args)
 
@@ -49,6 +50,11 @@
     lane = lax.broadcasted_iota(jnp.int32, (rows, 128), 1)
     found = jnp.transpose(jnp.where(lane == (ids & 127), found, 0.0))
     out_ref[...] = jnp.sum(found, axis=0, keepdims=True).astype(jnp.int32)
+
+
+def merge_kernel(*refs):
+    for at, ref in enumerate(refs[:-1]):
+        refs[-1][at : at + 1, :] = ref[...]
 
 
 def rotate_kernel(subs, direct, passages_ref, rotation_ref, codes_ref, after_ref, *refs):
@@ -212,7 +218,7 @@
         residual_ref[span, :] = (messages[at][:rows, :].astype(F32) - centre).astype(BF16)
 
 
-def sums_kernel(lists, direct, codes_ref, residual_ref, tally_ref, *refs):
+def sums_kernel(lists, direct, codes_ref, residual_ref, tally_ref, after_ref, *refs):
     outs, total_ref = refs[:-1], refs[-1]
     spaces, rows = codes_ref.shape
     width = residual_ref.shape[1]
@@ -281,7 +287,7 @@
 
 
 def restore_kernel(direct, passages_ref, rotation_ref, *refs):
-    pieces, out_ref = refs[:-1], refs[-1]
+    pieces, out_ref = refs[:-2], refs[-1]
     me = lax.axis_index("sub")
     if direct:
         blocks = [piece[...] for piece in pieces]
@@ -312,6 +318,14 @@
     return [values[0]] + [swap(values[step], axis, step) for step in range(1, len(values))]
 
 
+def spread(value, axis):
+    values, step = [value], 1
+    while step < lax.axis_size(axis):
+        values += [swap(one, axis, step) for one in values]
+        step *= 2
+    return values
+
+
 def all_swap(value, axis):
     return lax.all_to_all(value, axis, split_axis=0, concat_axis=0, tiled=True)
 
@@ -332,14 +346,20 @@
     tables = call(
         tables_kernel,
         shape((1, rows), jnp.int32),
-        40_000_000,
-        4 * list_slot.shape[0],
+        1_000,
+        0,
         list_ids.reshape(1, rows),
         list_slot.reshape(-1, 128),
     )
     if direct:
-        tables = jnp.concatenate(exchange([tables] * subs, "sub"), axis=0)
-        tables = exchange([tables] * lists, "lists")
+        tables = call(
+            merge_kernel,
+            shape((subs, rows), jnp.int32),
+            MERGE_FLOPS,
+            4 * subs * rows,
+            *spread(tables, "sub"),
+        )
+        tables = spread(tables, "lists")
     else:
         tables = jnp.broadcast_to(tables[None], (lists * subs, 1, rows))
         tables = [all_swap(tables, ("lists", "sub")).reshape(lists * subs, rows)]
@@ -359,7 +379,6 @@
             pltpu.SemaphoreType.DMA,
         ],
     )
-    fetched = pieces[0]
     if direct:
         pieces = exchange(pieces, "lists")
     else:
@@ -371,12 +390,12 @@
     messages = call(
         functools.partial(rotate_kernel, subs, direct),
         [shape((long, width), BF16)] * subs if direct else [shape((subs, long, width), BF16)],
-        2 * rows * model * model,
-        2 * model * model + 4 * rows * model,
+        1_000_000,
+        1_000,
         passages,
         rotation,
         codes,
-        fetched,
+        pieces[1] if direct else tables[0],
         loose=1,
         scratch=[pltpu.VMEM((codes.shape[1], rows), F32)],
     )
@@ -390,8 +409,8 @@
             shape((spaces, subs * rows), F32),
             shape((words, 128), F32),
         ],
-        1_000_000_000,
-        2_000_000,
+        1_000_000,
+        1_000,
         tables[0],
         codebook,
         *messages,
@@ -419,6 +438,8 @@
         codes_t,
         residual,
         tally,
+        rebuilt[1] if direct else residual,
+        loose=1,
         scratch=[pltpu.VMEM((words, width), F32)],
     )
     sums = exchange(sums, "lists") if direct else [all_swap(sums[0], "lists")]
@@ -430,6 +451,8 @@
         passages,
         rotation,
         *rebuilt,
+        sums[1] if direct else sums[0],
+        loose=1,
     )
     new_codebook = call(
         functools.partial(refine_kernel, spaces, direct),

time: 56.4 us -> 53.3 us (0.945)
  local copies, waits for them, and re-layouts: 5.04 us -> 1.63 us
  starting transfers between devices: 21.9 us -> 23.1 us
  waiting for transfers between devices: 17 us -> 16.2 us
    unnamed x14 -> x16, local copies, waits for them, and re-layouts: 5.04 us -> 1.63 us
    ppermute x18, starting transfers between devices: 21.9 us -> 23.1 us  [swap(): return lax.ppermute(value, axis, [(at, at ^ step) for at in range(count)])]
    ppermute x18, waiting for transfers between devices: 17 us -> 16.2 us  [swap(): return lax.ppermute(value, axis, [(at, at ^ step) for at in range(count)])]
    pallas_call x8 -> x9, Pallas kernels: 11.5 us -> 11.4 us  [call(): pl.pallas_call(kernel, out_shape=out_shape, in_specs=[whole() for _ in ar...]
  transfers between devices with their start and end apart: 18 -> 18, of which waited for: 8 -> 8; matrix products, arithmetic and copies ran while one was open for 0% -> 0% of each run, Pallas kernels for 6% -> 12%
where the time goes in v4:
time: 53.3 us; the launch traced here: 53.1 us
  starting transfers between devices  23.1 us (43%)
  waiting for transfers between devices  16.2 us (30%)
  Pallas kernels  11.4 us (21%)
  local copies, waits for them, and re-layouts  1.63 us (3%)
  between operations  0.76 us (1%)
    ppermute x18, starting transfers between devices, swap(): return lax.ppermute(value, axis, [(at, at ^ step) for at in range(count)])  23.1 us
    ppermute x18, waiting for transfers between devices, swap(): return lax.ppermute(value, axis, [(at, at ^ step) for at in range(count)])  16.2 us
    pallas_call x9, Pallas kernels, call(): pl.pallas_call(kernel, out_shape=out_shape, in_specs=[whole() for _ in ar...  11.4 us
    unnamed x16, local copies, waits for them, and re-layouts  1.63 us
  transfers between devices with their start and end apart: 18, of which 8 were waited for; matrix products, arithmetic and copies ran while one was open for 0% of the time, Pallas kernels for 12%

profile of v4, /device:TPU:0, one launch (start us, length us, event | category | flops | bytes accessed | tf_op | source)
XLA Modules:
  0.0 53.1 jit_solution(18083682068559095560)
XLA Ops:
  0.6 0.0 copy-start.3
  0.6 0.9 %copy-done.3 = s32[65536]{0:T(1024)S(1)} copy-done((s32[65536]{0:T(1024)S(1)}, s32[65536]{0:T(1024)}, u32[]{:S(2)}) %copy-start.3) | copy-done | bytes 262168
  1.6 0.0 copy-start.5
  1.6 0.7 %copy-done.5 = s32[128]{0:T(128)S(1)} copy-done((s32[128]{0:T(128)S(1)}, s32[128]{0:T(128)}, u32[]{:S(2)}) %copy-start.5) | copy-done | bytes 536
  2.2 0.0 slice-start
  2.2 0.4 shard_map.86.refs_0_
  2.7 0.0 slice-start.1
  2.7 0.5 collective-permute-start
  3.2 2.6 %collective-permute-start.1 = (s32[1,128]{1,0:T(1,128)S(1)}, s32[1,128]{1,0:T(1,128)S(1)}, u32[]{:S(2)}, u32[]{:S(2)}) collective-permute-start(s32[1,128]{1,0:T(1,128)S(1)} %shard_map.86.refs_0_), channel_id=1, source_target_pairs={{0,2},{1,3},{2,0},{3,1},{4,6},{5,7},{6,4},{7,5},{8,10},{9,11},{10,... | collective-permute-start | bytes 1544 | tf_op jit(solution)/shard_map/ppermute | solution.py:314
  5.8 0.0 collective-permute-done.refs_1_
  5.8 1.0 %collective-permute-start.2 = (s32[1,128]{1,0:T(1,128)S(1)}, s32[1,128]{1,0:T(1,128)S(1)}, u32[]{:S(2)}, u32[]{:S(2)}) collective-permute-start(s32[1,128]{1,0:T(1,128)S(1)} %collective-permute-done.refs_1_), channel_id=1, source_target_pairs={{0,2},{1,3},{2,0},{3,1},{4,6},{5,7},{6,4},{7,5},{8,10},{9,11},{10,... | collective-permute-start | bytes 1544 | tf_op jit(solution)/shard_map/ppermute | solution.py:314
  6.8 0.5 collective-permute-done.1.refs_2_
  7.3 2.0 %collective-permute-done.2.refs_3_ = s32[1,128]{1,0:T(1,128)S(1)} collective-permute-done((s32[1,128]{1,0:T(1,128)S(1)}, s32[1,128]{1,0:T(1,128)S(1)}, u32[]{:S(2)}, u32[]{:S(2)}) %collective-permute-start.2) | collective-permute-done | bytes 544 | tf_op jit(solution)/shard_map/ppermute | solution.py:314
  9.3 0.0 copy-start
  9.3 0.0 copy-start.1
  9.3 0.0 copy-start.4
  9.3 0.0 copy-start.2
  9.3 1.6 %collective-permute-start.3 = (s32[4,128]{1,0:T(4,128)S(1)}, s32[4,128]{1,0:T(4,128)S(1)}, u32[]{:S(2)}, u32[]{:S(2)}) collective-permute-start(s32[4,128]{1,0:T(4,128)S(1)} %shard_map.87.refs_0_.rows_ref), channel_id=1, source_target_pairs={{0,4},{4,0},{8,12},{12,8},{1,5},{5,1},{9,13},{13,9},{2,6},{6,2},{1... | collective-permute-start | bytes 6152 | tf_op jit(solution)/shard_map/ppermute | solution.py:314
  11.0 2.6 %collective-permute-start.4 = (s32[4,128]{1,0:T(4,128)S(1)}, s32[4,128]{1,0:T(4,128)S(1)}, u32[]{:S(2)}, u32[]{:S(2)}) collective-permute-start(s32[4,128]{1,0:T(4,128)S(1)} %shard_map.87.refs_0_.rows_ref), channel_id=1, source_target_pairs={{0,8},{4,12},{8,0},{12,4},{1,9},{5,13},{9,1},{13,5},{2,10},{6,14},... | collective-permute-start | bytes 6152 | tf_op jit(solution)/shard_map/ppermute | solution.py:314
  13.6 0.0 collective-permute-done.3.refs_1_
  13.6 2.0 %collective-permute-start.5 = (s32[4,128]{1,0:T(4,128)S(1)}, s32[4,128]{1,0:T(4,128)S(1)}, u32[]{:S(2)}, u32[]{:S(2)}) collective-permute-start(s32[4,128]{1,0:T(4,128)S(1)} %collective-permute-done.3.refs_1_), channel_id=1, source_target_pairs={{0,8},{4,12},{8,0},{12,4},{1,9},{5,13},{9,1},{13,5},{2,10},{6,14},... | collective-permute-start | bytes 6152 | tf_op jit(solution)/shard_map/ppermute | solution.py:314
  15.6 0.0 collective-permute-done.4.refs_2_
  15.6 2.5 %collective-permute-done.5.refs_3_ = s32[4,128]{1,0:T(4,128)S(1)} collective-permute-done((s32[4,128]{1,0:T(4,128)S(1)}, s32[4,128]{1,0:T(4,128)S(1)}, u32[]{:S(2)}, u32[]{:S(2)}) %collective-permute-start.5) | collective-permute-done | bytes 2080 | tf_op jit(solution)/shard_map/ppermute | solution.py:314
  18.1 0.0 slice-done
  18.1 0.0 slice-done.1
  18.1 2.8 %shard_map.88 = (bf16[4,64,256]{2,1,0:T(8,128)(2,1)S(1)}, bf16[4,64,256]{2,1,0:T(8,128)(2,1)S(1)}, bf16[4,64,256]{2,1,0:T(8,128)(2,1)S(1)}, bf16[4,64,256]{2,1,0:T(8,128)(2,1)S(1)}) custom-call(s32[4,128]{1,0:T(4,128)S(1)} %shard_map.87.refs_0_.rows_ref, s32[4,128]{1,0:T(4,128)S(1)} %collective-permute-done.3.refs_1_, ...), custom_call_target="tpu_custom_call" | custom-call | flops 600000000 | bytes 8388608 | tf_op jit(solution)/shard_map/pallas_call | solution.py:19
  20.9 1.1 %collective-permute-start.6 = (bf16[4,64,256]{2,1,0:T(8,128)(2,1)S(1)}, bf16[4,64,256]{2,1,0:T(8,128)(2,1)S(1)}, u32[]{:S(2)}, u32[]{:S(2)}) collective-permute-start(bf16[4,64,256]{2,1,0:T(8,128)(2,1)S(1)} %get-tuple-element.23), channel_id=1, source_target_pairs={{0,4},{4,0},{8,12},{12,8},{1,5},{5,1},{9,13},{13,9},{2,6},{6,2},{1... | collective-permute-start | bytes 393224 | tf_op jit(solution)/shard_map/ppermute | solution.py:314
  22.0 2.6 %collective-permute-start.10 = (bf16[4,64,256]{2,1,0:T(8,128)(2,1)S(1)}, bf16[4,64,256]{2,1,0:T(8,128)(2,1)S(1)}, u32[]{:S(2)}, u32[]{:S(2)}) collective-permute-start(bf16[4,64,256]{2,1,0:T(8,128)(2,1)S(1)} %get-tuple-element.31), channel_id=1, source_target_pairs={{0,8},{4,12},{8,0},{12,4},{1,9},{5,13},{9,1},{13,5},{2,10},{6,14},... | collective-permute-start | bytes 393224 | tf_op jit(solution)/shard_map/ppermute | solution.py:314
  24.6 0.8 %collective-permute-start.11 = (bf16[4,64,256]{2,1,0:T(8,128)(2,1)S(1)}, bf16[4,64,256]{2,1,0:T(8,128)(2,1)S(1)}, u32[]{:S(2)}, u32[]{:S(2)}) collective-permute-start(bf16[4,64,256]{2,1,0:T(8,128)(2,1)S(1)} %get-tuple-element.32), channel_id=1, source_target_pairs={{0,12},{4,8},{8,4},{12,0},{1,13},{5,9},{9,5},{13,1},{2,14},{6,10},... | collective-permute-start | bytes 393224 | tf_op jit(solution)/shard_map/ppermute | solution.py:314
  25.4 2.8 %collective-permute-done.6.after_ref.refs_5_ = bf16[4,64,256]{2,1,0:T(8,128)(2,1)S(1)} collective-permute-done((bf16[4,64,256]{2,1,0:T(8,128)(2,1)S(1)}, bf16[4,64,256]{2,1,0:T(8,128)(2,1)S(1)}, u32[]{:S(2)}, u32[]{:S(2)}) %collective-permute-start.6) | collective-permute-done | bytes 131104 | tf_op jit(solution)/shard_map/ppermute | solution.py:314
  28.2 0.0 copy-done
  28.2 0.0 copy-done.1
  28.2 0.0 copy-done.4
  28.2 0.5 shard_map.89
  28.7 0.1 collective-permute-start.7
  28.7 1.1 %collective-permute-start.8 = (bf16[144,256]{1,0:T(8,128)(2,1)S(1)}, bf16[144,256]{1,0:T(8,128)(2,1)S(1)}, u32[]{:S(2)}, u32[]{:S(2)}) collective-permute-start(bf16[144,256]{1,0:T(8,128)(2,1)S(1)} %get-tuple-element.26), channel_id=1, source_target_pairs={{0,2},{1,3},{2,0},{3,1},{4,6},{5,7},{6,4},{7,5},{8,10},{9,11},{10,... | collective-permute-start | bytes 221192 | tf_op jit(solution)/shard_map/ppermute | solution.py:314
  29.8 0.8 %collective-permute-start.9 = (bf16[144,256]{1,0:T(8,128)(2,1)S(1)}, bf16[144,256]{1,0:T(8,128)(2,1)S(1)}, u32[]{:S(2)}, u32[]{:S(2)}) collective-permute-start(bf16[144,256]{1,0:T(8,128)(2,1)S(1)} %get-tuple-element.27), channel_id=1, source_target_pairs={{0,3},{1,2},{2,1},{3,0},{4,7},{5,6},{6,5},{7,4},{8,11},{9,10},{10,... | collective-permute-start | bytes 221192 | tf_op jit(solution)/shard_map/ppermute | solution.py:314
  30.6 0.0 collective-permute-done.7.refs_1_
  30.6 3.3 %collective-permute-done.8.refs_2_ = bf16[144,256]{1,0:T(8,128)(2,1)S(1)} collective-permute-done((bf16[144,256]{1,0:T(8,128)(2,1)S(1)}, bf16[144,256]{1,0:T(8,128)(2,1)S(1)}, u32[]{:S(2)}, u32[]{:S(2)}) %collective-permute-start.8) | collective-permute-done | bytes 73760 | tf_op jit(solution)/shard_map/ppermute | solution.py:314
  33.9 0.7 %collective-permute-done.9.refs_3_ = bf16[144,256]{1,0:T(8,128)(2,1)S(1)} collective-permute-done((bf16[144,256]{1,0:T(8,128)(2,1)S(1)}, bf16[144,256]{1,0:T(8,128)(2,1)S(1)}, u32[]{:S(2)}, u32[]{:S(2)}) %collective-permute-start.9) | collective-permute-done | bytes 73760 | tf_op jit(solution)/shard_map/ppermute | solution.py:314
  34.5 0.0 copy-done.2
  34.6 2.4 %shard_map.90 = (bf16[512,256]{1,0:T(8,128)(2,1)S(1)}, f32[128,128]{1,0:T(8,128)S(1)}, f32[32,512]{1,0:T(8,128)S(1)}, f32[256,128]{1,0:T(8,128)S(1)}) custom-call(s32[4,128]{1,0:T(4,128)S(1)} %shard_map.87.refs_0_.rows_ref, bf16[32,2048]{1,0:T(8,128)(2,1)S(1)} %copy-done.2, bf16[144,256]{1,0:T(8,128)(2,1)S(1)} %get-tuple-element.24.refs_0_, ...), custom_call_target="tpu_custom_call" | custom-call | flops 1000000 | bytes 1000 | tf_op jit(solution)/shard_map/pallas_call | solution.py:19
  37.0 0.0 collective-permute-done.10.refs_6_
  37.0 0.0 collective-permute-done.11.refs_7_
  37.0 0.3 shard_map.91
  37.3 0.3 collective-permute-start.12
  37.6 1.0 %collective-permute-start.13 = (bf16[128,256]{1,0:T(8,128)(2,1)S(1)}, bf16[128,256]{1,0:T(8,128)(2,1)S(1)}, u32[]{:S(2)}, u32[]{:S(2)}) collective-permute-start(bf16[128,256]{1,0:T(8,128)(2,1)S(1)} %get-tuple-element.35), channel_id=1, source_target_pairs={{0,2},{1,3},{2,0},{3,1},{4,6},{5,7},{6,4},{7,5},{8,10},{9,11},{10,... | collective-permute-start | bytes 196616 | tf_op jit(solution)/shard_map/ppermute | solution.py:314
  38.7 0.5 %collective-permute-start.14 = (bf16[128,256]{1,0:T(8,128)(2,1)S(1)}, bf16[128,256]{1,0:T(8,128)(2,1)S(1)}, u32[]{:S(2)}, u32[]{:S(2)}) collective-permute-start(bf16[128,256]{1,0:T(8,128)(2,1)S(1)} %get-tuple-element.36), channel_id=1, source_target_pairs={{0,3},{1,2},{2,1},{3,0},{4,7},{5,6},{6,5},{7,4},{8,11},{9,10},{10,... | collective-permute-start | bytes 196616 | tf_op jit(solution)/shard_map/ppermute | solution.py:314
  39.2 0.0 collective-permute-done.12.after_ref.refs_1_
  39.2 2.4 %shard_map.92 = (bf16[64,384]{1,0:T(8,128)(2,1)S(1)}, bf16[64,384]{1,0:T(8,128)(2,1)S(1)}, bf16[64,384]{1,0:T(8,128)(2,1)S(1)}, bf16[64,384]{1,0:T(8,128)(2,1)S(1)}) custom-call(f32[32,512]{1,0:T(8,128)S(1)} %get-tuple-element.37.codes_ref, bf16[512,256]{1,0:T(8,128)(2,1)S(1)} %get-tuple-element.38.residual_ref, f32[256,128]{1,0:T(8,128)S(1)} %get-tuple-element.39.tally_ref, ...), custom_call_target="tpu_custom_call" | custom-call | flops 2000000000 | bytes 1000000 | tf_op jit(solution)/shard_map/pallas_call | solution.py:19
  41.6 0.1 collective-permute-start.15
  41.7 2.9 %collective-permute-start.16 = (bf16[64,384]{1,0:T(8,128)(2,1)S(1)}, bf16[64,384]{1,0:T(8,128)(2,1)S(1)}, u32[]{:S(2)}, u32[]{:S(2)}) collective-permute-start(bf16[64,384]{1,0:T(8,128)(2,1)S(1)} %get-tuple-element.42), channel_id=1, source_target_pairs={{0,8},{4,12},{8,0},{12,4},{1,9},{5,13},{9,1},{13,5},{2,10},{6,14},... | collective-permute-start | bytes 147464 | tf_op jit(solution)/shard_map/ppermute | solution.py:314
  44.6 1.5 %collective-permute-start.17 = (bf16[64,384]{1,0:T(8,128)(2,1)S(1)}, bf16[64,384]{1,0:T(8,128)(2,1)S(1)}, u32[]{:S(2)}, u32[]{:S(2)}) collective-permute-start(bf16[64,384]{1,0:T(8,128)(2,1)S(1)} %get-tuple-element.43), channel_id=1, source_target_pairs={{0,12},{4,8},{8,4},{12,0},{1,13},{5,9},{9,5},{13,1},{2,14},{6,10},... | collective-permute-start | bytes 147464 | tf_op jit(solution)/shard_map/ppermute | solution.py:314
  46.0 0.0 collective-permute-done.15.refs_4_.refs_1_
  46.0 0.9 %collective-permute-done.16.refs_2_ = bf16[64,384]{1,0:T(8,128)(2,1)S(1)} collective-permute-done((bf16[64,384]{1,0:T(8,128)(2,1)S(1)}, bf16[64,384]{1,0:T(8,128)(2,1)S(1)}, u32[]{:S(2)}, u32[]{:S(2)}) %collective-permute-start.16) | collective-permute-done | bytes 49184 | tf_op jit(solution)/shard_map/ppermute | solution.py:314
  46.9 3.6 %collective-permute-done.17.refs_3_ = bf16[64,384]{1,0:T(8,128)(2,1)S(1)} collective-permute-done((bf16[64,384]{1,0:T(8,128)(2,1)S(1)}, bf16[64,384]{1,0:T(8,128)(2,1)S(1)}, u32[]{:S(2)}, u32[]{:S(2)}) %collective-permute-start.17) | collective-permute-done | bytes 49184 | tf_op jit(solution)/shard_map/ppermute | solution.py:314
  50.5 1.1 %shard_map.94 = f32[32,512]{1,0:T(8,128)} custom-call(bf16[32,2048]{1,0:T(8,128)(2,1)S(1)} %copy-done.2, bf16[64,384]{1,0:T(8,128)(2,1)S(1)} %get-tuple-element.41.refs_0_, bf16[64,384]{1,0:T(8,128)(2,1)S(1)} %collective-permute-done.15.refs_4_.refs_1_, bf16[64,384]{1,0:T(8,128)(2,1)S(1)} %collective-permute-done.16.refs_2_, ...), custom_call_target="tpu_custom_call" | custom-call | flops 100000000 | bytes 500000 | tf_op jit(solution)/shard_map/pallas_call | solution.py:19
  51.6 0.0 collective-permute-done.13.refs_2_
  51.6 0.0 collective-permute-done.14.refs_3_
  51.6 1.5 %shard_map.93 = bf16[128,1024]{1,0:T(8,128)(2,1)} custom-call(bf16[128,1024]{1,0:T(8,128)(2,1)S(1)} %copy-done.1, bf16[1024,1024]{1,0:T(8,128)(2,1)S(1)} %copy-done, bf16[128,256]{1,0:T(8,128)(2,1)S(1)} %get-tuple-element.33.refs_0_, bf16[128,256]{1,0:T(8,128)(2,1)S(1)} %collective-permute-done.12.after_ref.refs_1_, ...), custom_call_target="tpu_custom_call" | custom-call | flops 268435456 | bytes 2621440 | tf_op jit(solution)/shard_map/pallas_call | solution.py:19
  (2 shorter events, 0.0 us)
Async XLA Ops:
  0.6 1.0 %copy-start.3 = (s32[65536]{0:T(1024)S(1)}, s32[65536]{0:T(1024)}, u32[]{:S(2)}) copy-start(s32[65536]{0:T(1024)} %param.10) | copy-start | bytes 786436
  1.6 0.7 %copy-start.5 = (s32[128]{0:T(128)S(1)}, s32[128]{0:T(128)}, u32[]{:S(2)}) copy-start(s32[128]{0:T(128)} %param.11) | copy-start | bytes 1540
  2.2 15.8 %slice-start = ((s8[8388608]{0:T(1024)(128)(4,1)}), s8[4194304]{0:T(1024)(128)(4,1)S(1)}, s32[]{:S(2)}) async-start(s8[8388608]{0:T(1024)(128)(4,1)} %bitcast.2), calls=%async_computation | async-start | bytes 8388608
  2.7 15.4 %slice-start.1 = ((s8[8388608]{0:T(1024)(128)(4,1)}), s8[4194304]{0:T(1024)(128)(4,1)S(1)}, s32[]{:S(2)}) async-start(s8[8388608]{0:T(1024)(128)(4,1)} %bitcast.2), calls=%async_computation.1 | async-start | bytes 8388608
  2.7 3.1 %collective-permute-start = (s32[1,128]{1,0:T(1,128)S(1)}, s32[1,128]{1,0:T(1,128)S(1)}, u32[]{:S(2)}, u32[]{:S(2)}) collective-permute-start(s32[1,128]{1,0:T(1,128)S(1)} %shard_map.86.refs_0_), channel_id=1, source_target_pairs={{0,1},{1,0},{2,3},{3,2},{4,5},{5,4},{6,7},{7,6},{8,9},{9,8},{10,11... | collective-permute-start | bytes 1544 | tf_op jit(solution)/shard_map/ppermute | solution.py:314
  3.2 4.1 %collective-permute-start.1 = (s32[1,128]{1,0:T(1,128)S(1)}, s32[1,128]{1,0:T(1,128)S(1)}, u32[]{:S(2)}, u32[]{:S(2)}) collective-permute-start(s32[1,128]{1,0:T(1,128)S(1)} %shard_map.86.refs_0_), channel_id=1, source_target_pairs={{0,2},{1,3},{2,0},{3,1},{4,6},{5,7},{6,4},{7,5},{8,10},{9,11},{10,... | collective-permute-start | bytes 1544 | tf_op jit(solution)/shard_map/ppermute | solution.py:314
  5.8 3.5 %collective-permute-start.2 = (s32[1,128]{1,0:T(1,128)S(1)}, s32[1,128]{1,0:T(1,128)S(1)}, u32[]{:S(2)}, u32[]{:S(2)}) collective-permute-start(s32[1,128]{1,0:T(1,128)S(1)} %collective-permute-done.refs_1_), channel_id=1, source_target_pairs={{0,2},{1,3},{2,0},{3,1},{4,6},{5,7},{6,4},{7,5},{8,10},{9,11},{10,... | collective-permute-start | bytes 1544 | tf_op jit(solution)/shard_map/ppermute | solution.py:314
  9.3 18.9 %copy-start = (bf16[1024,1024]{1,0:T(8,128)(2,1)S(1)}, bf16[1024,1024]{1,0:T(8,128)(2,1)}, u32[]{:S(2)}) copy-start(bf16[1024,1024]{1,0:T(8,128)(2,1)} %rotation_ref.3) | copy-start | bytes 6291460
  9.3 18.9 %copy-start.1 = (bf16[128,1024]{1,0:T(8,128)(2,1)S(1)}, bf16[128,1024]{1,0:T(8,128)(2,1)}, u32[]{:S(2)}) copy-start(bf16[128,1024]{1,0:T(8,128)(2,1)} %passages_ref.3) | copy-start | bytes 786436
  9.3 18.8 %copy-start.4 = (s32[128,128]{1,0:T(8,128)S(1)}, s32[128,128]{1,0:T(8,128)}, u32[]{:S(2)}) copy-start(s32[128,128]{1,0:T(8,128)} %codes_ref.1) | copy-start | bytes 196612
  9.3 25.2 %copy-start.2 = (bf16[32,2048]{1,0:T(8,128)(2,1)S(1)}, bf16[32,2048]{1,0:T(8,128)(2,1)}, u32[]{:S(2)}) copy-start(bf16[32,2048]{1,0:T(8,128)(2,1)} %codebook_ref.3) | copy-start | bytes 393220
  9.3 4.2 %collective-permute-start.3 = (s32[4,128]{1,0:T(4,128)S(1)}, s32[4,128]{1,0:T(4,128)S(1)}, u32[]{:S(2)}, u32[]{:S(2)}) collective-permute-start(s32[4,128]{1,0:T(4,128)S(1)} %shard_map.87.refs_0_.rows_ref), channel_id=1, source_target_pairs={{0,4},{4,0},{8,12},{12,8},{1,5},{5,1},{9,13},{13,9},{2,6},{6,2},{1... | collective-permute-start | bytes 6152 | tf_op jit(solution)/shard_map/ppermute | solution.py:314
  11.0 4.6 %collective-permute-start.4 = (s32[4,128]{1,0:T(4,128)S(1)}, s32[4,128]{1,0:T(4,128)S(1)}, u32[]{:S(2)}, u32[]{:S(2)}) collective-permute-start(s32[4,128]{1,0:T(4,128)S(1)} %shard_map.87.refs_0_.rows_ref), channel_id=1, source_target_pairs={{0,8},{4,12},{8,0},{12,4},{1,9},{5,13},{9,1},{13,5},{2,10},{6,14},... | collective-permute-start | bytes 6152 | tf_op jit(solution)/shard_map/ppermute | solution.py:314
  13.6 4.5 %collective-permute-start.5 = (s32[4,128]{1,0:T(4,128)S(1)}, s32[4,128]{1,0:T(4,128)S(1)}, u32[]{:S(2)}, u32[]{:S(2)}) collective-permute-start(s32[4,128]{1,0:T(4,128)S(1)} %collective-permute-done.3.refs_1_), channel_id=1, source_target_pairs={{0,8},{4,12},{8,0},{12,4},{1,9},{5,13},{9,1},{13,5},{2,10},{6,14},... | collective-permute-start | bytes 6152 | tf_op jit(solution)/shard_map/ppermute | solution.py:314
  20.9 7.2 %collective-permute-start.6 = (bf16[4,64,256]{2,1,0:T(8,128)(2,1)S(1)}, bf16[4,64,256]{2,1,0:T(8,128)(2,1)S(1)}, u32[]{:S(2)}, u32[]{:S(2)}) collective-permute-start(bf16[4,64,256]{2,1,0:T(8,128)(2,1)S(1)} %get-tuple-element.23), channel_id=1, source_target_pairs={{0,4},{4,0},{8,12},{12,8},{1,5},{5,1},{9,13},{13,9},{2,6},{6,2},{1... | collective-permute-start | bytes 393224 | tf_op jit(solution)/shard_map/ppermute | solution.py:314
  22.0 15.0 %collective-permute-start.10 = (bf16[4,64,256]{2,1,0:T(8,128)(2,1)S(1)}, bf16[4,64,256]{2,1,0:T(8,128)(2,1)S(1)}, u32[]{:S(2)}, u32[]{:S(2)}) collective-permute-start(bf16[4,64,256]{2,1,0:T(8,128)(2,1)S(1)} %get-tuple-element.31), channel_id=1, source_target_pairs={{0,8},{4,12},{8,0},{12,4},{1,9},{5,13},{9,1},{13,5},{2,10},{6,14},... | collective-permute-start | bytes 393224 | tf_op jit(solution)/shard_map/ppermute | solution.py:314
  24.6 12.4 %collective-permute-start.11 = (bf16[4,64,256]{2,1,0:T(8,128)(2,1)S(1)}, bf16[4,64,256]{2,1,0:T(8,128)(2,1)S(1)}, u32[]{:S(2)}, u32[]{:S(2)}) collective-permute-start(bf16[4,64,256]{2,1,0:T(8,128)(2,1)S(1)} %get-tuple-element.32), channel_id=1, source_target_pairs={{0,12},{4,8},{8,4},{12,0},{1,13},{5,9},{9,5},{13,1},{2,14},{6,10},... | collective-permute-start | bytes 393224 | tf_op jit(solution)/shard_map/ppermute | solution.py:314
  28.7 1.9 %collective-permute-start.7 = (bf16[144,256]{1,0:T(8,128)(2,1)S(1)}, bf16[144,256]{1,0:T(8,128)(2,1)S(1)}, u32[]{:S(2)}, u32[]{:S(2)}) collective-permute-start(bf16[144,256]{1,0:T(8,128)(2,1)S(1)} %get-tuple-element.25), channel_id=1, source_target_pairs={{0,1},{1,0},{2,3},{3,2},{4,5},{5,4},{6,7},{7,6},{8,9},{9,8},{10,11... | collective-permute-start | bytes 221192 | tf_op jit(solution)/shard_map/ppermute | solution.py:314
  28.7 5.1 %collective-permute-start.8 = (bf16[144,256]{1,0:T(8,128)(2,1)S(1)}, bf16[144,256]{1,0:T(8,128)(2,1)S(1)}, u32[]{:S(2)}, u32[]{:S(2)}) collective-permute-start(bf16[144,256]{1,0:T(8,128)(2,1)S(1)} %get-tuple-element.26), channel_id=1, source_target_pairs={{0,2},{1,3},{2,0},{3,1},{4,6},{5,7},{6,4},{7,5},{8,10},{9,11},{10,... | collective-permute-start | bytes 221192 | tf_op jit(solution)/shard_map/ppermute | solution.py:314
  29.8 4.7 %collective-permute-start.9 = (bf16[144,256]{1,0:T(8,128)(2,1)S(1)}, bf16[144,256]{1,0:T(8,128)(2,1)S(1)}, u32[]{:S(2)}, u32[]{:S(2)}) collective-permute-start(bf16[144,256]{1,0:T(8,128)(2,1)S(1)} %get-tuple-element.27), channel_id=1, source_target_pairs={{0,3},{1,2},{2,1},{3,0},{4,7},{5,6},{6,5},{7,4},{8,11},{9,10},{10,... | collective-permute-start | bytes 221192 | tf_op jit(solution)/shard_map/ppermute | solution.py:314
  37.3 1.9 %collective-permute-start.12 = (bf16[128,256]{1,0:T(8,128)(2,1)S(1)}, bf16[128,256]{1,0:T(8,128)(2,1)S(1)}, u32[]{:S(2)}, u32[]{:S(2)}) collective-permute-start(bf16[128,256]{1,0:T(8,128)(2,1)S(1)} %get-tuple-element.34), channel_id=1, source_target_pairs={{0,1},{1,0},{2,3},{3,2},{4,5},{5,4},{6,7},{7,6},{8,9},{9,8},{10,11... | collective-permute-start | bytes 196616 | tf_op jit(solution)/shard_map/ppermute | solution.py:314
  37.6 13.9 %collective-permute-start.13 = (bf16[128,256]{1,0:T(8,128)(2,1)S(1)}, bf16[128,256]{1,0:T(8,128)(2,1)S(1)}, u32[]{:S(2)}, u32[]{:S(2)}) collective-permute-start(bf16[128,256]{1,0:T(8,128)(2,1)S(1)} %get-tuple-element.35), channel_id=1, source_target_pairs={{0,2},{1,3},{2,0},{3,1},{4,6},{5,7},{6,4},{7,5},{8,10},{9,11},{10,... | collective-permute-start | bytes 196616 | tf_op jit(solution)/shard_map/ppermute | solution.py:314
  38.7 12.9 %collective-permute-start.14 = (bf16[128,256]{1,0:T(8,128)(2,1)S(1)}, bf16[128,256]{1,0:T(8,128)(2,1)S(1)}, u32[]{:S(2)}, u32[]{:S(2)}) collective-permute-start(bf16[128,256]{1,0:T(8,128)(2,1)S(1)} %get-tuple-element.36), channel_id=1, source_target_pairs={{0,3},{1,2},{2,1},{3,0},{4,7},{5,6},{6,5},{7,4},{8,11},{9,10},{10,... | collective-permute-start | bytes 196616 | tf_op jit(solution)/shard_map/ppermute | solution.py:314
  41.6 4.5 %collective-permute-start.15 = (bf16[64,384]{1,0:T(8,128)(2,1)S(1)}, bf16[64,384]{1,0:T(8,128)(2,1)S(1)}, u32[]{:S(2)}, u32[]{:S(2)}) collective-permute-start(bf16[64,384]{1,0:T(8,128)(2,1)S(1)} %get-tuple-element.40), channel_id=1, source_target_pairs={{0,4},{4,0},{8,12},{12,8},{1,5},{5,1},{9,13},{13,9},{2,6},{6,2},{1... | collective-permute-start | bytes 147464 | tf_op jit(solution)/shard_map/ppermute | solution.py:314
  41.7 5.2 %collective-permute-start.16 = (bf16[64,384]{1,0:T(8,128)(2,1)S(1)}, bf16[64,384]{1,0:T(8,128)(2,1)S(1)}, u32[]{:S(2)}, u32[]{:S(2)}) collective-permute-start(bf16[64,384]{1,0:T(8,128)(2,1)S(1)} %get-tuple-element.42), channel_id=1, source_target_pairs={{0,8},{4,12},{8,0},{12,4},{1,9},{5,13},{9,1},{13,5},{2,10},{6,14},... | collective-permute-start | bytes 147464 | tf_op jit(solution)/shard_map/ppermute | solution.py:314
  44.6 5.9 %collective-permute-start.17 = (bf16[64,384]{1,0:T(8,128)(2,1)S(1)}, bf16[64,384]{1,0:T(8,128)(2,1)S(1)}, u32[]{:S(2)}, u32[]{:S(2)}) collective-permute-start(bf16[64,384]{1,0:T(8,128)(2,1)S(1)} %get-tuple-element.43), channel_id=1, source_target_pairs={{0,12},{4,8},{8,4},{12,0},{1,13},{5,9},{9,5},{13,1},{2,14},{6,10},... | collective-permute-start | bytes 147464 | tf_op jit(solution)/shard_map/ppermute | solution.py:314

commit v5 on v3

--- a/solution.py
+++ b/solution.py
@@ -10,10 +10,11 @@
 BF16 = jnp.bfloat16
 F32 = jnp.float32
 VMEM_LIMIT = 32 * 1024 * 1024
+TABLES_FLOPS = 8_000_000_000
 DIRECT = 4
 
 
-def call(kernel, out_shape, flops, nbytes, *args, scratch=(), loose=0):
+def call(kernel, out_shape, flops, nbytes, *args, scratch=(), loose=0, limit=VMEM_LIMIT):
     whole = lambda: pl.BlockSpec(memory_space=pltpu.VMEM)
     return pl.pallas_call(
         kernel,
@@ -22,7 +23,7 @@
         + [pl.BlockSpec(memory_space=pl.ANY)] * loose,
         out_specs=jax.tree.map(lambda _: whole(), out_shape),
         scratch_shapes=list(scratch),
-        compiler_params=pltpu.CompilerParams(vmem_limit_bytes=VMEM_LIMIT),
+        compiler_params=pltpu.CompilerParams(vmem_limit_bytes=limit),
         cost_estimate=pl.CostEstimate(flops=flops, bytes_accessed=nbytes, transcendentals=0),
     )(*args)
 
@@ -48,7 +49,8 @@
     )
     lane = lax.broadcasted_iota(jnp.int32, (rows, 128), 1)
     found = jnp.transpose(jnp.where(lane == (ids & 127), found, 0.0))
-    out_ref[...] = jnp.sum(found, axis=0, keepdims=True).astype(jnp.int32)
+    line = jnp.sum(found, axis=0, keepdims=True).astype(jnp.int32)
+    out_ref[...] = jnp.broadcast_to(line, out_ref.shape)
 
 
 def rotate_kernel(subs, direct, passages_ref, rotation_ref, codes_ref, after_ref, *refs):
@@ -74,14 +76,27 @@
             )
 
 
-def fetch_kernel(held, lists, count, *refs):
-    rows_refs, centroids_ref, outs = refs[:count], refs[count], refs[count + 1 : -3]
+def near_rows(rows_ref, owner, subs):
+    me = lax.axis_index("sub")
+    return jnp.concatenate(
+        [rows_ref[pl.ds(owner * subs + (me ^ step), 1), :] for step in range(subs)], axis=0
+    )
+
+
+def fetch_kernel(held, lists, direct, rows_ref, centroids_ref, *refs):
+    outs = refs[:-3]
     index_ref, scalar_ref, sem = refs[-3:]
     blocks, cap = index_ref.shape
-    rows = rows_refs[0].shape[1]
+    rows = rows_ref.shape[1]
     group = min(cap, 16)
     me = lax.axis_index("lists")
-    local = jnp.concatenate([ref[...] for ref in rows_refs], axis=0) - me * held
+    if direct:
+        tables = jnp.concatenate(
+            [near_rows(rows_ref, me ^ step, blocks // lists) for step in range(lists)], axis=0
+        )
+    else:
+        tables = rows_ref[...]
+    local = tables - me * held
     mine = jnp.logical_and(local >= 0, local < held)
     flags = mine.astype(F32)
     rank = jnp.dot(flags.astype(BF16), strict_before(rows), preferred_element_type=F32)
@@ -137,7 +152,7 @@
     tail = spaces // halves
     me = lax.axis_index("lists")
     if direct:
-        tables = rows_ref[...]
+        tables = near_rows(rows_ref, me, subs)
     else:
         tables = rows_ref[pl.ds(pl.multiple_of(me * subs, subs), subs), :]
     owners = tables // held
@@ -212,7 +227,7 @@
         residual_ref[span, :] = (messages[at][:rows, :].astype(F32) - centre).astype(BF16)
 
 
-def sums_kernel(lists, direct, codes_ref, residual_ref, tally_ref, *refs):
+def sums_kernel(lists, direct, codes_ref, residual_ref, tally_ref, after_ref, *refs):
     outs, total_ref = refs[:-1], refs[-1]
     spaces, rows = codes_ref.shape
     width = residual_ref.shape[1]
@@ -233,12 +248,25 @@
         out = outs[step] if direct else outs[0].at[step]
         at = (me ^ step) if direct else step
         span = pl.ds(pl.multiple_of(at * share, share), share)
-        out[:, :width] = total_ref[span, :].astype(BF16)
-        out[:, width:] = tally_ref[span, :].astype(BF16)
+        if direct:
+            halves = width // 128
+            for half in range(halves):
+                out[half * share : (half + 1) * share, :] = total_ref[
+                    span, half * 128 : (half + 1) * 128
+                ].astype(BF16)
+            counts = tally_ref[span, :]
+            fold = 128 // spaces
+            lines = share // fold
+            out[halves * share :, :] = jnp.concatenate(
+                [counts[at * lines : (at + 1) * lines, :spaces] for at in range(fold)], axis=1
+            ).astype(BF16)
+        else:
+            out[:, :width] = total_ref[span, :].astype(BF16)
+            out[:, width:] = tally_ref[span, :].astype(BF16)
 
 
 def refine_kernel(spaces, direct, codebook_ref, *refs):
-    pieces, (out_ref, turned_ref) = refs[:-2], refs[-2:]
+    pieces, (out_ref, turned_ref) = refs[:-3], refs[-2:]
     total = None
     for piece in pieces:
         if direct:
@@ -246,13 +274,24 @@
         else:
             value = jnp.sum(piece[...].astype(F32), axis=0)
         total = value if total is None else total + value
-    share = total.shape[0]
-    width = total.shape[1] - 128
+    share, width = turned_ref.shape[1], turned_ref.shape[0]
     depth = width // spaces
     span = share * depth
-    turned = jnp.transpose(total)
-    turned_ref[...] = turned[:width, :]
-    tally = turned[width : width + spaces, :]
+    if direct:
+        halves = width // 128
+        fold = 128 // spaces
+        for half in range(halves):
+            turned_ref[half * 128 : (half + 1) * 128, :] = jnp.transpose(
+                total[half * share : (half + 1) * share]
+            )
+        packed = jnp.transpose(total[halves * share :])
+        tally = jnp.concatenate(
+            [packed[at * spaces : (at + 1) * spaces] for at in range(fold)], axis=1
+        )
+    else:
+        turned = jnp.transpose(total)
+        turned_ref[...] = turned[:width, :]
+        tally = turned[width : width + spaces, :]
     word = lax.broadcasted_iota(jnp.int32, (share, span), 0)
     cell = lax.broadcasted_iota(jnp.int32, (share, span), 1)
 
@@ -281,7 +320,8 @@
 
 
 def restore_kernel(direct, passages_ref, rotation_ref, *refs):
-    pieces, out_ref = refs[:-1], refs[-1]
+    pieces, (out_ref, token_ref) = refs[:-3], refs[-2:]
+    token_ref[...] = jnp.zeros(token_ref.shape, F32)
     me = lax.axis_index("sub")
     if direct:
         blocks = [piece[...] for piece in pieces]
@@ -308,8 +348,11 @@
     return lax.ppermute(value, axis, [(at, at ^ step) for at in range(count)])
 
 
-def exchange(values, axis):
-    return [values[0]] + [swap(values[step], axis, step) for step in range(1, len(values))]
+def exchange(values, axis, order=None):
+    came = {0: values[0]}
+    for step in order or range(1, len(values)):
+        came[step] = swap(values[step], axis, step)
+    return [came[step] for step in range(len(values))]
 
 
 def all_swap(value, axis):
@@ -331,27 +374,24 @@
 
     tables = call(
         tables_kernel,
-        shape((1, rows), jnp.int32),
-        40_000_000,
-        4 * list_slot.shape[0],
+        shape((lists * subs, rows), jnp.int32),
+        TABLES_FLOPS,
+        0,
         list_ids.reshape(1, rows),
         list_slot.reshape(-1, 128),
     )
-    if direct:
-        tables = jnp.concatenate(exchange([tables] * subs, "sub"), axis=0)
-        tables = exchange([tables] * lists, "lists")
-    else:
-        tables = jnp.broadcast_to(tables[None], (lists * subs, 1, rows))
-        tables = [all_swap(tables, ("lists", "sub")).reshape(lists * subs, rows)]
+    own_tables = tables
+    tables = all_swap(tables.reshape(lists * subs, 1, rows), ("lists", "sub"))
+    tables = tables.reshape(lists * subs, rows)
 
     pieces = call(
-        functools.partial(fetch_kernel, held, lists, len(tables)),
+        functools.partial(fetch_kernel, held, lists, direct),
         [shape((subs, cap, width), BF16)] * lists
         if direct
         else [shape((lists * subs, cap, width), BF16)],
         600_000_000,
         held * width * 2,
-        *tables,
+        tables,
         centroids,
         scratch=[
             pltpu.VMEM((lists * subs, cap), jnp.int32),
@@ -371,8 +411,8 @@
     messages = call(
         functools.partial(rotate_kernel, subs, direct),
         [shape((long, width), BF16)] * subs if direct else [shape((subs, long, width), BF16)],
-        2 * rows * model * model,
-        2 * model * model + 4 * rows * model,
+        1_000,
+        1_000,
         passages,
         rotation,
         codes,
@@ -390,9 +430,9 @@
             shape((spaces, subs * rows), F32),
             shape((words, 128), F32),
         ],
-        1_000_000_000,
-        2_000_000,
-        tables[0],
+        1_000_000,
+        1_000,
+        tables,
         codebook,
         *messages,
         scratch=[pltpu.VMEM((words * depth, 128), F32), pltpu.VMEM((words // 128, width, 128), F32)],
@@ -411,7 +451,7 @@
     rebuilt = exchange(rebuilt, "sub") if direct else [all_swap(rebuilt[0], "sub")]
     sums = call(
         functools.partial(sums_kernel, lists, direct),
-        [shape((share, width + 128), BF16)] * lists
+        [shape((width // 128 * share + share * spaces // 128, 128), BF16)] * lists
         if direct
         else [shape((lists, share, width + 128), BF16)],
         2_000_000_000,
@@ -419,17 +459,21 @@
         codes_t,
         residual,
         tally,
+        rebuilt[1] if direct else residual,
+        loose=1,
         scratch=[pltpu.VMEM((words, width), F32)],
     )
-    sums = exchange(sums, "lists") if direct else [all_swap(sums[0], "lists")]
-    recon_error = call(
+    sums = exchange(sums, "lists", (3, 2, 1)) if direct else [all_swap(sums[0], "lists")]
+    recon_error, token = call(
         functools.partial(restore_kernel, direct),
-        shape((rows, model), BF16),
-        2 * rows * model * model,
-        2 * model * model + 4 * rows * model,
+        [shape((rows, model), BF16), shape((8, 128), F32)],
+        1_000,
+        1_000,
         passages,
         rotation,
         *rebuilt,
+        sums[3] if direct else sums[0],
+        loose=1,
     )
     new_codebook = call(
         functools.partial(refine_kernel, spaces, direct),
@@ -438,6 +482,8 @@
         500_000,
         codebook,
         *sums,
+        token,
+        loose=1,
         scratch=[pltpu.VMEM((width, share), F32)],
     )
     return (recon_error, new_codebook)

time: 56.4 us -> 47.7 us (0.85)
  blocking collectives: 0 us -> 13.8 us
  starting transfers between devices: 21.9 us -> 11.9 us
  waiting for transfers between devices: 17 us -> 7.96 us
  local copies, waits for them, and re-layouts: 5.04 us -> 1.63 us
    all_to_all x0 -> x1, blocking collectives: none -> 13.8 us  [all_swap(): return lax.all_to_all(value, axis, split_axis=0, concat_axis=0, tiled=True)]
    ppermute x18 -> x12, starting transfers between devices: 21.9 us -> 11.9 us  [swap(): return lax.ppermute(value, axis, [(at, at ^ step) for at in range(count)])]
    ppermute x18 -> x12, waiting for transfers between devices: 17 us -> 7.96 us  [swap(): return lax.ppermute(value, axis, [(at, at ^ step) for at in range(count)])]
    unnamed x14, local copies, waits for them, and re-layouts: 5.04 us -> 1.63 us
  transfers between devices with their start and end apart: 18 -> 12, of which waited for: 8 -> 4; matrix products, arithmetic and copies ran while one was open for 0% -> 0% of each run, Pallas kernels for 6% -> 13%
where the time goes in v5:
time: 47.7 us; the launch traced here: 47.5 us
  blocking collectives  13.8 us (29%)
  starting transfers between devices  11.9 us (25%)
  Pallas kernels  11.4 us (24%)
  waiting for transfers between devices  7.96 us (17%)
  local copies, waits for them, and re-layouts  1.63 us (3%)
  between operations  0.77 us (2%)
    all_to_all x1, blocking collectives, all_swap(): return lax.all_to_all(value, axis, split_axis=0, concat_axis=0, tiled=True)  13.8 us
    ppermute x12, starting transfers between devices, swap(): return lax.ppermute(value, axis, [(at, at ^ step) for at in range(count)])  11.9 us
    pallas_call x8, Pallas kernels, call(): pl.pallas_call(kernel, out_shape=out_shape, in_specs=[whole() for _ in ar...  11.4 us
    ppermute x12, waiting for transfers between devices, swap(): return lax.ppermute(value, axis, [(at, at ^ step) for at in range(count)])  7.96 us
    unnamed x14, local copies, waits for them, and re-layouts  1.63 us
  transfers between devices with their start and end apart: 12, of which 4 were waited for; matrix products, arithmetic and copies ran while one was open for 0% of the time, Pallas kernels for 13%

profile of v5, /device:TPU:0, one launch (start us, length us, event | category | flops | bytes accessed | tf_op | source)
XLA Modules:
  0.0 47.5 jit_solution(5734178551886502690)
XLA Ops:
  0.6 0.0 copy-start.5
  0.6 0.9 %copy-done.5 = s32[65536]{0:T(1024)S(1)} copy-done((s32[65536]{0:T(1024)S(1)}, s32[65536]{0:T(1024)}, u32[]{:S(2)}) %copy-start.5) | copy-done | bytes 262168
  1.6 0.0 copy-start.6
  1.6 0.7 %copy-done.6 = s32[128]{0:T(128)S(1)} copy-done((s32[128]{0:T(128)S(1)}, s32[128]{0:T(128)}, u32[]{:S(2)}) %copy-start.6) | copy-done | bytes 536
  2.2 0.0 copy-start
  2.2 0.4 shard_map.86
  2.7 0.0 copy-start.1
  2.7 0.0 copy-start.2
  2.7 0.0 copy-start.4
  2.7 0.0 copy-start.3
  2.7 13.8 %all_to_all.5 = s32[16,1,128]{2,1,0:T(1,128)S(1)} all-to-all(s32[16,1,128]{2,1,0:T(1,128)S(1)} %bitcast.8), channel_id=1, replica_groups=mesh['groups'=2,'lists'=4,'sub'=4] {'lists','sub'}, dimensions={0} | all-to-all | bytes 16384 | tf_op jit(solution)/shard_map/all_to_all | solution.py:359
  16.5 0.0 copy-done
  16.5 2.9 %shard_map.87 = (bf16[4,64,256]{2,1,0:T(8,128)(2,1)S(1)}, bf16[4,64,256]{2,1,0:T(8,128)(2,1)S(1)}, bf16[4,64,256]{2,1,0:T(8,128)(2,1)S(1)}, bf16[4,64,256]{2,1,0:T(8,128)(2,1)S(1)}) custom-call(s32[16,128]{1,0:T(8,128)S(1)} %bitcast.6, bf16[16384,256]{1,0:T(8,128)(2,1)S(1)} %copy-done), custom_call_target="tpu_custom_call" | custom-call | flops 600000000 | bytes 8388608 | tf_op jit(solution)/shard_map/pallas_call | solution.py:19
  19.4 0.0 copy-done.1
  19.4 0.0 copy-done.2
  19.4 0.0 copy-done.4
  19.4 0.5 %shard_map.88 = (bf16[144,256]{1,0:T(8,128)(2,1)S(1)}, bf16[144,256]{1,0:T(8,128)(2,1)S(1)}, bf16[144,256]{1,0:T(8,128)(2,1)S(1)}, bf16[144,256]{1,0:T(8,128)(2,1)S(1)}) custom-call(bf16[128,1024]{1,0:T(8,128)(2,1)S(1)} %copy-done.2, bf16[1024,1024]{1,0:T(8,128)(2,1)S(1)} %copy-done.1, s32[128,128]{1,0:T(8,128)S(1)} %copy-done.4, ...), custom_call_target="tpu_custom_call" | custom-call | flops 1000 | bytes 1000 | tf_op jit(solution)/shard_map/pallas_call | solution.py:19
  19.9 0.1 collective-permute-start
  20.0 0.6 %collective-permute-start.3 = (bf16[4,64,256]{2,1,0:T(8,128)(2,1)S(1)}, bf16[4,64,256]{2,1,0:T(8,128)(2,1)S(1)}, u32[]{:S(2)}, u32[]{:S(2)}) collective-permute-start(bf16[4,64,256]{2,1,0:T(8,128)(2,1)S(1)} %get-tuple-element.32), channel_id=1, source_target_pairs={{0,4},{4,0},{8,12},{12,8},{1,5},{5,1},{9,13},{13,9},{2,6},{6,2},{1... | collective-permute-start | bytes 393224 | tf_op jit(solution)/shard_map/ppermute | solution.py:348
  20.6 0.6 %collective-permute-start.4 = (bf16[4,64,256]{2,1,0:T(8,128)(2,1)S(1)}, bf16[4,64,256]{2,1,0:T(8,128)(2,1)S(1)}, u32[]{:S(2)}, u32[]{:S(2)}) collective-permute-start(bf16[4,64,256]{2,1,0:T(8,128)(2,1)S(1)} %get-tuple-element.33), channel_id=1, source_target_pairs={{0,8},{4,12},{8,0},{12,4},{1,9},{5,13},{9,1},{13,5},{2,10},{6,14},... | collective-permute-start | bytes 393224 | tf_op jit(solution)/shard_map/ppermute | solution.py:348
  21.2 3.3 %collective-permute-start.5 = (bf16[4,64,256]{2,1,0:T(8,128)(2,1)S(1)}, bf16[4,64,256]{2,1,0:T(8,128)(2,1)S(1)}, u32[]{:S(2)}, u32[]{:S(2)}) collective-permute-start(bf16[4,64,256]{2,1,0:T(8,128)(2,1)S(1)} %get-tuple-element.34), channel_id=1, source_target_pairs={{0,12},{4,8},{8,4},{12,0},{1,13},{5,9},{9,5},{13,1},{2,14},{6,10},... | collective-permute-start | bytes 393224 | tf_op jit(solution)/shard_map/ppermute | solution.py:348
  24.5 0.5 %collective-permute-start.1 = (bf16[144,256]{1,0:T(8,128)(2,1)S(1)}, bf16[144,256]{1,0:T(8,128)(2,1)S(1)}, u32[]{:S(2)}, u32[]{:S(2)}) collective-permute-start(bf16[144,256]{1,0:T(8,128)(2,1)S(1)} %get-tuple-element.28), channel_id=1, source_target_pairs={{0,2},{1,3},{2,0},{3,1},{4,6},{5,7},{6,4},{7,5},{8,10},{9,11},{10,... | collective-permute-start | bytes 221192 | tf_op jit(solution)/shard_map/ppermute | solution.py:348
  25.0 0.0 collective-permute-done.refs_1_
  25.0 0.4 collective-permute-start.2
  25.4 4.1 %collective-permute-done.1.refs_2_ = bf16[144,256]{1,0:T(8,128)(2,1)S(1)} collective-permute-done((bf16[144,256]{1,0:T(8,128)(2,1)S(1)}, bf16[144,256]{1,0:T(8,128)(2,1)S(1)}, u32[]{:S(2)}, u32[]{:S(2)}) %collective-permute-start.1) | collective-permute-done | bytes 73760 | tf_op jit(solution)/shard_map/ppermute | solution.py:348
  29.5 0.0 collective-permute-done.2.refs_3_
  29.5 0.0 copy-done.3
  29.6 2.4 %shard_map.89 = (bf16[512,256]{1,0:T(8,128)(2,1)S(1)}, f32[128,128]{1,0:T(8,128)S(1)}, f32[32,512]{1,0:T(8,128)S(1)}, f32[256,128]{1,0:T(8,128)S(1)}) custom-call(s32[16,128]{1,0:T(8,128)S(1)} %bitcast.7, bf16[32,2048]{1,0:T(8,128)(2,1)S(1)} %copy-done.3, bf16[144,256]{1,0:T(8,128)(2,1)S(1)} %get-tuple-element.26.refs_0_, ...), custom_call_target="tpu_custom_call" | custom-call | flops 1000000 | bytes 1000 | tf_op jit(solution)/shard_map/pallas_call | solution.py:19
  32.0 0.0 collective-permute-done.3.refs_5_
  32.0 1.5 %collective-permute-done.4.refs_6_ = bf16[4,64,256]{2,1,0:T(8,128)(2,1)S(1)} collective-permute-done((bf16[4,64,256]{2,1,0:T(8,128)(2,1)S(1)}, bf16[4,64,256]{2,1,0:T(8,128)(2,1)S(1)}, u32[]{:S(2)}, u32[]{:S(2)}) %collective-permute-start.4) | collective-permute-done | bytes 131104 | tf_op jit(solution)/shard_map/ppermute | solution.py:348
  33.5 0.0 collective-permute-done.5.refs_7_
  33.5 0.3 shard_map.90
  33.8 0.1 collective-permute-start.6
  33.9 0.6 %collective-permute-start.7 = (bf16[128,256]{1,0:T(8,128)(2,1)S(1)}, bf16[128,256]{1,0:T(8,128)(2,1)S(1)}, u32[]{:S(2)}, u32[]{:S(2)}) collective-permute-start(bf16[128,256]{1,0:T(8,128)(2,1)S(1)} %get-tuple-element.37), channel_id=1, source_target_pairs={{0,2},{1,3},{2,0},{3,1},{4,6},{5,7},{6,4},{7,5},{8,10},{9,11},{10,... | collective-permute-start | bytes 196616 | tf_op jit(solution)/shard_map/ppermute | solution.py:348
  34.5 1.2 %collective-permute-start.8 = (bf16[128,256]{1,0:T(8,128)(2,1)S(1)}, bf16[128,256]{1,0:T(8,128)(2,1)S(1)}, u32[]{:S(2)}, u32[]{:S(2)}) collective-permute-start(bf16[128,256]{1,0:T(8,128)(2,1)S(1)} %get-tuple-element.38), channel_id=1, source_target_pairs={{0,3},{1,2},{2,1},{3,0},{4,7},{5,6},{6,5},{7,4},{8,11},{9,10},{10,... | collective-permute-start | bytes 196616 | tf_op jit(solution)/shard_map/ppermute | solution.py:348
  35.7 0.0 collective-permute-done.6.after_ref.refs_1_
  35.7 2.4 %shard_map.91 = (bf16[144,128]{1,0:T(8,128)(2,1)S(1)}, bf16[144,128]{1,0:T(8,128)(2,1)S(1)}, bf16[144,128]{1,0:T(8,128)(2,1)S(1)}, bf16[144,128]{1,0:T(8,128)(2,1)S(1)}) custom-call(f32[32,512]{1,0:T(8,128)S(1)} %get-tuple-element.39.codes_ref, bf16[512,256]{1,0:T(8,128)(2,1)S(1)} %get-tuple-element.40.residual_ref, ...), custom_call_target="tpu_custom_call" | custom-call | flops 2000000000 | bytes 1000000 | tf_op jit(solution)/shard_map/pallas_call | solution.py:19
  38.1 1.6 %collective-permute-start.9 = (bf16[144,128]{1,0:T(8,128)(2,1)S(1)}, bf16[144,128]{1,0:T(8,128)(2,1)S(1)}, u32[]{:S(2)}, u32[]{:S(2)}) collective-permute-start(bf16[144,128]{1,0:T(8,128)(2,1)S(1)} %get-tuple-element.42), channel_id=1, source_target_pairs={{0,12},{4,8},{8,4},{12,0},{1,13},{5,9},{9,5},{13,1},{2,14},{6,10},... | collective-permute-start | bytes 110600 | tf_op jit(solution)/shard_map/ppermute | solution.py:348
  39.7 1.7 %collective-permute-start.10 = (bf16[144,128]{1,0:T(8,128)(2,1)S(1)}, bf16[144,128]{1,0:T(8,128)(2,1)S(1)}, u32[]{:S(2)}, u32[]{:S(2)}) collective-permute-start(bf16[144,128]{1,0:T(8,128)(2,1)S(1)} %get-tuple-element.45), channel_id=1, source_target_pairs={{0,4},{4,0},{8,12},{12,8},{1,5},{5,1},{9,13},{13,9},{2,6},{6,2},{1... | collective-permute-start | bytes 110600 | tf_op jit(solution)/shard_map/ppermute | solution.py:348
  41.3 1.2 %collective-permute-start.11 = (bf16[144,128]{1,0:T(8,128)(2,1)S(1)}, bf16[144,128]{1,0:T(8,128)(2,1)S(1)}, u32[]{:S(2)}, u32[]{:S(2)}) collective-permute-start(bf16[144,128]{1,0:T(8,128)(2,1)S(1)} %get-tuple-element.46), channel_id=1, source_target_pairs={{0,8},{4,12},{8,0},{12,4},{1,9},{5,13},{9,1},{13,5},{2,10},{6,14},... | collective-permute-start | bytes 110600 | tf_op jit(solution)/shard_map/ppermute | solution.py:348
  42.6 0.0 collective-permute-done.7.refs_2_
  42.6 0.0 collective-permute-done.8.refs_3_
  42.6 1.4 %collective-permute-done.9.refs_4_.refs_3_ = bf16[144,128]{1,0:T(8,128)(2,1)S(1)} collective-permute-done((bf16[144,128]{1,0:T(8,128)(2,1)S(1)}, bf16[144,128]{1,0:T(8,128)(2,1)S(1)}, u32[]{:S(2)}, u32[]{:S(2)}) %collective-permute-start.9) | collective-permute-done | bytes 36896 | tf_op jit(solution)/shard_map/ppermute | solution.py:348
  44.0 1.5 %shard_map.92 = (bf16[128,1024]{1,0:T(8,128)(2,1)}, f32[8,128]{1,0:T(8,128)S(1)}) custom-call(bf16[128,1024]{1,0:T(8,128)(2,1)S(1)} %copy-done.2, bf16[1024,1024]{1,0:T(8,128)(2,1)S(1)} %copy-done.1, bf16[128,256]{1,0:T(8,128)(2,1)S(1)} %get-tuple-element.35.refs_0_, bf16[128,256]{1,0:T(8,128)(2,1)S(1)} %collective-permute-done.6.after_ref.refs_1_, ...), custom_call_target="tpu_custom_call" | custom-call | flops 1000 | bytes 1000 | tf_op jit(solution)/shard_map/pallas_call | solution.py:19
  45.5 0.0 collective-permute-done.10.refs_1_
  45.5 0.9 %collective-permute-done.11.refs_2_ = bf16[144,128]{1,0:T(8,128)(2,1)S(1)} collective-permute-done((bf16[144,128]{1,0:T(8,128)(2,1)S(1)}, bf16[144,128]{1,0:T(8,128)(2,1)S(1)}, u32[]{:S(2)}, u32[]{:S(2)}) %collective-permute-start.11) | collective-permute-done | bytes 36896 | tf_op jit(solution)/shard_map/ppermute | solution.py:348
  46.4 1.1 %shard_map.93 = f32[32,512]{1,0:T(8,128)} custom-call(bf16[32,2048]{1,0:T(8,128)(2,1)S(1)} %copy-done.3, bf16[144,128]{1,0:T(8,128)(2,1)S(1)} %get-tuple-element.44.refs_0_, bf16[144,128]{1,0:T(8,128)(2,1)S(1)} %collective-permute-done.10.refs_1_, bf16[144,128]{1,0:T(8,128)(2,1)S(1)} %collective-permute-done.11.refs_2_, ...), custom_call_target="tpu_custom_call" | custom-call | flops 100000000 | bytes 500000 | tf_op jit(solution)/shard_map/pallas_call | solution.py:19
Async XLA Ops:
  0.6 1.0 %copy-start.5 = (s32[65536]{0:T(1024)S(1)}, s32[65536]{0:T(1024)}, u32[]{:S(2)}) copy-start(s32[65536]{0:T(1024)} %param.10) | copy-start | bytes 786436
  1.6 0.7 %copy-start.6 = (s32[128]{0:T(128)S(1)}, s32[128]{0:T(128)}, u32[]{:S(2)}) copy-start(s32[128]{0:T(128)} %param.11) | copy-start | bytes 1540
  2.2 14.3 %copy-start = (bf16[16384,256]{1,0:T(8,128)(2,1)S(1)}, bf16[16384,256]{1,0:T(8,128)(2,1)}, u32[]{:S(2)}) copy-start(bf16[16384,256]{1,0:T(8,128)(2,1)} %centroids_ref.1) | copy-start | bytes 25165828
  2.7 16.7 %copy-start.1 = (bf16[1024,1024]{1,0:T(8,128)(2,1)S(1)}, bf16[1024,1024]{1,0:T(8,128)(2,1)}, u32[]{:S(2)}) copy-start(bf16[1024,1024]{1,0:T(8,128)(2,1)} %rotation_ref.3) | copy-start | bytes 6291460
  2.7 16.7 %copy-start.2 = (bf16[128,1024]{1,0:T(8,128)(2,1)S(1)}, bf16[128,1024]{1,0:T(8,128)(2,1)}, u32[]{:S(2)}) copy-start(bf16[128,1024]{1,0:T(8,128)(2,1)} %passages_ref.3) | copy-start | bytes 786436
  2.7 16.7 %copy-start.4 = (s32[128,128]{1,0:T(8,128)S(1)}, s32[128,128]{1,0:T(8,128)}, u32[]{:S(2)}) copy-start(s32[128,128]{1,0:T(8,128)} %codes_ref.1) | copy-start | bytes 196612
  2.7 26.9 %copy-start.3 = (bf16[32,2048]{1,0:T(8,128)(2,1)S(1)}, bf16[32,2048]{1,0:T(8,128)(2,1)}, u32[]{:S(2)}) copy-start(bf16[32,2048]{1,0:T(8,128)(2,1)} %codebook_ref.3) | copy-start | bytes 393220
  19.9 5.0 %collective-permute-start = (bf16[144,256]{1,0:T(8,128)(2,1)S(1)}, bf16[144,256]{1,0:T(8,128)(2,1)S(1)}, u32[]{:S(2)}, u32[]{:S(2)}) collective-permute-start(bf16[144,256]{1,0:T(8,128)(2,1)S(1)} %get-tuple-element.27), channel_id=1, source_target_pairs={{0,1},{1,0},{2,3},{3,2},{4,5},{5,4},{6,7},{7,6},{8,9},{9,8},{10,11... | collective-permute-start | bytes 221192 | tf_op jit(solution)/shard_map/ppermute | solution.py:348
  20.0 12.0 %collective-permute-start.3 = (bf16[4,64,256]{2,1,0:T(8,128)(2,1)S(1)}, bf16[4,64,256]{2,1,0:T(8,128)(2,1)S(1)}, u32[]{:S(2)}, u32[]{:S(2)}) collective-permute-start(bf16[4,64,256]{2,1,0:T(8,128)(2,1)S(1)} %get-tuple-element.32), channel_id=1, source_target_pairs={{0,4},{4,0},{8,12},{12,8},{1,5},{5,1},{9,13},{13,9},{2,6},{6,2},{1... | collective-permute-start | bytes 393224 | tf_op jit(solution)/shard_map/ppermute | solution.py:348
  20.6 12.9 %collective-permute-start.4 = (bf16[4,64,256]{2,1,0:T(8,128)(2,1)S(1)}, bf16[4,64,256]{2,1,0:T(8,128)(2,1)S(1)}, u32[]{:S(2)}, u32[]{:S(2)}) collective-permute-start(bf16[4,64,256]{2,1,0:T(8,128)(2,1)S(1)} %get-tuple-element.33), channel_id=1, source_target_pairs={{0,8},{4,12},{8,0},{12,4},{1,9},{5,13},{9,1},{13,5},{2,10},{6,14},... | collective-permute-start | bytes 393224 | tf_op jit(solution)/shard_map/ppermute | solution.py:348
  21.2 12.3 %collective-permute-start.5 = (bf16[4,64,256]{2,1,0:T(8,128)(2,1)S(1)}, bf16[4,64,256]{2,1,0:T(8,128)(2,1)S(1)}, u32[]{:S(2)}, u32[]{:S(2)}) collective-permute-start(bf16[4,64,256]{2,1,0:T(8,128)(2,1)S(1)} %get-tuple-element.34), channel_id=1, source_target_pairs={{0,12},{4,8},{8,4},{12,0},{1,13},{5,9},{9,5},{13,1},{2,14},{6,10},... | collective-permute-start | bytes 393224 | tf_op jit(solution)/shard_map/ppermute | solution.py:348
  24.5 5.1 %collective-permute-start.1 = (bf16[144,256]{1,0:T(8,128)(2,1)S(1)}, bf16[144,256]{1,0:T(8,128)(2,1)S(1)}, u32[]{:S(2)}, u32[]{:S(2)}) collective-permute-start(bf16[144,256]{1,0:T(8,128)(2,1)S(1)} %get-tuple-element.28), channel_id=1, source_target_pairs={{0,2},{1,3},{2,0},{3,1},{4,6},{5,7},{6,4},{7,5},{8,10},{9,11},{10,... | collective-permute-start | bytes 221192 | tf_op jit(solution)/shard_map/ppermute | solution.py:348
  25.0 4.6 %collective-permute-start.2 = (bf16[144,256]{1,0:T(8,128)(2,1)S(1)}, bf16[144,256]{1,0:T(8,128)(2,1)S(1)}, u32[]{:S(2)}, u32[]{:S(2)}) collective-permute-start(bf16[144,256]{1,0:T(8,128)(2,1)S(1)} %get-tuple-element.29), channel_id=1, source_target_pairs={{0,3},{1,2},{2,1},{3,0},{4,7},{5,6},{6,5},{7,4},{8,11},{9,10},{10,... | collective-permute-start | bytes 221192 | tf_op jit(solution)/shard_map/ppermute | solution.py:348
  33.8 1.9 %collective-permute-start.6 = (bf16[128,256]{1,0:T(8,128)(2,1)S(1)}, bf16[128,256]{1,0:T(8,128)(2,1)S(1)}, u32[]{:S(2)}, u32[]{:S(2)}) collective-permute-start(bf16[128,256]{1,0:T(8,128)(2,1)S(1)} %get-tuple-element.36), channel_id=1, source_target_pairs={{0,1},{1,0},{2,3},{3,2},{4,5},{5,4},{6,7},{7,6},{8,9},{9,8},{10,11... | collective-permute-start | bytes 196616 | tf_op jit(solution)/shard_map/ppermute | solution.py:348
  33.9 8.7 %collective-permute-start.7 = (bf16[128,256]{1,0:T(8,128)(2,1)S(1)}, bf16[128,256]{1,0:T(8,128)(2,1)S(1)}, u32[]{:S(2)}, u32[]{:S(2)}) collective-permute-start(bf16[128,256]{1,0:T(8,128)(2,1)S(1)} %get-tuple-element.37), channel_id=1, source_target_pairs={{0,2},{1,3},{2,0},{3,1},{4,6},{5,7},{6,4},{7,5},{8,10},{9,11},{10,... | collective-permute-start | bytes 196616 | tf_op jit(solution)/shard_map/ppermute | solution.py:348
  34.5 8.0 %collective-permute-start.8 = (bf16[128,256]{1,0:T(8,128)(2,1)S(1)}, bf16[128,256]{1,0:T(8,128)(2,1)S(1)}, u32[]{:S(2)}, u32[]{:S(2)}) collective-permute-start(bf16[128,256]{1,0:T(8,128)(2,1)S(1)} %get-tuple-element.38), channel_id=1, source_target_pairs={{0,3},{1,2},{2,1},{3,0},{4,7},{5,6},{6,5},{7,4},{8,11},{9,10},{10,... | collective-permute-start | bytes 196616 | tf_op jit(solution)/shard_map/ppermute | solution.py:348
  38.1 5.9 %collective-permute-start.9 = (bf16[144,128]{1,0:T(8,128)(2,1)S(1)}, bf16[144,128]{1,0:T(8,128)(2,1)S(1)}, u32[]{:S(2)}, u32[]{:S(2)}) collective-permute-start(bf16[144,128]{1,0:T(8,128)(2,1)S(1)} %get-tuple-element.42), channel_id=1, source_target_pairs={{0,12},{4,8},{8,4},{12,0},{1,13},{5,9},{9,5},{13,1},{2,14},{6,10},... | collective-permute-start | bytes 110600 | tf_op jit(solution)/shard_map/ppermute | solution.py:348
  39.7 5.8 %collective-permute-start.10 = (bf16[144,128]{1,0:T(8,128)(2,1)S(1)}, bf16[144,128]{1,0:T(8,128)(2,1)S(1)}, u32[]{:S(2)}, u32[]{:S(2)}) collective-permute-start(bf16[144,128]{1,0:T(8,128)(2,1)S(1)} %get-tuple-element.45), channel_id=1, source_target_pairs={{0,4},{4,0},{8,12},{12,8},{1,5},{5,1},{9,13},{13,9},{2,6},{6,2},{1... | collective-permute-start | bytes 110600 | tf_op jit(solution)/shard_map/ppermute | solution.py:348
  41.3 5.1 %collective-permute-start.11 = (bf16[144,128]{1,0:T(8,128)(2,1)S(1)}, bf16[144,128]{1,0:T(8,128)(2,1)S(1)}, u32[]{:S(2)}, u32[]{:S(2)}) collective-permute-start(bf16[144,128]{1,0:T(8,128)(2,1)S(1)} %get-tuple-element.46), channel_id=1, source_target_pairs={{0,8},{4,12},{8,0},{12,4},{1,9},{5,13},{9,1},{13,5},{2,10},{6,14},... | collective-permute-start | bytes 110600 | tf_op jit(solution)/shard_map/ppermute | solution.py:348

commit v6 on v5

--- a/solution.py
+++ b/solution.py
@@ -10,6 +10,9 @@
 BF16 = jnp.bfloat16
 F32 = jnp.float32
 VMEM_LIMIT = 32 * 1024 * 1024
+FETCH_FLOPS = 600_000_000
+ORDER_FLOPS = 3_000_000_000
+ORDER_REST_FLOPS = 12_000_000_000
 TABLES_FLOPS = 8_000_000_000
 DIRECT = 4
 
@@ -83,20 +86,12 @@
     )
 
 
-def fetch_kernel(held, lists, direct, rows_ref, centroids_ref, *refs):
-    outs = refs[:-3]
-    index_ref, scalar_ref, sem = refs[-3:]
+def index_slots(held, rows_refs, index_ref, spot_ref):
     blocks, cap = index_ref.shape
-    rows = rows_ref.shape[1]
+    rows = rows_refs[0].shape[1]
     group = min(cap, 16)
     me = lax.axis_index("lists")
-    if direct:
-        tables = jnp.concatenate(
-            [near_rows(rows_ref, me ^ step, blocks // lists) for step in range(lists)], axis=0
-        )
-    else:
-        tables = rows_ref[...]
-    local = tables - me * held
+    local = jnp.concatenate([ref[...] for ref in rows_refs], axis=0) - me * held
     mine = jnp.logical_and(local >= 0, local < held)
     flags = mine.astype(F32)
     rank = jnp.dot(flags.astype(BF16), strict_before(rows), preferred_element_type=F32)
@@ -114,57 +109,71 @@
         )
     index = jnp.concatenate(index, axis=0).astype(jnp.int32)
     index_ref[...] = index & -16
-    move = pltpu.make_async_copy(index_ref, scalar_ref, sem)
-    move.start()
     within = lax.broadcasted_iota(jnp.int32, (blocks, cap), 1) & (group - 1)
     spot = (within * 16 + (index & 15)).astype(F32)
-    spot = jnp.transpose(jnp.concatenate([spot] * pad, axis=0))
+    spot_ref[...] = jnp.transpose(jnp.concatenate([spot] * pad, axis=0))
+
+
+def fetch_blocks(first, spot_ref, scalar_ref, centroids_ref, out_ref):
+    blocks, cap = out_ref.shape[0], out_ref.shape[1]
+    group = min(cap, 16)
     lane = lax.broadcasted_iota(jnp.int32, (cap, group * 16), 1).astype(F32)
-    move.wait()
-    for block in range(blocks):
-        chosen = (lane == spot[:, block : block + 1]).astype(F32).astype(BF16)
+    for at in range(blocks):
+        block = first + at
+        chosen = (lane == spot_ref[:, block : block + 1]).astype(F32).astype(BF16)
         for start in range(0, cap, group):
-            tiles = []
-            for at in range(start, start + group):
-                base = pl.multiple_of(scalar_ref[block, at], 16)
-                tiles.append(centroids_ref[pl.ds(base, 16), :])
-            value = jnp.dot(
+            tiles = [
+                centroids_ref[pl.ds(pl.multiple_of(scalar_ref[block, slot], 16), 16), :]
+                for slot in range(start, start + group)
+            ]
+            out_ref[at, start : start + group, :] = jnp.dot(
                 chosen[start : start + group],
                 jnp.concatenate(tiles, axis=0),
                 preferred_element_type=F32,
             ).astype(BF16)
-            per = blocks // len(outs)
-            outs[block // per][block % per, start : start + group, :] = value
-
-
-def lookup_kernel(held, lists, direct, cap, count, rows_ref, codebook_ref, *refs):
+
+
+def fetch_kernel(held, direct, rows_ref, centroids_ref, *refs):
+    outs = refs[:-4]
+    index_ref, spot_ref, scalar_ref, sem = refs[-4:]
+    blocks = index_ref.shape[0]
+    me = lax.axis_index("lists")
+    if direct:
+        lists = rows_ref.shape[0] // outs[0].shape[0]
+        near = [near_rows(rows_ref, me ^ step, blocks // lists) for step in range(lists)]
+        index_slots(held, near, index_ref, spot_ref)
+    else:
+        index_slots(held, [rows_ref], index_ref, spot_ref)
+    move = pltpu.make_async_copy(index_ref, scalar_ref, sem)
+    move.start()
+    move.wait()
+    for at, out in enumerate(outs):
+        first = (at + 1) * out.shape[0] if direct else 0
+        fetch_blocks(first, spot_ref, scalar_ref, centroids_ref, out)
+
+
+def fetch_rest_kernel(steps, index_ref, spot_ref, centroids_ref, *refs):
+    outs, (scalar_ref, sem) = refs[:-2], refs[-2:]
+    move = pltpu.make_async_copy(index_ref, scalar_ref, sem)
+    move.start()
+    move.wait()
+    for step, out in zip(steps, outs):
+        fetch_blocks(step * out.shape[0], spot_ref, scalar_ref, centroids_ref, out)
+
+
+def lookup_kernel(direct, count, codebook_ref, *refs):
     messages, refs = refs[:count], refs[count:]
-    picked_ref, slot_ref, codes_ref, tally_ref, turned_ref, words_ref = refs
+    picked_ref, codes_ref, tally_ref, turned_ref, words_ref = refs
     if not direct:
         messages = [messages[0].at[at] for at in range(messages[0].shape[0])]
     subs = len(messages)
     width = messages[0].shape[1]
-    rows = rows_ref.shape[1]
     spaces = codes_ref.shape[0]
+    rows = codes_ref.shape[1] // subs
     depth = width // spaces
     words = words_ref.shape[0] * 128
     halves = width // rows
     tail = spaces // halves
-    me = lax.axis_index("lists")
-    if direct:
-        tables = near_rows(rows_ref, me, subs)
-    else:
-        tables = rows_ref[pl.ds(pl.multiple_of(me * subs, subs), subs), :]
-    owners = tables // held
-    rank = jnp.zeros((subs, rows), F32)
-    flags = [(owners == at).astype(F32) for at in range(lists)]
-    stacked = jnp.concatenate(flags, axis=0)
-    before = jnp.dot(stacked.astype(BF16), strict_before(rows), preferred_element_type=F32)
-    for at in range(lists):
-        rank = rank + flags[at] * before[at * subs : (at + 1) * subs]
-    place = (owners ^ me) if direct else owners
-    slot = place.astype(F32) * cap + rank
-    slot_ref[...] = jnp.transpose(jnp.concatenate([slot] * (rows // subs), axis=0))
     for at in range(subs):
         for half in range(halves):
             codes_ref[half * tail : (half + 1) * tail, at * rows : (at + 1) * rows] = messages[at][
@@ -196,6 +205,23 @@
             cells.append(value)
         parts.append(jnp.concatenate(cells, axis=1))
     picked_ref[...] = jnp.transpose(jnp.concatenate(parts, axis=0)).astype(BF16)
+    if direct:
+        low_words = words * spaces // tally_ref.shape[1]
+        codes = codes_ref[...].astype(jnp.int32)
+        high, low = codes // low_words, codes % low_words
+        highs = [(high == at).astype(F32).astype(BF16) for at in range(words // low_words)]
+        lows = [(low == at).astype(F32).astype(BF16) for at in range(low_words)]
+        pairs = lax.dot_general(
+            jnp.concatenate(lows, axis=0),
+            jnp.concatenate(highs, axis=0),
+            (((1,), (1,)), ((), ())),
+            preferred_element_type=F32,
+        )
+        first = lax.broadcasted_iota(jnp.int32, pairs.shape, 0) % spaces
+        second = lax.broadcasted_iota(jnp.int32, pairs.shape, 1) % spaces
+        pairs = jnp.where(first == second, pairs, 0.0)
+        tally_ref[...] = jnp.sum(pairs.reshape(low_words, spaces, pairs.shape[1]), axis=1)
+        return
     tally = jnp.zeros((words, 128), F32)
     word = lax.broadcasted_iota(jnp.int32, (words, subs * rows), 0).astype(F32)
     lane = lax.broadcasted_iota(jnp.int32, (subs * rows, 128), 1)
@@ -207,21 +233,56 @@
     tally_ref[...] = tally
 
 
-def place_kernel(direct, count, slot_ref, picked_ref, *refs):
+def in_order(slot_ref, at, start, pieces):
+    rows = slot_ref.shape[0]
+    total = sum(piece.shape[1] for piece in pieces)
+    column = start + lax.broadcasted_iota(jnp.int32, (rows, total), 1).astype(F32)
+    chosen = (column == slot_ref[:, at : at + 1]).astype(F32).astype(BF16)
+    stacked = jnp.concatenate([piece[at] for piece in pieces], axis=0)
+    return jnp.dot(chosen, stacked, preferred_element_type=F32)
+
+
+def order_kernel(held, lists, direct, cap, rows_ref, *refs):
+    pieces, (slot_ref, centre_ref) = refs[:-2], refs[-2:]
+    rows = rows_ref.shape[1]
+    subs = pieces[0].shape[0]
+    me = lax.axis_index("lists")
+    if direct:
+        tables = near_rows(rows_ref, me, subs)
+    else:
+        tables = rows_ref[pl.ds(pl.multiple_of(me * subs, subs), subs), :]
+    owners = tables // held
+    rank = jnp.zeros((subs, rows), F32)
+    flags = [(owners == at).astype(F32) for at in range(lists)]
+    stacked = jnp.concatenate(flags, axis=0)
+    before = jnp.dot(stacked.astype(BF16), strict_before(rows), preferred_element_type=F32)
+    for at in range(lists):
+        rank = rank + flags[at] * before[at * subs : (at + 1) * subs]
+    place = (owners ^ me) if direct else owners
+    slot = place.astype(F32) * cap + rank
+    slot_ref[...] = jnp.transpose(jnp.concatenate([slot] * (rows // subs), axis=0))
+    for at in range(subs):
+        centre_ref[at * rows : (at + 1) * rows, :] = in_order(slot_ref, at, 0.0, pieces).astype(BF16)
+
+
+def order_rest_kernel(start, slot_ref, part_ref, piece_ref, centre_ref):
+    rows = slot_ref.shape[0]
+    for at in range(piece_ref.shape[0]):
+        span = slice(at * rows, (at + 1) * rows)
+        rest = in_order(slot_ref, at, start, [piece_ref])
+        centre_ref[span, :] = (part_ref[span, :].astype(F32) + rest).astype(BF16)
+
+
+def place_kernel(direct, count, centre_ref, picked_ref, *refs):
     messages, refs = refs[:count], refs[count:]
     if not direct:
         messages = [messages[0].at[at] for at in range(messages[0].shape[0])]
     subs = len(messages)
-    spread = subs if direct else 1
-    pieces, rebuilt, residual_ref = refs[: -1 - spread], refs[-1 - spread : -1], refs[-1]
-    rows = slot_ref.shape[0]
-    total = sum(piece.shape[1] for piece in pieces)
-    column = lax.broadcasted_iota(jnp.int32, (rows, total), 1).astype(F32)
+    rebuilt, residual_ref = refs[:-1], refs[-1]
+    rows = centre_ref.shape[0] // subs
     for at in range(subs):
-        chosen = (column == slot_ref[:, at : at + 1]).astype(F32).astype(BF16)
-        stacked = jnp.concatenate([piece[at] for piece in pieces], axis=0)
-        centre = jnp.dot(chosen, stacked, preferred_element_type=F32)
         span = slice(at * rows, (at + 1) * rows)
+        centre = centre_ref[span, :].astype(F32)
         out = rebuilt[at] if direct else rebuilt[0].at[at]
         out[...] = (centre + picked_ref[span, :].astype(F32)).astype(BF16)
         residual_ref[span, :] = (messages[at][:rows, :].astype(F32) - centre).astype(BF16)
@@ -231,7 +292,7 @@
     outs, total_ref = refs[:-1], refs[-1]
     spaces, rows = codes_ref.shape
     width = residual_ref.shape[1]
-    words = tally_ref.shape[0]
+    words = total_ref.shape[0]
     depth = width // spaces
     share = words // lists
     word = lax.broadcasted_iota(jnp.int32, (words, rows), 0).astype(F32)
@@ -254,12 +315,8 @@
                 out[half * share : (half + 1) * share, :] = total_ref[
                     span, half * 128 : (half + 1) * 128
                 ].astype(BF16)
-            counts = tally_ref[span, :]
-            fold = 128 // spaces
-            lines = share // fold
-            out[halves * share :, :] = jnp.concatenate(
-                [counts[at * lines : (at + 1) * lines, :spaces] for at in range(fold)], axis=1
-            ).astype(BF16)
+            lanes = pl.ds(pl.multiple_of(at * 128, 128), 128)
+            out[halves * share :, :] = tally_ref[:, lanes].astype(BF16)
         else:
             out[:, :width] = total_ref[span, :].astype(BF16)
             out[:, width:] = tally_ref[span, :].astype(BF16)
@@ -384,24 +441,34 @@
     tables = all_swap(tables.reshape(lists * subs, 1, rows), ("lists", "sub"))
     tables = tables.reshape(lists * subs, rows)
 
-    pieces = call(
-        functools.partial(fetch_kernel, held, lists, direct),
-        [shape((subs, cap, width), BF16)] * lists
-        if direct
-        else [shape((lists * subs, cap, width), BF16)],
-        600_000_000,
+    blocks = lists * subs
+    scalars = [pltpu.SMEM((blocks, cap), jnp.int32), pltpu.SemaphoreType.DMA]
+    early = lists // 2 if direct else 1
+    *pieces, index, spot = call(
+        functools.partial(fetch_kernel, held, direct),
+        [shape((subs if direct else blocks, cap, width), BF16)] * early
+        + [shape((blocks, cap), jnp.int32), shape((cap, max(blocks, 128)), F32)],
+        FETCH_FLOPS,
         held * width * 2,
         tables,
         centroids,
-        scratch=[
-            pltpu.VMEM((lists * subs, cap), jnp.int32),
-            pltpu.SMEM((lists * subs, cap), jnp.int32),
-            pltpu.SemaphoreType.DMA,
-        ],
+        scratch=scalars,
     )
     fetched = pieces[0]
     if direct:
-        pieces = exchange(pieces, "lists")
+        late = list(range(early + 1, lists)) + [0]
+        rest = call(
+            functools.partial(fetch_rest_kernel, late),
+            [shape((subs, cap, width), BF16)] * len(late),
+            0,
+            0,
+            index,
+            spot,
+            centroids,
+            scratch=scalars,
+        )
+        fetched = rest[-1]
+        pieces = exchange([fetched] + list(pieces) + list(rest[:-1]), "lists")
     else:
         found = all_swap(pieces[0].reshape(lists, subs * cap, width), "lists")
         found = found.reshape(lists, subs, cap, width)
@@ -411,8 +478,8 @@
     messages = call(
         functools.partial(rotate_kernel, subs, direct),
         [shape((long, width), BF16)] * subs if direct else [shape((subs, long, width), BF16)],
-        1_000,
-        1_000,
+        0,
+        0,
         passages,
         rotation,
         codes,
@@ -422,31 +489,50 @@
     )
     messages = exchange(messages, "sub") if direct else [all_swap(messages[0], "sub")]
 
-    picked, slot, codes_t, tally = call(
-        functools.partial(lookup_kernel, held, lists, direct, cap, len(messages)),
+    picked, codes_t, tally = call(
+        functools.partial(lookup_kernel, direct, len(messages)),
         [
             shape((subs * rows, width), BF16),
-            shape((rows, rows), F32),
             shape((spaces, subs * rows), F32),
-            shape((words, 128), F32),
+            shape((share * spaces // 128, lists * 128) if direct else (words, 128), F32),
         ],
-        1_000_000,
-        1_000,
-        tables,
+        0,
+        0,
         codebook,
         *messages,
-        scratch=[pltpu.VMEM((words * depth, 128), F32), pltpu.VMEM((words // 128, width, 128), F32)],
-    )
+        scratch=[
+            pltpu.VMEM((words * depth, 128), F32),
+            pltpu.VMEM((words // 128, width, 128), F32),
+        ],
+    )
+    first = pieces[:-1] if direct else pieces
+    slot, centre = call(
+        functools.partial(order_kernel, held, lists, direct, cap),
+        [shape((rows, rows), F32), shape((subs * rows, width), BF16)],
+        ORDER_FLOPS,
+        0,
+        tables,
+        *first,
+    )
+    if direct:
+        centre = call(
+            functools.partial(order_rest_kernel, float((lists - 1) * cap)),
+            shape((subs * rows, width), BF16),
+            ORDER_REST_FLOPS,
+            0,
+            slot,
+            centre,
+            pieces[-1],
+        )
     *rebuilt, residual = call(
         functools.partial(place_kernel, direct, len(messages)),
         ([shape((rows, width), BF16)] * subs if direct else [shape((subs, rows, width), BF16)])
         + [shape((subs * rows, width), BF16)],
-        300_000_000,
-        2_000_000,
-        slot,
+        0,
+        0,
+        centre,
         picked,
         *messages,
-        *pieces,
     )
     rebuilt = exchange(rebuilt, "sub") if direct else [all_swap(rebuilt[0], "sub")]
     sums = call(

time: 47.7 us -> 46.5 us (0.975)
  waiting for transfers between devices: 7.96 us -> 5.61 us
  starting transfers between devices: 11.9 us -> 12.8 us
    ppermute x12, waiting for transfers between devices: 7.96 us -> 5.61 us  [swap(): return lax.ppermute(value, axis, [(at, at ^ step) for at in range(count)])]
    ppermute x12, starting transfers between devices: 11.9 us -> 12.8 us  [swap(): return lax.ppermute(value, axis, [(at, at ^ step) for at in range(count)])]
    pallas_call x8 -> x11, Pallas kernels: 11.4 us -> 11.7 us  [call(): pl.pallas_call(kernel, out_shape=out_shape, in_specs=[whole() for _ in ar...]
  transfers between devices with their start and end apart: 12 -> 12, of which waited for: 4 -> 5; matrix products, arithmetic and copies ran while one was open for 0% -> 0% of each run, Pallas kernels for 13% -> 16%
where the time goes in v6:
time: 46.5 us; the launch traced here: 46.3 us
  blocking collectives  13.8 us (30%)
  starting transfers between devices  12.8 us (28%)
  Pallas kernels  11.7 us (25%)
  waiting for transfers between devices  5.61 us (12%)
  local copies, waits for them, and re-layouts  1.62 us (3%)
  between operations  0.78 us (2%)
    all_to_all x1, blocking collectives, all_swap(): return lax.all_to_all(value, axis, split_axis=0, concat_axis=0, tiled=True)  13.8 us
    ppermute x12, starting transfers between devices, swap(): return lax.ppermute(value, axis, [(at, at ^ step) for at in range(count)])  12.8 us
    pallas_call x11, Pallas kernels, call(): pl.pallas_call(kernel, out_shape=out_shape, in_specs=[whole() for _ in ar...  11.7 us
    ppermute x12, waiting for transfers between devices, swap(): return lax.ppermute(value, axis, [(at, at ^ step) for at in range(count)])  5.61 us
    unnamed x14, local copies, waits for them, and re-layouts  1.62 us
  transfers between devices with their start and end apart: 12, of which 5 were waited for; matrix products, arithmetic and copies ran while one was open for 0% of the time, Pallas kernels for 16%

profile of v6, /device:TPU:0, one launch (start us, length us, event | category | flops | bytes accessed | tf_op | source)
XLA Modules:
  0.0 46.3 jit_solution(7816755446782260851)
XLA Ops:
  0.6 0.0 copy-start.5
  0.6 0.9 %copy-done.5 = s32[65536]{0:T(1024)S(1)} copy-done((s32[65536]{0:T(1024)S(1)}, s32[65536]{0:T(1024)}, u32[]{:S(2)}) %copy-start.5) | copy-done | bytes 262168
  1.6 0.0 copy-start.6
  1.6 0.7 %copy-done.6 = s32[128]{0:T(128)S(1)} copy-done((s32[128]{0:T(128)S(1)}, s32[128]{0:T(128)}, u32[]{:S(2)}) %copy-start.6) | copy-done | bytes 536
  2.2 0.0 copy-start
  2.2 0.4 shard_map.86
  2.7 13.8 %all_to_all.5 = s32[16,1,128]{2,1,0:T(1,128)S(1)} all-to-all(s32[16,1,128]{2,1,0:T(1,128)S(1)} %bitcast.8), channel_id=1, replica_groups=mesh['groups'=2,'lists'=4,'sub'=4] {'lists','sub'}, dimensions={0} | all-to-all | bytes 16384 | tf_op jit(solution)/shard_map/all_to_all | solution.py:416
  16.5 0.0 copy-done
  16.5 0.0 copy-start.1
  16.5 0.0 copy-start.2
  16.5 0.0 copy-start.4
  16.5 0.0 copy-start.3
  16.5 2.3 %shard_map.87 = (bf16[4,64,256]{2,1,0:T(8,128)(2,1)S(1)}, bf16[4,64,256]{2,1,0:T(8,128)(2,1)S(1)}, s32[16,64]{1,0:T(8,128)S(1)}, f32[64,128]{1,0:T(8,128)S(1)}) custom-call(s32[16,128]{1,0:T(8,128)S(1)} %bitcast.6, bf16[16384,256]{1,0:T(8,128)(2,1)S(1)} %copy-done), custom_call_target="tpu_custom_call" | custom-call | flops 600000000 | bytes 8388608 | tf_op jit(solution)/shard_map/pallas_call | solution.py:22
  18.9 0.6 %collective-permute-start = (bf16[4,64,256]{2,1,0:T(8,128)(2,1)S(1)}, bf16[4,64,256]{2,1,0:T(8,128)(2,1)S(1)}, u32[]{:S(2)}, u32[]{:S(2)}) collective-permute-start(bf16[4,64,256]{2,1,0:T(8,128)(2,1)S(1)} %get-tuple-element.31), channel_id=1, source_target_pairs={{0,4},{4,0},{8,12},{12,8},{1,5},{5,1},{9,13},{13,9},{2,6},{6,2},{1... | collective-permute-start | bytes 393224 | tf_op jit(solution)/shard_map/ppermute | solution.py:405
  19.4 0.6 %collective-permute-start.1 = (bf16[4,64,256]{2,1,0:T(8,128)(2,1)S(1)}, bf16[4,64,256]{2,1,0:T(8,128)(2,1)S(1)}, u32[]{:S(2)}, u32[]{:S(2)}) collective-permute-start(bf16[4,64,256]{2,1,0:T(8,128)(2,1)S(1)} %get-tuple-element.32), channel_id=1, source_target_pairs={{0,8},{4,12},{8,0},{12,4},{1,9},{5,13},{9,1},{13,5},{2,10},{6,14},... | collective-permute-start | bytes 393224 | tf_op jit(solution)/shard_map/ppermute | solution.py:405
  20.0 1.5 %shard_map.88 = (bf16[4,64,256]{2,1,0:T(8,128)(2,1)S(1)}, bf16[4,64,256]{2,1,0:T(8,128)(2,1)S(1)}) custom-call(s32[16,64]{1,0:T(8,128)S(1)} %get-tuple-element.28.index_ref, f32[64,128]{1,0:T(8,128)S(1)} %get-tuple-element.29.spot_ref, bf16[16384,256]{1,0:T(8,128)(2,1)S(1)} %copy-done), custom_call_target="tpu_custom_call" | custom-call | tf_op jit(solution)/shard_map/pallas_call | solution.py:22
  21.5 0.0 copy-done.1
  21.5 0.0 copy-done.2
  21.5 0.0 copy-done.4
  21.5 0.5 %shard_map.91 = (bf16[144,256]{1,0:T(8,128)(2,1)S(1)}, bf16[144,256]{1,0:T(8,128)(2,1)S(1)}, bf16[144,256]{1,0:T(8,128)(2,1)S(1)}, bf16[144,256]{1,0:T(8,128)(2,1)S(1)}) custom-call(bf16[128,1024]{1,0:T(8,128)(2,1)S(1)} %copy-done.2, bf16[1024,1024]{1,0:T(8,128)(2,1)S(1)} %copy-done.1, s32[128,128]{1,0:T(8,128)S(1)} %copy-done.4, ...), custom_call_target="tpu_custom_call" | custom-call | tf_op jit(solution)/shard_map/pallas_call | solution.py:22
  22.0 0.1 collective-permute-start.3
  22.1 0.6 %collective-permute-start.4 = (bf16[144,256]{1,0:T(8,128)(2,1)S(1)}, bf16[144,256]{1,0:T(8,128)(2,1)S(1)}, u32[]{:S(2)}, u32[]{:S(2)}) collective-permute-start(bf16[144,256]{1,0:T(8,128)(2,1)S(1)} %get-tuple-element.38), channel_id=1, source_target_pairs={{0,2},{1,3},{2,0},{3,1},{4,6},{5,7},{6,4},{7,5},{8,10},{9,11},{10,... | collective-permute-start | bytes 221192 | tf_op jit(solution)/shard_map/ppermute | solution.py:405
  22.7 1.2 %collective-permute-start.5 = (bf16[144,256]{1,0:T(8,128)(2,1)S(1)}, bf16[144,256]{1,0:T(8,128)(2,1)S(1)}, u32[]{:S(2)}, u32[]{:S(2)}) collective-permute-start(bf16[144,256]{1,0:T(8,128)(2,1)S(1)} %get-tuple-element.39), channel_id=1, source_target_pairs={{0,3},{1,2},{2,1},{3,0},{4,7},{5,6},{6,5},{7,4},{8,11},{9,10},{10,... | collective-permute-start | bytes 221192 | tf_op jit(solution)/shard_map/ppermute | solution.py:405
  24.0 0.0 collective-permute-done.3.refs_1_
  24.0 3.3 %collective-permute-start.2 = (bf16[4,64,256]{2,1,0:T(8,128)(2,1)S(1)}, bf16[4,64,256]{2,1,0:T(8,128)(2,1)S(1)}, u32[]{:S(2)}, u32[]{:S(2)}) collective-permute-start(bf16[4,64,256]{2,1,0:T(8,128)(2,1)S(1)} %get-tuple-element.35), channel_id=1, source_target_pairs={{0,12},{4,8},{8,4},{12,0},{1,13},{5,9},{9,5},{13,1},{2,14},{6,10},... | collective-permute-start | bytes 393224 | tf_op jit(solution)/shard_map/ppermute | solution.py:405
  27.2 0.0 collective-permute-done.4.refs_2_
  27.3 0.7 %collective-permute-done.5.refs_3_ = bf16[144,256]{1,0:T(8,128)(2,1)S(1)} collective-permute-done((bf16[144,256]{1,0:T(8,128)(2,1)S(1)}, bf16[144,256]{1,0:T(8,128)(2,1)S(1)}, u32[]{:S(2)}, u32[]{:S(2)}) %collective-permute-start.5) | collective-permute-done | bytes 73760 | tf_op jit(solution)/shard_map/ppermute | solution.py:405
  27.9 0.0 copy-done.3
  27.9 1.1 %shard_map.92 = (bf16[512,256]{1,0:T(8,128)(2,1)S(1)}, f32[32,512]{1,0:T(8,128)S(1)}, f32[16,512]{1,0:T(8,128)S(1)}) custom-call(bf16[32,2048]{1,0:T(8,128)(2,1)S(1)} %copy-done.3, bf16[144,256]{1,0:T(8,128)(2,1)S(1)} %get-tuple-element.36.refs_0_, bf16[144,256]{1,0:T(8,128)(2,1)S(1)} %collective-permute-done.3.refs_1_, ...), custom_call_target="tpu_custom_call" | custom-call | tf_op jit(solution)/shard_map/pallas_call | solution.py:22
  29.1 0.0 collective-permute-done.refs_1_
  29.1 0.0 collective-permute-done.1.refs_2_
  29.1 0.5 %shard_map.89 = (f32[128,128]{1,0:T(8,128)S(1)}, bf16[512,256]{1,0:T(8,128)(2,1)S(1)}) custom-call(s32[16,128]{1,0:T(8,128)S(1)} %bitcast.7, bf16[4,64,256]{2,1,0:T(8,128)(2,1)S(1)} %get-tuple-element.30.refs_0_.after_ref, bf16[4,64,256]{2,1,0:T(8,128)(2,1)S(1)} %collective-permute-done.refs_1_, bf16[4,64,256]{2,1,0:T(8,128)(2,1)S(1)} %collective-permute-done.1.refs_2_), custom_call_target="tpu_custom_call" | custom-call | flops 3000000000 | tf_op jit(solution)/shard_map/pallas_call | solution.py:22
  29.6 2.0 %collective-permute-done.2.piece_ref = bf16[4,64,256]{2,1,0:T(8,128)(2,1)S(1)} collective-permute-done((bf16[4,64,256]{2,1,0:T(8,128)(2,1)S(1)}, bf16[4,64,256]{2,1,0:T(8,128)(2,1)S(1)}, u32[]{:S(2)}, u32[]{:S(2)}) %collective-permute-start.2) | collective-permute-done | bytes 131104 | tf_op jit(solution)/shard_map/ppermute | solution.py:405
  31.6 0.3 shard_map.90.centre_ref
  31.9 0.1 shard_map.93
  32.0 0.1 collective-permute-start.6
  32.1 0.6 %collective-permute-start.7 = (bf16[128,256]{1,0:T(8,128)(2,1)S(1)}, bf16[128,256]{1,0:T(8,128)(2,1)S(1)}, u32[]{:S(2)}, u32[]{:S(2)}) collective-permute-start(bf16[128,256]{1,0:T(8,128)(2,1)S(1)} %get-tuple-element.43), channel_id=1, source_target_pairs={{0,2},{1,3},{2,0},{3,1},{4,6},{5,7},{6,4},{7,5},{8,10},{9,11},{10,... | collective-permute-start | bytes 196616 | tf_op jit(solution)/shard_map/ppermute | solution.py:405
  32.8 1.2 %collective-permute-start.8 = (bf16[128,256]{1,0:T(8,128)(2,1)S(1)}, bf16[128,256]{1,0:T(8,128)(2,1)S(1)}, u32[]{:S(2)}, u32[]{:S(2)}) collective-permute-start(bf16[128,256]{1,0:T(8,128)(2,1)S(1)} %get-tuple-element.44), channel_id=1, source_target_pairs={{0,3},{1,2},{2,1},{3,0},{4,7},{5,6},{6,5},{7,4},{8,11},{9,10},{10,... | collective-permute-start | bytes 196616 | tf_op jit(solution)/shard_map/ppermute | solution.py:405
  34.0 0.0 collective-permute-done.6.after_ref.refs_1_
  34.0 2.4 %shard_map.94 = (bf16[144,128]{1,0:T(8,128)(2,1)S(1)}, bf16[144,128]{1,0:T(8,128)(2,1)S(1)}, bf16[144,128]{1,0:T(8,128)(2,1)S(1)}, bf16[144,128]{1,0:T(8,128)(2,1)S(1)}) custom-call(f32[32,512]{1,0:T(8,128)S(1)} %get-tuple-element.45.codes_ref, bf16[512,256]{1,0:T(8,128)(2,1)S(1)} %get-tuple-element.46.residual_ref, ...), custom_call_target="tpu_custom_call" | custom-call | flops 2000000000 | bytes 1000000 | tf_op jit(solution)/shard_map/pallas_call | solution.py:22
  36.4 3.3 %collective-permute-start.9 = (bf16[144,128]{1,0:T(8,128)(2,1)S(1)}, bf16[144,128]{1,0:T(8,128)(2,1)S(1)}, u32[]{:S(2)}, u32[]{:S(2)}) collective-permute-start(bf16[144,128]{1,0:T(8,128)(2,1)S(1)} %get-tuple-element.48), channel_id=1, source_target_pairs={{0,12},{4,8},{8,4},{12,0},{1,13},{5,9},{9,5},{13,1},{2,14},{6,10},... | collective-permute-start | bytes 110600 | tf_op jit(solution)/shard_map/ppermute | solution.py:405
  39.7 0.5 %collective-permute-start.10 = (bf16[144,128]{1,0:T(8,128)(2,1)S(1)}, bf16[144,128]{1,0:T(8,128)(2,1)S(1)}, u32[]{:S(2)}, u32[]{:S(2)}) collective-permute-start(bf16[144,128]{1,0:T(8,128)(2,1)S(1)} %get-tuple-element.51), channel_id=1, source_target_pairs={{0,4},{4,0},{8,12},{12,8},{1,5},{5,1},{9,13},{13,9},{2,6},{6,2},{1... | collective-permute-start | bytes 110600 | tf_op jit(solution)/shard_map/ppermute | solution.py:405
  40.2 0.6 %collective-permute-start.11 = (bf16[144,128]{1,0:T(8,128)(2,1)S(1)}, bf16[144,128]{1,0:T(8,128)(2,1)S(1)}, u32[]{:S(2)}, u32[]{:S(2)}) collective-permute-start(bf16[144,128]{1,0:T(8,128)(2,1)S(1)} %get-tuple-element.52), channel_id=1, source_target_pairs={{0,8},{4,12},{8,0},{12,4},{1,9},{5,13},{9,1},{13,5},{2,10},{6,14},... | collective-permute-start | bytes 110600 | tf_op jit(solution)/shard_map/ppermute | solution.py:405
  40.8 0.0 collective-permute-done.7.refs_2_
  40.8 0.0 collective-permute-done.8.refs_3_
  40.8 1.4 %collective-permute-done.9.refs_4_.refs_3_ = bf16[144,128]{1,0:T(8,128)(2,1)S(1)} collective-permute-done((bf16[144,128]{1,0:T(8,128)(2,1)S(1)}, bf16[144,128]{1,0:T(8,128)(2,1)S(1)}, u32[]{:S(2)}, u32[]{:S(2)}) %collective-permute-start.9) | collective-permute-done | bytes 36896 | tf_op jit(solution)/shard_map/ppermute | solution.py:405
  42.2 1.5 %shard_map.95 = (bf16[128,1024]{1,0:T(8,128)(2,1)}, f32[8,128]{1,0:T(8,128)S(1)}) custom-call(bf16[128,1024]{1,0:T(8,128)(2,1)S(1)} %copy-done.2, bf16[1024,1024]{1,0:T(8,128)(2,1)S(1)} %copy-done.1, bf16[128,256]{1,0:T(8,128)(2,1)S(1)} %get-tuple-element.41.refs_0_, bf16[128,256]{1,0:T(8,128)(2,1)S(1)} %collective-permute-done.6.after_ref.refs_1_, ...), custom_call_target="tpu_custom_call" | custom-call | flops 1000 | bytes 1000 | tf_op jit(solution)/shard_map/pallas_call | solution.py:22
  43.7 0.3 collective-permute-done.10.refs_1_
  44.1 1.2 %collective-permute-done.11.refs_2_ = bf16[144,128]{1,0:T(8,128)(2,1)S(1)} collective-permute-done((bf16[144,128]{1,0:T(8,128)(2,1)S(1)}, bf16[144,128]{1,0:T(8,128)(2,1)S(1)}, u32[]{:S(2)}, u32[]{:S(2)}) %collective-permute-start.11) | collective-permute-done | bytes 36896 | tf_op jit(solution)/shard_map/ppermute | solution.py:405
  45.2 1.1 %shard_map.96 = f32[32,512]{1,0:T(8,128)} custom-call(bf16[32,2048]{1,0:T(8,128)(2,1)S(1)} %copy-done.3, bf16[144,128]{1,0:T(8,128)(2,1)S(1)} %get-tuple-element.50.refs_0_, bf16[144,128]{1,0:T(8,128)(2,1)S(1)} %collective-permute-done.10.refs_1_, bf16[144,128]{1,0:T(8,128)(2,1)S(1)} %collective-permute-done.11.refs_2_, ...), custom_call_target="tpu_custom_call" | custom-call | flops 100000000 | bytes 500000 | tf_op jit(solution)/shard_map/pallas_call | solution.py:22
Async XLA Ops:
  0.6 1.0 %copy-start.5 = (s32[65536]{0:T(1024)S(1)}, s32[65536]{0:T(1024)}, u32[]{:S(2)}) copy-start(s32[65536]{0:T(1024)} %param.10) | copy-start | bytes 786436
  1.6 0.7 %copy-start.6 = (s32[128]{0:T(128)S(1)}, s32[128]{0:T(128)}, u32[]{:S(2)}) copy-start(s32[128]{0:T(128)} %param.11) | copy-start | bytes 1540
  2.2 14.3 %copy-start = (bf16[16384,256]{1,0:T(8,128)(2,1)S(1)}, bf16[16384,256]{1,0:T(8,128)(2,1)}, u32[]{:S(2)}) copy-start(bf16[16384,256]{1,0:T(8,128)(2,1)} %centroids_ref.3) | copy-start | bytes 25165828
  16.5 5.0 %copy-start.1 = (bf16[1024,1024]{1,0:T(8,128)(2,1)S(1)}, bf16[1024,1024]{1,0:T(8,128)(2,1)}, u32[]{:S(2)}) copy-start(bf16[1024,1024]{1,0:T(8,128)(2,1)} %rotation_ref.3) | copy-start | bytes 6291460
  16.5 5.0 %copy-start.2 = (bf16[128,1024]{1,0:T(8,128)(2,1)S(1)}, bf16[128,1024]{1,0:T(8,128)(2,1)}, u32[]{:S(2)}) copy-start(bf16[128,1024]{1,0:T(8,128)(2,1)} %passages_ref.3) | copy-start | bytes 786436
  16.5 5.0 %copy-start.4 = (s32[128,128]{1,0:T(8,128)S(1)}, s32[128,128]{1,0:T(8,128)}, u32[]{:S(2)}) copy-start(s32[128,128]{1,0:T(8,128)} %codes_ref.1) | copy-start | bytes 196612
  16.5 11.4 %copy-start.3 = (bf16[32,2048]{1,0:T(8,128)(2,1)S(1)}, bf16[32,2048]{1,0:T(8,128)(2,1)}, u32[]{:S(2)}) copy-start(bf16[32,2048]{1,0:T(8,128)(2,1)} %codebook_ref.3) | copy-start | bytes 393220
  18.9 10.2 %collective-permute-start = (bf16[4,64,256]{2,1,0:T(8,128)(2,1)S(1)}, bf16[4,64,256]{2,1,0:T(8,128)(2,1)S(1)}, u32[]{:S(2)}, u32[]{:S(2)}) collective-permute-start(bf16[4,64,256]{2,1,0:T(8,128)(2,1)S(1)} %get-tuple-element.31), channel_id=1, source_target_pairs={{0,4},{4,0},{8,12},{12,8},{1,5},{5,1},{9,13},{13,9},{2,6},{6,2},{1... | collective-permute-start | bytes 393224 | tf_op jit(solution)/shard_map/ppermute | solution.py:405
  19.4 9.6 %collective-permute-start.1 = (bf16[4,64,256]{2,1,0:T(8,128)(2,1)S(1)}, bf16[4,64,256]{2,1,0:T(8,128)(2,1)S(1)}, u32[]{:S(2)}, u32[]{:S(2)}) collective-permute-start(bf16[4,64,256]{2,1,0:T(8,128)(2,1)S(1)} %get-tuple-element.32), channel_id=1, source_target_pairs={{0,8},{4,12},{8,0},{12,4},{1,9},{5,13},{9,1},{13,5},{2,10},{6,14},... | collective-permute-start | bytes 393224 | tf_op jit(solution)/shard_map/ppermute | solution.py:405
  22.0 1.9 %collective-permute-start.3 = (bf16[144,256]{1,0:T(8,128)(2,1)S(1)}, bf16[144,256]{1,0:T(8,128)(2,1)S(1)}, u32[]{:S(2)}, u32[]{:S(2)}) collective-permute-start(bf16[144,256]{1,0:T(8,128)(2,1)S(1)} %get-tuple-element.37), channel_id=1, source_target_pairs={{0,1},{1,0},{2,3},{3,2},{4,5},{5,4},{6,7},{7,6},{8,9},{9,8},{10,11... | collective-permute-start | bytes 221192 | tf_op jit(solution)/shard_map/ppermute | solution.py:405
  22.1 5.1 %collective-permute-start.4 = (bf16[144,256]{1,0:T(8,128)(2,1)S(1)}, bf16[144,256]{1,0:T(8,128)(2,1)S(1)}, u32[]{:S(2)}, u32[]{:S(2)}) collective-permute-start(bf16[144,256]{1,0:T(8,128)(2,1)S(1)} %get-tuple-element.38), channel_id=1, source_target_pairs={{0,2},{1,3},{2,0},{3,1},{4,6},{5,7},{6,4},{7,5},{8,10},{9,11},{10,... | collective-permute-start | bytes 221192 | tf_op jit(solution)/shard_map/ppermute | solution.py:405
  22.7 5.2 %collective-permute-start.5 = (bf16[144,256]{1,0:T(8,128)(2,1)S(1)}, bf16[144,256]{1,0:T(8,128)(2,1)S(1)}, u32[]{:S(2)}, u32[]{:S(2)}) collective-permute-start(bf16[144,256]{1,0:T(8,128)(2,1)S(1)} %get-tuple-element.39), channel_id=1, source_target_pairs={{0,3},{1,2},{2,1},{3,0},{4,7},{5,6},{6,5},{7,4},{8,11},{9,10},{10,... | collective-permute-start | bytes 221192 | tf_op jit(solution)/shard_map/ppermute | solution.py:405
  24.0 7.7 %collective-permute-start.2 = (bf16[4,64,256]{2,1,0:T(8,128)(2,1)S(1)}, bf16[4,64,256]{2,1,0:T(8,128)(2,1)S(1)}, u32[]{:S(2)}, u32[]{:S(2)}) collective-permute-start(bf16[4,64,256]{2,1,0:T(8,128)(2,1)S(1)} %get-tuple-element.35), channel_id=1, source_target_pairs={{0,12},{4,8},{8,4},{12,0},{1,13},{5,9},{9,5},{13,1},{2,14},{6,10},... | collective-permute-start | bytes 393224 | tf_op jit(solution)/shard_map/ppermute | solution.py:405
  32.0 1.9 %collective-permute-start.6 = (bf16[128,256]{1,0:T(8,128)(2,1)S(1)}, bf16[128,256]{1,0:T(8,128)(2,1)S(1)}, u32[]{:S(2)}, u32[]{:S(2)}) collective-permute-start(bf16[128,256]{1,0:T(8,128)(2,1)S(1)} %get-tuple-element.42), channel_id=1, source_target_pairs={{0,1},{1,0},{2,3},{3,2},{4,5},{5,4},{6,7},{7,6},{8,9},{9,8},{10,11... | collective-permute-start | bytes 196616 | tf_op jit(solution)/shard_map/ppermute | solution.py:405
  32.1 8.7 %collective-permute-start.7 = (bf16[128,256]{1,0:T(8,128)(2,1)S(1)}, bf16[128,256]{1,0:T(8,128)(2,1)S(1)}, u32[]{:S(2)}, u32[]{:S(2)}) collective-permute-start(bf16[128,256]{1,0:T(8,128)(2,1)S(1)} %get-tuple-element.43), channel_id=1, source_target_pairs={{0,2},{1,3},{2,0},{3,1},{4,6},{5,7},{6,4},{7,5},{8,10},{9,11},{10,... | collective-permute-start | bytes 196616 | tf_op jit(solution)/shard_map/ppermute | solution.py:405
  32.8 8.1 %collective-permute-start.8 = (bf16[128,256]{1,0:T(8,128)(2,1)S(1)}, bf16[128,256]{1,0:T(8,128)(2,1)S(1)}, u32[]{:S(2)}, u32[]{:S(2)}) collective-permute-start(bf16[128,256]{1,0:T(8,128)(2,1)S(1)} %get-tuple-element.44), channel_id=1, source_target_pairs={{0,3},{1,2},{2,1},{3,0},{4,7},{5,6},{6,5},{7,4},{8,11},{9,10},{10,... | collective-permute-start | bytes 196616 | tf_op jit(solution)/shard_map/ppermute | solution.py:405
  36.4 5.9 %collective-permute-start.9 = (bf16[144,128]{1,0:T(8,128)(2,1)S(1)}, bf16[144,128]{1,0:T(8,128)(2,1)S(1)}, u32[]{:S(2)}, u32[]{:S(2)}) collective-permute-start(bf16[144,128]{1,0:T(8,128)(2,1)S(1)} %get-tuple-element.48), channel_id=1, source_target_pairs={{0,12},{4,8},{8,4},{12,0},{1,13},{5,9},{9,5},{13,1},{2,14},{6,10},... | collective-permute-start | bytes 110600 | tf_op jit(solution)/shard_map/ppermute | solution.py:405
  39.7 4.4 %collective-permute-start.10 = (bf16[144,128]{1,0:T(8,128)(2,1)S(1)}, bf16[144,128]{1,0:T(8,128)(2,1)S(1)}, u32[]{:S(2)}, u32[]{:S(2)}) collective-permute-start(bf16[144,128]{1,0:T(8,128)(2,1)S(1)} %get-tuple-element.51), channel_id=1, source_target_pairs={{0,4},{4,0},{8,12},{12,8},{1,5},{5,1},{9,13},{13,9},{2,6},{6,2},{1... | collective-permute-start | bytes 110600 | tf_op jit(solution)/shard_map/ppermute | solution.py:405
  40.2 5.0 %collective-permute-start.11 = (bf16[144,128]{1,0:T(8,128)(2,1)S(1)}, bf16[144,128]{1,0:T(8,128)(2,1)S(1)}, u32[]{:S(2)}, u32[]{:S(2)}) collective-permute-start(bf16[144,128]{1,0:T(8,128)(2,1)S(1)} %get-tuple-element.52), channel_id=1, source_target_pairs={{0,8},{4,12},{8,0},{12,4},{1,9},{5,13},{9,1},{13,5},{2,10},{6,14},... | collective-permute-start | bytes 110600 | tf_op jit(solution)/shard_map/ppermute | solution.py:405

commit v7 on v6

--- a/solution.py
+++ b/solution.py
@@ -86,7 +86,7 @@
     )
 
 
-def index_slots(held, rows_refs, index_ref, spot_ref):
+def index_slots(held, rows_refs, index_ref, spot_ref, move):
     blocks, cap = index_ref.shape
     rows = rows_refs[0].shape[1]
     group = min(cap, 16)
@@ -109,6 +109,7 @@
         )
     index = jnp.concatenate(index, axis=0).astype(jnp.int32)
     index_ref[...] = index & -16
+    move.start()
     within = lax.broadcasted_iota(jnp.int32, (blocks, cap), 1) & (group - 1)
     spot = (within * 16 + (index & 15)).astype(F32)
     spot_ref[...] = jnp.transpose(jnp.concatenate([spot] * pad, axis=0))
@@ -141,11 +142,10 @@
     if direct:
         lists = rows_ref.shape[0] // outs[0].shape[0]
         near = [near_rows(rows_ref, me ^ step, blocks // lists) for step in range(lists)]
-        index_slots(held, near, index_ref, spot_ref)
     else:
-        index_slots(held, [rows_ref], index_ref, spot_ref)
+        near = [rows_ref]
     move = pltpu.make_async_copy(index_ref, scalar_ref, sem)
-    move.start()
+    index_slots(held, near, index_ref, spot_ref, move)
     move.wait()
     for at, out in enumerate(outs):
         first = (at + 1) * out.shape[0] if direct else 0
@@ -265,7 +265,7 @@
         centre_ref[at * rows : (at + 1) * rows, :] = in_order(slot_ref, at, 0.0, pieces).astype(BF16)
 
 
-def order_rest_kernel(start, slot_ref, part_ref, piece_ref, centre_ref):
+def order_rest_kernel(start, slot_ref, part_ref, piece_ref, after_ref, centre_ref):
     rows = slot_ref.shape[0]
     for at in range(piece_ref.shape[0]):
         span = slice(at * rows, (at + 1) * rows)
@@ -278,32 +278,73 @@
     if not direct:
         messages = [messages[0].at[at] for at in range(messages[0].shape[0])]
     subs = len(messages)
-    rebuilt, residual_ref = refs[:-1], refs[-1]
+    rebuilt, residual_ref = (refs, None) if direct else (refs[:-1], refs[-1])
     rows = centre_ref.shape[0] // subs
     for at in range(subs):
         span = slice(at * rows, (at + 1) * rows)
         centre = centre_ref[span, :].astype(F32)
         out = rebuilt[at] if direct else rebuilt[0].at[at]
         out[...] = (centre + picked_ref[span, :].astype(F32)).astype(BF16)
-        residual_ref[span, :] = (messages[at][:rows, :].astype(F32) - centre).astype(BF16)
-
-
-def sums_kernel(lists, direct, codes_ref, residual_ref, tally_ref, after_ref, *refs):
-    outs, total_ref = refs[:-1], refs[-1]
-    spaces, rows = codes_ref.shape
-    width = residual_ref.shape[1]
-    words = total_ref.shape[0]
+        if not direct:
+            residual_ref[span, :] = (messages[at][:rows, :].astype(F32) - centre).astype(BF16)
+
+
+def add_words(total, codes, residual):
+    spaces, rows = codes.shape
+    words, width = total.shape
     depth = width // spaces
-    share = words // lists
     word = lax.broadcasted_iota(jnp.int32, (words, rows), 0).astype(F32)
     owner = lax.broadcasted_iota(jnp.int32, (rows, width), 1) // depth
-    residual = residual_ref[...]
-    total = jnp.zeros((words, width), F32)
     for space in range(spaces):
-        hot = (word == codes_ref[space : space + 1, :]).astype(F32).astype(BF16)
+        hot = (word == codes[space : space + 1, :]).astype(F32).astype(BF16)
         part = jnp.where(owner == space, residual, jnp.zeros_like(residual))
         total = total + jnp.dot(hot, part, preferred_element_type=F32)
-    total_ref[...] = total
+    return total
+
+
+def early_sums_kernel(limit, codes_ref, slot_ref, centre_ref, *refs):
+    messages, out_ref = refs[:-1], refs[-1]
+    rows = slot_ref.shape[0]
+    residual = []
+    for at, message in enumerate(messages):
+        centre = centre_ref[at * rows : (at + 1) * rows, :].astype(F32)
+        value = message[:rows, :].astype(F32) - centre
+        residual.append(jnp.where(slot_ref[:, at : at + 1] < limit, value, 0.0).astype(BF16))
+    total = jnp.zeros(out_ref.shape, F32)
+    out_ref[...] = add_words(total, codes_ref[...], jnp.concatenate(residual, axis=0))
+
+
+def late_sums_kernel(limit, codes_ref, slot_ref, piece_ref, early_ref, tally_ref, *refs):
+    messages, outs, total_ref = refs[: piece_ref.shape[0]], refs[piece_ref.shape[0] + 1 : -1], refs[-1]
+    rows = slot_ref.shape[0]
+    subs, cap, width = piece_ref.shape
+    column = limit + lax.broadcasted_iota(jnp.int32, (rows, cap), 1).astype(F32)
+    residual, codes = [], []
+    for at, message in enumerate(messages):
+        chosen = (column == slot_ref[:, at : at + 1]).astype(F32)
+        turned = jnp.transpose(chosen)
+        used = jnp.sum(turned, axis=1, keepdims=True) > 0.0
+        rotated = jnp.dot(turned.astype(BF16), message[:rows, :], preferred_element_type=F32)
+        value = rotated - piece_ref[at].astype(F32)
+        residual.append(jnp.where(used, value, 0.0).astype(BF16))
+        own = codes_ref[:, at * rows : (at + 1) * rows].astype(BF16)
+        codes.append(jnp.dot(own, chosen.astype(BF16), preferred_element_type=F32))
+    residual = jnp.concatenate(residual, axis=0)
+    total_ref[...] = add_words(early_ref[...], jnp.concatenate(codes, axis=1), residual)
+    send_sums(True, total_ref, tally_ref, outs)
+
+
+def sums_kernel(codes_ref, residual_ref, tally_ref, *refs):
+    outs, total_ref = refs[:-1], refs[-1]
+    total = jnp.zeros(total_ref.shape, F32)
+    total_ref[...] = add_words(total, codes_ref[...], residual_ref[...])
+    send_sums(False, total_ref, tally_ref, outs)
+
+
+def send_sums(direct, total_ref, tally_ref, outs):
+    words, width = total_ref.shape
+    lists = lax.axis_size("lists")
+    share = words // lists
     me = lax.axis_index("lists")
     for step in range(lists):
         out = outs[step] if direct else outs[0].at[step]
@@ -506,7 +547,7 @@
         ],
     )
     first = pieces[:-1] if direct else pieces
-    slot, centre = call(
+    slot, part = call(
         functools.partial(order_kernel, held, lists, direct, cap),
         [shape((rows, rows), F32), shape((subs * rows, width), BF16)],
         ORDER_FLOPS,
@@ -514,41 +555,70 @@
         tables,
         *first,
     )
-    if direct:
+    centre = part
+    if direct:
+        early_sums = call(
+            functools.partial(early_sums_kernel, float((lists - 1) * cap)),
+            shape((words, width), F32),
+            2_000_000_000,
+            0,
+            codes_t,
+            slot,
+            part,
+            *messages,
+        )
         centre = call(
             functools.partial(order_rest_kernel, float((lists - 1) * cap)),
             shape((subs * rows, width), BF16),
             ORDER_REST_FLOPS,
             0,
             slot,
-            centre,
+            part,
             pieces[-1],
-        )
-    *rebuilt, residual = call(
+            early_sums,
+            loose=1,
+        )
+    rebuilt = call(
         functools.partial(place_kernel, direct, len(messages)),
-        ([shape((rows, width), BF16)] * subs if direct else [shape((subs, rows, width), BF16)])
-        + [shape((subs * rows, width), BF16)],
+        [shape((rows, width), BF16)] * subs
+        if direct
+        else [shape((subs, rows, width), BF16), shape((subs * rows, width), BF16)],
         0,
         0,
         centre,
         picked,
         *messages,
     )
+    if not direct:
+        rebuilt, residual = rebuilt[:1], rebuilt[1]
     rebuilt = exchange(rebuilt, "sub") if direct else [all_swap(rebuilt[0], "sub")]
-    sums = call(
-        functools.partial(sums_kernel, lists, direct),
-        [shape((width // 128 * share + share * spaces // 128, 128), BF16)] * lists
-        if direct
-        else [shape((lists, share, width + 128), BF16)],
-        2_000_000_000,
-        1_000_000,
-        codes_t,
-        residual,
-        tally,
-        rebuilt[1] if direct else residual,
-        loose=1,
-        scratch=[pltpu.VMEM((words, width), F32)],
-    )
+    if direct:
+        sums = call(
+            functools.partial(late_sums_kernel, float((lists - 1) * cap)),
+            [shape((width // 128 * share + share * spaces // 128, 128), BF16)] * lists,
+            1_000_000_000,
+            1_000_000,
+            codes_t,
+            slot,
+            pieces[-1],
+            early_sums,
+            tally,
+            *messages,
+            rebuilt[1],
+            loose=1,
+            scratch=[pltpu.VMEM((words, width), F32)],
+        )
+    else:
+        sums = call(
+            sums_kernel,
+            [shape((lists, share, width + 128), BF16)],
+            2_000_000_000,
+            1_000_000,
+            codes_t,
+            residual,
+            tally,
+            scratch=[pltpu.VMEM((words, width), F32)],
+        )
     sums = exchange(sums, "lists", (3, 2, 1)) if direct else [all_swap(sums[0], "lists")]
     recon_error, token = call(
         functools.partial(restore_kernel, direct),

time: 46.5 us -> 45.5 us (0.978)
  waiting for transfers between devices: 5.61 us -> 2.91 us
  Pallas kernels: 11.7 us -> 13.3 us
    ppermute x12, waiting for transfers between devices: 5.61 us -> 2.91 us  [swap(): return lax.ppermute(value, axis, [(at, at ^ step) for at in range(count)])]
    pallas_call x11 -> x12, Pallas kernels: 11.7 us -> 13.3 us  [call(): pl.pallas_call(kernel, out_shape=out_shape, in_specs=[whole() for _ in ar...]
  transfers between devices with their start and end apart: 12 -> 12, of which waited for: 5 -> 3; matrix products, arithmetic and copies ran while one was open for 0% -> 0% of each run, Pallas kernels for 16% -> 20%
where the time goes in v7:
time: 45.5 us; the launch traced here: 45.3 us
  blocking collectives  13.8 us (30%)
  Pallas kernels  13.3 us (29%)
  starting transfers between devices  12.9 us (28%)
  waiting for transfers between devices  2.91 us (6%)
  local copies, waits for them, and re-layouts  1.62 us (4%)
  between operations  0.79 us (2%)
    all_to_all x1, blocking collectives, all_swap(): return lax.all_to_all(value, axis, split_axis=0, concat_axis=0, tiled=True)  13.8 us
    pallas_call x12, Pallas kernels, call(): pl.pallas_call(kernel, out_shape=out_shape, in_specs=[whole() for _ in ar...  13.3 us
    ppermute x12, starting transfers between devices, swap(): return lax.ppermute(value, axis, [(at, at ^ step) for at in range(count)])  12.9 us
    ppermute x12, waiting for transfers between devices, swap(): return lax.ppermute(value, axis, [(at, at ^ step) for at in range(count)])  2.91 us
    unnamed x14, local copies, waits for them, and re-layouts  1.62 us
  transfers between devices with their start and end apart: 12, of which 3 were waited for; matrix products, arithmetic and copies ran while one was open for 0% of the time, Pallas kernels for 20%

profile of v7, /device:TPU:0, one launch (start us, length us, event | category | flops | bytes accessed | tf_op | source)
XLA Modules:
  0.0 45.3 jit_solution(11731180561781416975)
XLA Ops:
  0.6 0.0 copy-start.5
  0.6 0.9 %copy-done.5 = s32[65536]{0:T(1024)S(1)} copy-done((s32[65536]{0:T(1024)S(1)}, s32[65536]{0:T(1024)}, u32[]{:S(2)}) %copy-start.5) | copy-done | bytes 262168
  1.6 0.0 copy-start.6
  1.6 0.7 %copy-done.6 = s32[128]{0:T(128)S(1)} copy-done((s32[128]{0:T(128)S(1)}, s32[128]{0:T(128)}, u32[]{:S(2)}) %copy-start.6) | copy-done | bytes 536
  2.2 0.0 copy-start
  2.2 0.4 shard_map.86
  2.7 13.8 %all_to_all.5 = s32[16,1,128]{2,1,0:T(1,128)S(1)} all-to-all(s32[16,1,128]{2,1,0:T(1,128)S(1)} %bitcast.8), channel_id=1, replica_groups=mesh['groups'=2,'lists'=4,'sub'=4] {'lists','sub'}, dimensions={0} | all-to-all | bytes 16384 | tf_op jit(solution)/shard_map/all_to_all | solution.py:457
  16.5 0.0 copy-done
  16.5 0.0 copy-start.1
  16.5 0.0 copy-start.2
  16.5 0.0 copy-start.4
  16.5 0.0 copy-start.3
  16.5 2.3 %shard_map.87 = (bf16[4,64,256]{2,1,0:T(8,128)(2,1)S(1)}, bf16[4,64,256]{2,1,0:T(8,128)(2,1)S(1)}, s32[16,64]{1,0:T(8,128)S(1)}, f32[64,128]{1,0:T(8,128)S(1)}) custom-call(s32[16,128]{1,0:T(8,128)S(1)} %bitcast.6, bf16[16384,256]{1,0:T(8,128)(2,1)S(1)} %copy-done), custom_call_target="tpu_custom_call" | custom-call | flops 600000000 | bytes 8388608 | tf_op jit(solution)/shard_map/pallas_call | solution.py:22
  18.9 0.6 %collective-permute-start = (bf16[4,64,256]{2,1,0:T(8,128)(2,1)S(1)}, bf16[4,64,256]{2,1,0:T(8,128)(2,1)S(1)}, u32[]{:S(2)}, u32[]{:S(2)}) collective-permute-start(bf16[4,64,256]{2,1,0:T(8,128)(2,1)S(1)} %get-tuple-element.30), channel_id=1, source_target_pairs={{0,4},{4,0},{8,12},{12,8},{1,5},{5,1},{9,13},{13,9},{2,6},{6,2},{1... | collective-permute-start | bytes 393224 | tf_op jit(solution)/shard_map/ppermute | solution.py:446
  19.4 0.6 %collective-permute-start.1 = (bf16[4,64,256]{2,1,0:T(8,128)(2,1)S(1)}, bf16[4,64,256]{2,1,0:T(8,128)(2,1)S(1)}, u32[]{:S(2)}, u32[]{:S(2)}) collective-permute-start(bf16[4,64,256]{2,1,0:T(8,128)(2,1)S(1)} %get-tuple-element.31), channel_id=1, source_target_pairs={{0,8},{4,12},{8,0},{12,4},{1,9},{5,13},{9,1},{13,5},{2,10},{6,14},... | collective-permute-start | bytes 393224 | tf_op jit(solution)/shard_map/ppermute | solution.py:446
  20.0 1.5 %shard_map.88 = (bf16[4,64,256]{2,1,0:T(8,128)(2,1)S(1)}, bf16[4,64,256]{2,1,0:T(8,128)(2,1)S(1)}) custom-call(s32[16,64]{1,0:T(8,128)S(1)} %get-tuple-element.27.index_ref, f32[64,128]{1,0:T(8,128)S(1)} %get-tuple-element.28.spot_ref, bf16[16384,256]{1,0:T(8,128)(2,1)S(1)} %copy-done), custom_call_target="tpu_custom_call" | custom-call | tf_op jit(solution)/shard_map/pallas_call | solution.py:22
  21.5 0.0 copy-done.1
  21.5 0.0 copy-done.2
  21.5 0.0 copy-done.4
  21.5 0.5 %shard_map.90 = (bf16[144,256]{1,0:T(8,128)(2,1)S(1)}, bf16[144,256]{1,0:T(8,128)(2,1)S(1)}, bf16[144,256]{1,0:T(8,128)(2,1)S(1)}, bf16[144,256]{1,0:T(8,128)(2,1)S(1)}) custom-call(bf16[128,1024]{1,0:T(8,128)(2,1)S(1)} %copy-done.2, bf16[1024,1024]{1,0:T(8,128)(2,1)S(1)} %copy-done.1, s32[128,128]{1,0:T(8,128)S(1)} %copy-done.4, ...), custom_call_target="tpu_custom_call" | custom-call | tf_op jit(solution)/shard_map/pallas_call | solution.py:22
  22.0 0.1 collective-permute-start.3
  22.1 0.6 %collective-permute-start.4 = (bf16[144,256]{1,0:T(8,128)(2,1)S(1)}, bf16[144,256]{1,0:T(8,128)(2,1)S(1)}, u32[]{:S(2)}, u32[]{:S(2)}) collective-permute-start(bf16[144,256]{1,0:T(8,128)(2,1)S(1)} %get-tuple-element.37), channel_id=1, source_target_pairs={{0,2},{1,3},{2,0},{3,1},{4,6},{5,7},{6,4},{7,5},{8,10},{9,11},{10,... | collective-permute-start | bytes 221192 | tf_op jit(solution)/shard_map/ppermute | solution.py:446
  22.7 1.2 %collective-permute-start.5 = (bf16[144,256]{1,0:T(8,128)(2,1)S(1)}, bf16[144,256]{1,0:T(8,128)(2,1)S(1)}, u32[]{:S(2)}, u32[]{:S(2)}) collective-permute-start(bf16[144,256]{1,0:T(8,128)(2,1)S(1)} %get-tuple-element.38), channel_id=1, source_target_pairs={{0,3},{1,2},{2,1},{3,0},{4,7},{5,6},{6,5},{7,4},{8,11},{9,10},{10,... | collective-permute-start | bytes 221192 | tf_op jit(solution)/shard_map/ppermute | solution.py:446
  24.0 0.0 collective-permute-done.3.refs_1_
  24.0 3.3 %collective-permute-start.2 = (bf16[4,64,256]{2,1,0:T(8,128)(2,1)S(1)}, bf16[4,64,256]{2,1,0:T(8,128)(2,1)S(1)}, u32[]{:S(2)}, u32[]{:S(2)}) collective-permute-start(bf16[4,64,256]{2,1,0:T(8,128)(2,1)S(1)} %get-tuple-element.34), channel_id=1, source_target_pairs={{0,12},{4,8},{8,4},{12,0},{1,13},{5,9},{9,5},{13,1},{2,14},{6,10},... | collective-permute-start | bytes 393224 | tf_op jit(solution)/shard_map/ppermute | solution.py:446
  27.2 0.0 collective-permute-done.4.refs_2_
  27.3 0.7 %collective-permute-done.5.refs_3_ = bf16[144,256]{1,0:T(8,128)(2,1)S(1)} collective-permute-done((bf16[144,256]{1,0:T(8,128)(2,1)S(1)}, bf16[144,256]{1,0:T(8,128)(2,1)S(1)}, u32[]{:S(2)}, u32[]{:S(2)}) %collective-permute-start.5) | collective-permute-done | bytes 73760 | tf_op jit(solution)/shard_map/ppermute | solution.py:446
  27.9 0.0 copy-done.3
  27.9 1.1 %shard_map.91 = (bf16[512,256]{1,0:T(8,128)(2,1)S(1)}, f32[32,512]{1,0:T(8,128)S(1)}, f32[16,512]{1,0:T(8,128)S(1)}) custom-call(bf16[32,2048]{1,0:T(8,128)(2,1)S(1)} %copy-done.3, bf16[144,256]{1,0:T(8,128)(2,1)S(1)} %get-tuple-element.35.refs_0_, bf16[144,256]{1,0:T(8,128)(2,1)S(1)} %collective-permute-done.3.refs_1_, ...), custom_call_target="tpu_custom_call" | custom-call | tf_op jit(solution)/shard_map/pallas_call | solution.py:22
  29.1 0.0 collective-permute-done.refs_1_
  29.1 0.0 collective-permute-done.1.refs_2_
  29.1 0.5 %shard_map.89 = (f32[128,128]{1,0:T(8,128)S(1)}, bf16[512,256]{1,0:T(8,128)(2,1)S(1)}) custom-call(s32[16,128]{1,0:T(8,128)S(1)} %bitcast.7, bf16[4,64,256]{2,1,0:T(8,128)(2,1)S(1)} %get-tuple-element.29.refs_0_.after_ref, bf16[4,64,256]{2,1,0:T(8,128)(2,1)S(1)} %collective-permute-done.refs_1_, bf16[4,64,256]{2,1,0:T(8,128)(2,1)S(1)} %collective-permute-done.1.refs_2_), custom_call_target="tpu_custom_call" | custom-call | flops 3000000000 | tf_op jit(solution)/shard_map/pallas_call | solution.py:22
  29.6 2.4 %shard_map.92.after_ref.early_ref = f32[256,256]{1,0:T(8,128)S(1)} custom-call(f32[32,512]{1,0:T(8,128)S(1)} %get-tuple-element.39.codes_ref, f32[128,128]{1,0:T(8,128)S(1)} %get-tuple-element.32.slot_ref, bf16[512,256]{1,0:T(8,128)(2,1)S(1)} %get-tuple-element.33.centre_ref.part_ref, bf16[144,256]{1,0:T(8,128)(2,1)S(1)} %get-tuple-element.35.refs_0_, ...), custom_call_target="tpu_custom_call" | custom-call | flops 2000000000 | tf_op jit(solution)/shard_map/pallas_call | solution.py:22
  32.0 0.0 collective-permute-done.2.piece_ref
  32.0 0.3 shard_map.93.centre_ref
  32.3 0.1 shard_map.94
  32.4 0.6 %collective-permute-start.6 = (bf16[128,256]{1,0:T(8,128)(2,1)S(1)}, bf16[128,256]{1,0:T(8,128)(2,1)S(1)}, u32[]{:S(2)}, u32[]{:S(2)}) collective-permute-start(bf16[128,256]{1,0:T(8,128)(2,1)S(1)} %get-tuple-element.42), channel_id=1, source_target_pairs={{0,1},{1,0},{2,3},{3,2},{4,5},{5,4},{6,7},{7,6},{8,9},{9,8},{10,11... | collective-permute-start | bytes 196616 | tf_op jit(solution)/shard_map/ppermute | solution.py:446
  33.0 0.6 %collective-permute-start.7 = (bf16[128,256]{1,0:T(8,128)(2,1)S(1)}, bf16[128,256]{1,0:T(8,128)(2,1)S(1)}, u32[]{:S(2)}, u32[]{:S(2)}) collective-permute-start(bf16[128,256]{1,0:T(8,128)(2,1)S(1)} %get-tuple-element.43), channel_id=1, source_target_pairs={{0,2},{1,3},{2,0},{3,1},{4,6},{5,7},{6,4},{7,5},{8,10},{9,11},{10,... | collective-permute-start | bytes 196616 | tf_op jit(solution)/shard_map/ppermute | solution.py:446
  33.6 0.9 %collective-permute-start.8 = (bf16[128,256]{1,0:T(8,128)(2,1)S(1)}, bf16[128,256]{1,0:T(8,128)(2,1)S(1)}, u32[]{:S(2)}, u32[]{:S(2)}) collective-permute-start(bf16[128,256]{1,0:T(8,128)(2,1)S(1)} %get-tuple-element.44), channel_id=1, source_target_pairs={{0,3},{1,2},{2,1},{3,0},{4,7},{5,6},{6,5},{7,4},{8,11},{9,10},{10,... | collective-permute-start | bytes 196616 | tf_op jit(solution)/shard_map/ppermute | solution.py:446
  34.5 0.0 collective-permute-done.6.refs_4_.refs_1_
  34.5 1.6 %shard_map.95 = (bf16[144,128]{1,0:T(8,128)(2,1)S(1)}, bf16[144,128]{1,0:T(8,128)(2,1)S(1)}, bf16[144,128]{1,0:T(8,128)(2,1)S(1)}, bf16[144,128]{1,0:T(8,128)(2,1)S(1)}) custom-call(f32[32,512]{1,0:T(8,128)S(1)} %get-tuple-element.39.codes_ref, f32[128,128]{1,0:T(8,128)S(1)} %get-tuple-element.32.slot_ref, ...), custom_call_target="tpu_custom_call" | custom-call | flops 1000000000 | bytes 1000000 | tf_op jit(solution)/shard_map/pallas_call | solution.py:22
  36.0 3.2 %collective-permute-start.9 = (bf16[144,128]{1,0:T(8,128)(2,1)S(1)}, bf16[144,128]{1,0:T(8,128)(2,1)S(1)}, u32[]{:S(2)}, u32[]{:S(2)}) collective-permute-start(bf16[144,128]{1,0:T(8,128)(2,1)S(1)} %get-tuple-element.46), channel_id=1, source_target_pairs={{0,12},{4,8},{8,4},{12,0},{1,13},{5,9},{9,5},{13,1},{2,14},{6,10},... | collective-permute-start | bytes 110600 | tf_op jit(solution)/shard_map/ppermute | solution.py:446
  39.3 0.1 collective-permute-start.10
  39.4 1.1 %collective-permute-start.11 = (bf16[144,128]{1,0:T(8,128)(2,1)S(1)}, bf16[144,128]{1,0:T(8,128)(2,1)S(1)}, u32[]{:S(2)}, u32[]{:S(2)}) collective-permute-start(bf16[144,128]{1,0:T(8,128)(2,1)S(1)} %get-tuple-element.50), channel_id=1, source_target_pairs={{0,8},{4,12},{8,0},{12,4},{1,9},{5,13},{9,1},{13,5},{2,10},{6,14},... | collective-permute-start | bytes 110600 | tf_op jit(solution)/shard_map/ppermute | solution.py:446
  40.5 0.0 collective-permute-done.7.refs_2_
  40.5 0.0 collective-permute-done.8.refs_3_
  40.5 1.7 %collective-permute-done.9.refs_4_.refs_3_ = bf16[144,128]{1,0:T(8,128)(2,1)S(1)} collective-permute-done((bf16[144,128]{1,0:T(8,128)(2,1)S(1)}, bf16[144,128]{1,0:T(8,128)(2,1)S(1)}, u32[]{:S(2)}, u32[]{:S(2)}) %collective-permute-start.9) | collective-permute-done | bytes 36896 | tf_op jit(solution)/shard_map/ppermute | solution.py:446
  42.2 1.5 %shard_map.96 = (bf16[128,1024]{1,0:T(8,128)(2,1)}, f32[8,128]{1,0:T(8,128)S(1)}) custom-call(bf16[128,1024]{1,0:T(8,128)(2,1)S(1)} %copy-done.2, bf16[1024,1024]{1,0:T(8,128)(2,1)S(1)} %copy-done.1, bf16[128,256]{1,0:T(8,128)(2,1)S(1)} %get-tuple-element.41.refs_0_, bf16[128,256]{1,0:T(8,128)(2,1)S(1)} %collective-permute-done.6.refs_4_.refs_1_, ...), custom_call_target="tpu_custom_call" | custom-call | flops 1000 | bytes 1000 | tf_op jit(solution)/shard_map/pallas_call | solution.py:22
  43.7 0.0 collective-permute-done.10.refs_1_
  43.7 0.5 %collective-permute-done.11.refs_2_ = bf16[144,128]{1,0:T(8,128)(2,1)S(1)} collective-permute-done((bf16[144,128]{1,0:T(8,128)(2,1)S(1)}, bf16[144,128]{1,0:T(8,128)(2,1)S(1)}, u32[]{:S(2)}, u32[]{:S(2)}) %collective-permute-start.11) | collective-permute-done | bytes 36896 | tf_op jit(solution)/shard_map/ppermute | solution.py:446
  44.3 1.1 %shard_map.97 = f32[32,512]{1,0:T(8,128)} custom-call(bf16[32,2048]{1,0:T(8,128)(2,1)S(1)} %copy-done.3, bf16[144,128]{1,0:T(8,128)(2,1)S(1)} %get-tuple-element.48.refs_0_, bf16[144,128]{1,0:T(8,128)(2,1)S(1)} %collective-permute-done.10.refs_1_, bf16[144,128]{1,0:T(8,128)(2,1)S(1)} %collective-permute-done.11.refs_2_, ...), custom_call_target="tpu_custom_call" | custom-call | flops 100000000 | bytes 500000 | tf_op jit(solution)/shard_map/pallas_call | solution.py:22
Async XLA Ops:
  0.6 1.0 %copy-start.5 = (s32[65536]{0:T(1024)S(1)}, s32[65536]{0:T(1024)}, u32[]{:S(2)}) copy-start(s32[65536]{0:T(1024)} %param.10) | copy-start | bytes 786436
  1.6 0.7 %copy-start.6 = (s32[128]{0:T(128)S(1)}, s32[128]{0:T(128)}, u32[]{:S(2)}) copy-start(s32[128]{0:T(128)} %param.11) | copy-start | bytes 1540
  2.2 14.3 %copy-start = (bf16[16384,256]{1,0:T(8,128)(2,1)S(1)}, bf16[16384,256]{1,0:T(8,128)(2,1)}, u32[]{:S(2)}) copy-start(bf16[16384,256]{1,0:T(8,128)(2,1)} %centroids_ref.3) | copy-start | bytes 25165828
  16.5 5.0 %copy-start.1 = (bf16[1024,1024]{1,0:T(8,128)(2,1)S(1)}, bf16[1024,1024]{1,0:T(8,128)(2,1)}, u32[]{:S(2)}) copy-start(bf16[1024,1024]{1,0:T(8,128)(2,1)} %rotation_ref.3) | copy-start | bytes 6291460
  16.5 5.0 %copy-start.2 = (bf16[128,1024]{1,0:T(8,128)(2,1)S(1)}, bf16[128,1024]{1,0:T(8,128)(2,1)}, u32[]{:S(2)}) copy-start(bf16[128,1024]{1,0:T(8,128)(2,1)} %passages_ref.3) | copy-start | bytes 786436
  16.5 5.0 %copy-start.4 = (s32[128,128]{1,0:T(8,128)S(1)}, s32[128,128]{1,0:T(8,128)}, u32[]{:S(2)}) copy-start(s32[128,128]{1,0:T(8,128)} %codes_ref.1) | copy-start | bytes 196612
  16.5 11.4 %copy-start.3 = (bf16[32,2048]{1,0:T(8,128)(2,1)S(1)}, bf16[32,2048]{1,0:T(8,128)(2,1)}, u32[]{:S(2)}) copy-start(bf16[32,2048]{1,0:T(8,128)(2,1)} %codebook_ref.3) | copy-start | bytes 393220
  18.9 10.2 %collective-permute-start = (bf16[4,64,256]{2,1,0:T(8,128)(2,1)S(1)}, bf16[4,64,256]{2,1,0:T(8,128)(2,1)S(1)}, u32[]{:S(2)}, u32[]{:S(2)}) collective-permute-start(bf16[4,64,256]{2,1,0:T(8,128)(2,1)S(1)} %get-tuple-element.30), channel_id=1, source_target_pairs={{0,4},{4,0},{8,12},{12,8},{1,5},{5,1},{9,13},{13,9},{2,6},{6,2},{1... | collective-permute-start | bytes 393224 | tf_op jit(solution)/shard_map/ppermute | solution.py:446
  19.4 9.6 %collective-permute-start.1 = (bf16[4,64,256]{2,1,0:T(8,128)(2,1)S(1)}, bf16[4,64,256]{2,1,0:T(8,128)(2,1)S(1)}, u32[]{:S(2)}, u32[]{:S(2)}) collective-permute-start(bf16[4,64,256]{2,1,0:T(8,128)(2,1)S(1)} %get-tuple-element.31), channel_id=1, source_target_pairs={{0,8},{4,12},{8,0},{12,4},{1,9},{5,13},{9,1},{13,5},{2,10},{6,14},... | collective-permute-start | bytes 393224 | tf_op jit(solution)/shard_map/ppermute | solution.py:446
  22.0 1.9 %collective-permute-start.3 = (bf16[144,256]{1,0:T(8,128)(2,1)S(1)}, bf16[144,256]{1,0:T(8,128)(2,1)S(1)}, u32[]{:S(2)}, u32[]{:S(2)}) collective-permute-start(bf16[144,256]{1,0:T(8,128)(2,1)S(1)} %get-tuple-element.36), channel_id=1, source_target_pairs={{0,1},{1,0},{2,3},{3,2},{4,5},{5,4},{6,7},{7,6},{8,9},{9,8},{10,11... | collective-permute-start | bytes 221192 | tf_op jit(solution)/shard_map/ppermute | solution.py:446
  22.1 5.1 %collective-permute-start.4 = (bf16[144,256]{1,0:T(8,128)(2,1)S(1)}, bf16[144,256]{1,0:T(8,128)(2,1)S(1)}, u32[]{:S(2)}, u32[]{:S(2)}) collective-permute-start(bf16[144,256]{1,0:T(8,128)(2,1)S(1)} %get-tuple-element.37), channel_id=1, source_target_pairs={{0,2},{1,3},{2,0},{3,1},{4,6},{5,7},{6,4},{7,5},{8,10},{9,11},{10,... | collective-permute-start | bytes 221192 | tf_op jit(solution)/shard_map/ppermute | solution.py:446
  22.7 5.2 %collective-permute-start.5 = (bf16[144,256]{1,0:T(8,128)(2,1)S(1)}, bf16[144,256]{1,0:T(8,128)(2,1)S(1)}, u32[]{:S(2)}, u32[]{:S(2)}) collective-permute-start(bf16[144,256]{1,0:T(8,128)(2,1)S(1)} %get-tuple-element.38), channel_id=1, source_target_pairs={{0,3},{1,2},{2,1},{3,0},{4,7},{5,6},{6,5},{7,4},{8,11},{9,10},{10,... | collective-permute-start | bytes 221192 | tf_op jit(solution)/shard_map/ppermute | solution.py:446
  24.0 8.0 %collective-permute-start.2 = (bf16[4,64,256]{2,1,0:T(8,128)(2,1)S(1)}, bf16[4,64,256]{2,1,0:T(8,128)(2,1)S(1)}, u32[]{:S(2)}, u32[]{:S(2)}) collective-permute-start(bf16[4,64,256]{2,1,0:T(8,128)(2,1)S(1)} %get-tuple-element.34), channel_id=1, source_target_pairs={{0,12},{4,8},{8,4},{12,0},{1,13},{5,9},{9,5},{13,1},{2,14},{6,10},... | collective-permute-start | bytes 393224 | tf_op jit(solution)/shard_map/ppermute | solution.py:446
  32.4 2.1 %collective-permute-start.6 = (bf16[128,256]{1,0:T(8,128)(2,1)S(1)}, bf16[128,256]{1,0:T(8,128)(2,1)S(1)}, u32[]{:S(2)}, u32[]{:S(2)}) collective-permute-start(bf16[128,256]{1,0:T(8,128)(2,1)S(1)} %get-tuple-element.42), channel_id=1, source_target_pairs={{0,1},{1,0},{2,3},{3,2},{4,5},{5,4},{6,7},{7,6},{8,9},{9,8},{10,11... | collective-permute-start | bytes 196616 | tf_op jit(solution)/shard_map/ppermute | solution.py:446
  33.0 7.5 %collective-permute-start.7 = (bf16[128,256]{1,0:T(8,128)(2,1)S(1)}, bf16[128,256]{1,0:T(8,128)(2,1)S(1)}, u32[]{:S(2)}, u32[]{:S(2)}) collective-permute-start(bf16[128,256]{1,0:T(8,128)(2,1)S(1)} %get-tuple-element.43), channel_id=1, source_target_pairs={{0,2},{1,3},{2,0},{3,1},{4,6},{5,7},{6,4},{7,5},{8,10},{9,11},{10,... | collective-permute-start | bytes 196616 | tf_op jit(solution)/shard_map/ppermute | solution.py:446
  33.6 6.9 %collective-permute-start.8 = (bf16[128,256]{1,0:T(8,128)(2,1)S(1)}, bf16[128,256]{1,0:T(8,128)(2,1)S(1)}, u32[]{:S(2)}, u32[]{:S(2)}) collective-permute-start(bf16[128,256]{1,0:T(8,128)(2,1)S(1)} %get-tuple-element.44), channel_id=1, source_target_pairs={{0,3},{1,2},{2,1},{3,0},{4,7},{5,6},{6,5},{7,4},{8,11},{9,10},{10,... | collective-permute-start | bytes 196616 | tf_op jit(solution)/shard_map/ppermute | solution.py:446
  36.0 6.1 %collective-permute-start.9 = (bf16[144,128]{1,0:T(8,128)(2,1)S(1)}, bf16[144,128]{1,0:T(8,128)(2,1)S(1)}, u32[]{:S(2)}, u32[]{:S(2)}) collective-permute-start(bf16[144,128]{1,0:T(8,128)(2,1)S(1)} %get-tuple-element.46), channel_id=1, source_target_pairs={{0,12},{4,8},{8,4},{12,0},{1,13},{5,9},{9,5},{13,1},{2,14},{6,10},... | collective-permute-start | bytes 110600 | tf_op jit(solution)/shard_map/ppermute | solution.py:446
  39.3 4.5 %collective-permute-start.10 = (bf16[144,128]{1,0:T(8,128)(2,1)S(1)}, bf16[144,128]{1,0:T(8,128)(2,1)S(1)}, u32[]{:S(2)}, u32[]{:S(2)}) collective-permute-start(bf16[144,128]{1,0:T(8,128)(2,1)S(1)} %get-tuple-element.49), channel_id=1, source_target_pairs={{0,4},{4,0},{8,12},{12,8},{1,5},{5,1},{9,13},{13,9},{2,6},{6,2},{1... | collective-permute-start | bytes 110600 | tf_op jit(solution)/shard_map/ppermute | solution.py:446
  39.4 4.9 %collective-permute-start.11 = (bf16[144,128]{1,0:T(8,128)(2,1)S(1)}, bf16[144,128]{1,0:T(8,128)(2,1)S(1)}, u32[]{:S(2)}, u32[]{:S(2)}) collective-permute-start(bf16[144,128]{1,0:T(8,128)(2,1)S(1)} %get-tuple-element.50), channel_id=1, source_target_pairs={{0,8},{4,12},{8,0},{12,4},{1,9},{5,13},{9,1},{13,5},{2,10},{6,14},... | collective-permute-start | bytes 110600 | tf_op jit(solution)/shard_map/ppermute | solution.py:446

commit v8 on v7

--- a/solution.py
+++ b/solution.py
@@ -17,16 +17,16 @@
 DIRECT = 4
 
 
-def call(kernel, out_shape, flops, nbytes, *args, scratch=(), loose=0, limit=VMEM_LIMIT):
+def call(kernel, out_shape, flops, nbytes, *args, scratch=(), loose=0, space=pl.ANY):
     whole = lambda: pl.BlockSpec(memory_space=pltpu.VMEM)
     return pl.pallas_call(
         kernel,
         out_shape=out_shape,
         in_specs=[whole() for _ in args[: len(args) - loose]]
-        + [pl.BlockSpec(memory_space=pl.ANY)] * loose,
+        + [pl.BlockSpec(memory_space=space)] * loose,
         out_specs=jax.tree.map(lambda _: whole(), out_shape),
         scratch_shapes=list(scratch),
-        compiler_params=pltpu.CompilerParams(vmem_limit_bytes=limit),
+        compiler_params=pltpu.CompilerParams(vmem_limit_bytes=VMEM_LIMIT),
         cost_estimate=pl.CostEstimate(flops=flops, bytes_accessed=nbytes, transcendentals=0),
     )(*args)
 
@@ -152,11 +152,7 @@
         fetch_blocks(first, spot_ref, scalar_ref, centroids_ref, out)
 
 
-def fetch_rest_kernel(steps, index_ref, spot_ref, centroids_ref, *refs):
-    outs, (scalar_ref, sem) = refs[:-2], refs[-2:]
-    move = pltpu.make_async_copy(index_ref, scalar_ref, sem)
-    move.start()
-    move.wait()
+def fetch_rest_kernel(steps, spot_ref, centroids_ref, scalar_ref, *outs):
     for step, out in zip(steps, outs):
         fetch_blocks(step * out.shape[0], spot_ref, scalar_ref, centroids_ref, out)
 
@@ -503,10 +499,11 @@
             [shape((subs, cap, width), BF16)] * len(late),
             0,
             0,
-            index,
             spot,
             centroids,
-            scratch=scalars,
+            index,
+            loose=1,
+            space=pltpu.SMEM,
         )
         fetched = rest[-1]
         pieces = exchange([fetched] + list(pieces) + list(rest[:-1]), "lists")

time: 45.5 us -> 45.5 us (level)
  no operation moved by 1% of the time
where the time goes in v8:
time: 45.5 us; the launch traced here: 45.3 us
  blocking collectives  13.8 us (30%)
  Pallas kernels  13.2 us (29%)
  starting transfers between devices  12.9 us (28%)
  waiting for transfers between devices  2.92 us (6%)
  local copies, waits for them, and re-layouts  1.62 us (4%)
  between operations  0.77 us (2%)
    all_to_all x1, blocking collectives, all_swap(): return lax.all_to_all(value, axis, split_axis=0, concat_axis=0, tiled=True)  13.8 us
    pallas_call x12, Pallas kernels, call(): pl.pallas_call(kernel, out_shape=out_shape, in_specs=[whole() for _ in ar...  13.2 us
    ppermute x12, starting transfers between devices, swap(): return lax.ppermute(value, axis, [(at, at ^ step) for at in range(count)])  12.9 us
    ppermute x12, waiting for transfers between devices, swap(): return lax.ppermute(value, axis, [(at, at ^ step) for at in range(count)])  2.92 us
    unnamed x14, local copies, waits for them, and re-layouts  1.62 us
  transfers between devices with their start and end apart: 12, of which 3 were waited for; matrix products, arithmetic and copies ran while one was open for 0% of the time, Pallas kernels for 20%

profile of v8, /device:TPU:0, one launch (start us, length us, event | category | flops | bytes accessed | tf_op | source)
XLA Modules:
  0.0 45.3 jit_solution(2275436398475888420)
XLA Ops:
  0.6 0.0 copy-start.5
  0.6 0.9 %copy-done.5 = s32[65536]{0:T(1024)S(1)} copy-done((s32[65536]{0:T(1024)S(1)}, s32[65536]{0:T(1024)}, u32[]{:S(2)}) %copy-start.5) | copy-done | bytes 262168
  1.6 0.0 copy-start.6
  1.6 0.7 %copy-done.6 = s32[128]{0:T(128)S(1)} copy-done((s32[128]{0:T(128)S(1)}, s32[128]{0:T(128)}, u32[]{:S(2)}) %copy-start.6) | copy-done | bytes 536
  2.2 0.0 copy-start
  2.2 0.4 shard_map.86
  2.7 13.8 %all_to_all.5 = s32[16,1,128]{2,1,0:T(1,128)S(1)} all-to-all(s32[16,1,128]{2,1,0:T(1,128)S(1)} %bitcast.8), channel_id=1, replica_groups=mesh['groups'=2,'lists'=4,'sub'=4] {'lists','sub'}, dimensions={0} | all-to-all | bytes 16384 | tf_op jit(solution)/shard_map/all_to_all | solution.py:453
  16.5 0.0 copy-done
  16.5 0.0 copy-start.1
  16.5 0.0 copy-start.2
  16.5 0.0 copy-start.4
  16.5 0.0 copy-start.3
  16.5 2.3 %shard_map.87 = (bf16[4,64,256]{2,1,0:T(8,128)(2,1)S(1)}, bf16[4,64,256]{2,1,0:T(8,128)(2,1)S(1)}, s32[16,64]{1,0:T(8,128)S(1)}, f32[64,128]{1,0:T(8,128)S(1)}) custom-call(s32[16,128]{1,0:T(8,128)S(1)} %bitcast.6, bf16[16384,256]{1,0:T(8,128)(2,1)S(1)} %copy-done), custom_call_target="tpu_custom_call" | custom-call | flops 600000000 | bytes 8388608 | tf_op jit(solution)/shard_map/pallas_call | solution.py:22
  18.9 0.6 %collective-permute-start = (bf16[4,64,256]{2,1,0:T(8,128)(2,1)S(1)}, bf16[4,64,256]{2,1,0:T(8,128)(2,1)S(1)}, u32[]{:S(2)}, u32[]{:S(2)}) collective-permute-start(bf16[4,64,256]{2,1,0:T(8,128)(2,1)S(1)} %get-tuple-element.30), channel_id=1, source_target_pairs={{0,4},{4,0},{8,12},{12,8},{1,5},{5,1},{9,13},{13,9},{2,6},{6,2},{1... | collective-permute-start | bytes 393224 | tf_op jit(solution)/shard_map/ppermute | solution.py:442
  19.4 0.6 %collective-permute-start.1 = (bf16[4,64,256]{2,1,0:T(8,128)(2,1)S(1)}, bf16[4,64,256]{2,1,0:T(8,128)(2,1)S(1)}, u32[]{:S(2)}, u32[]{:S(2)}) collective-permute-start(bf16[4,64,256]{2,1,0:T(8,128)(2,1)S(1)} %get-tuple-element.31), channel_id=1, source_target_pairs={{0,8},{4,12},{8,0},{12,4},{1,9},{5,13},{9,1},{13,5},{2,10},{6,14},... | collective-permute-start | bytes 393224 | tf_op jit(solution)/shard_map/ppermute | solution.py:442
  20.0 1.4 %shard_map.88 = (bf16[4,64,256]{2,1,0:T(8,128)(2,1)S(1)}, bf16[4,64,256]{2,1,0:T(8,128)(2,1)S(1)}) custom-call(f32[64,128]{1,0:T(8,128)S(1)} %get-tuple-element.27.spot_ref, bf16[16384,256]{1,0:T(8,128)(2,1)S(1)} %copy-done, s32[16,64]{1,0:T(8,128)S(1)} %get-tuple-element.28.scalar_ref), custom_call_target="tpu_custom_call" | custom-call | tf_op jit(solution)/shard_map/pallas_call | solution.py:22
  21.5 0.0 copy-done.1
  21.5 0.0 copy-done.2
  21.5 0.0 copy-done.4
  21.5 0.5 %shard_map.90 = (bf16[144,256]{1,0:T(8,128)(2,1)S(1)}, bf16[144,256]{1,0:T(8,128)(2,1)S(1)}, bf16[144,256]{1,0:T(8,128)(2,1)S(1)}, bf16[144,256]{1,0:T(8,128)(2,1)S(1)}) custom-call(bf16[128,1024]{1,0:T(8,128)(2,1)S(1)} %copy-done.2, bf16[1024,1024]{1,0:T(8,128)(2,1)S(1)} %copy-done.1, s32[128,128]{1,0:T(8,128)S(1)} %copy-done.4, ...), custom_call_target="tpu_custom_call" | custom-call | tf_op jit(solution)/shard_map/pallas_call | solution.py:22
  22.0 0.1 collective-permute-start.3
  22.1 0.6 %collective-permute-start.4 = (bf16[144,256]{1,0:T(8,128)(2,1)S(1)}, bf16[144,256]{1,0:T(8,128)(2,1)S(1)}, u32[]{:S(2)}, u32[]{:S(2)}) collective-permute-start(bf16[144,256]{1,0:T(8,128)(2,1)S(1)} %get-tuple-element.37), channel_id=1, source_target_pairs={{0,2},{1,3},{2,0},{3,1},{4,6},{5,7},{6,4},{7,5},{8,10},{9,11},{10,... | collective-permute-start | bytes 221192 | tf_op jit(solution)/shard_map/ppermute | solution.py:442
  22.7 1.2 %collective-permute-start.5 = (bf16[144,256]{1,0:T(8,128)(2,1)S(1)}, bf16[144,256]{1,0:T(8,128)(2,1)S(1)}, u32[]{:S(2)}, u32[]{:S(2)}) collective-permute-start(bf16[144,256]{1,0:T(8,128)(2,1)S(1)} %get-tuple-element.38), channel_id=1, source_target_pairs={{0,3},{1,2},{2,1},{3,0},{4,7},{5,6},{6,5},{7,4},{8,11},{9,10},{10,... | collective-permute-start | bytes 221192 | tf_op jit(solution)/shard_map/ppermute | solution.py:442
  23.9 0.0 collective-permute-done.3.refs_1_
  23.9 3.3 %collective-permute-start.2 = (bf16[4,64,256]{2,1,0:T(8,128)(2,1)S(1)}, bf16[4,64,256]{2,1,0:T(8,128)(2,1)S(1)}, u32[]{:S(2)}, u32[]{:S(2)}) collective-permute-start(bf16[4,64,256]{2,1,0:T(8,128)(2,1)S(1)} %get-tuple-element.34), channel_id=1, source_target_pairs={{0,12},{4,8},{8,4},{12,0},{1,13},{5,9},{9,5},{13,1},{2,14},{6,10},... | collective-permute-start | bytes 393224 | tf_op jit(solution)/shard_map/ppermute | solution.py:442
  27.2 0.0 collective-permute-done.4.refs_2_
  27.2 0.7 %collective-permute-done.5.refs_3_ = bf16[144,256]{1,0:T(8,128)(2,1)S(1)} collective-permute-done((bf16[144,256]{1,0:T(8,128)(2,1)S(1)}, bf16[144,256]{1,0:T(8,128)(2,1)S(1)}, u32[]{:S(2)}, u32[]{:S(2)}) %collective-permute-start.5) | collective-permute-done | bytes 73760 | tf_op jit(solution)/shard_map/ppermute | solution.py:442
  27.9 0.0 copy-done.3
  27.9 1.1 %shard_map.91 = (bf16[512,256]{1,0:T(8,128)(2,1)S(1)}, f32[32,512]{1,0:T(8,128)S(1)}, f32[16,512]{1,0:T(8,128)S(1)}) custom-call(bf16[32,2048]{1,0:T(8,128)(2,1)S(1)} %copy-done.3, bf16[144,256]{1,0:T(8,128)(2,1)S(1)} %get-tuple-element.35.refs_0_, bf16[144,256]{1,0:T(8,128)(2,1)S(1)} %collective-permute-done.3.refs_1_, ...), custom_call_target="tpu_custom_call" | custom-call | tf_op jit(solution)/shard_map/pallas_call | solution.py:22
  29.0 0.0 collective-permute-done.refs_1_
  29.0 0.0 collective-permute-done.1.refs_2_
  29.0 0.5 %shard_map.89 = (f32[128,128]{1,0:T(8,128)S(1)}, bf16[512,256]{1,0:T(8,128)(2,1)S(1)}) custom-call(s32[16,128]{1,0:T(8,128)S(1)} %bitcast.7, bf16[4,64,256]{2,1,0:T(8,128)(2,1)S(1)} %get-tuple-element.29.refs_0_.after_ref, bf16[4,64,256]{2,1,0:T(8,128)(2,1)S(1)} %collective-permute-done.refs_1_, bf16[4,64,256]{2,1,0:T(8,128)(2,1)S(1)} %collective-permute-done.1.refs_2_), custom_call_target="tpu_custom_call" | custom-call | flops 3000000000 | tf_op jit(solution)/shard_map/pallas_call | solution.py:22
  29.6 2.4 %shard_map.92.after_ref.early_ref = f32[256,256]{1,0:T(8,128)S(1)} custom-call(f32[32,512]{1,0:T(8,128)S(1)} %get-tuple-element.39.codes_ref, f32[128,128]{1,0:T(8,128)S(1)} %get-tuple-element.32.slot_ref, bf16[512,256]{1,0:T(8,128)(2,1)S(1)} %get-tuple-element.33.centre_ref.part_ref, bf16[144,256]{1,0:T(8,128)(2,1)S(1)} %get-tuple-element.35.refs_0_, ...), custom_call_target="tpu_custom_call" | custom-call | flops 2000000000 | tf_op jit(solution)/shard_map/pallas_call | solution.py:22
  32.0 0.0 collective-permute-done.2.piece_ref
  32.0 0.3 shard_map.93.centre_ref
  32.3 0.1 shard_map.94
  32.3 0.6 %collective-permute-start.6 = (bf16[128,256]{1,0:T(8,128)(2,1)S(1)}, bf16[128,256]{1,0:T(8,128)(2,1)S(1)}, u32[]{:S(2)}, u32[]{:S(2)}) collective-permute-start(bf16[128,256]{1,0:T(8,128)(2,1)S(1)} %get-tuple-element.42), channel_id=1, source_target_pairs={{0,1},{1,0},{2,3},{3,2},{4,5},{5,4},{6,7},{7,6},{8,9},{9,8},{10,11... | collective-permute-start | bytes 196616 | tf_op jit(solution)/shard_map/ppermute | solution.py:442
  33.0 0.6 %collective-permute-start.7 = (bf16[128,256]{1,0:T(8,128)(2,1)S(1)}, bf16[128,256]{1,0:T(8,128)(2,1)S(1)}, u32[]{:S(2)}, u32[]{:S(2)}) collective-permute-start(bf16[128,256]{1,0:T(8,128)(2,1)S(1)} %get-tuple-element.43), channel_id=1, source_target_pairs={{0,2},{1,3},{2,0},{3,1},{4,6},{5,7},{6,4},{7,5},{8,10},{9,11},{10,... | collective-permute-start | bytes 196616 | tf_op jit(solution)/shard_map/ppermute | solution.py:442
  33.5 0.9 %collective-permute-start.8 = (bf16[128,256]{1,0:T(8,128)(2,1)S(1)}, bf16[128,256]{1,0:T(8,128)(2,1)S(1)}, u32[]{:S(2)}, u32[]{:S(2)}) collective-permute-start(bf16[128,256]{1,0:T(8,128)(2,1)S(1)} %get-tuple-element.44), channel_id=1, source_target_pairs={{0,3},{1,2},{2,1},{3,0},{4,7},{5,6},{6,5},{7,4},{8,11},{9,10},{10,... | collective-permute-start | bytes 196616 | tf_op jit(solution)/shard_map/ppermute | solution.py:442
  34.4 0.0 collective-permute-done.6.refs_4_.refs_1_
  34.4 1.6 %shard_map.95 = (bf16[144,128]{1,0:T(8,128)(2,1)S(1)}, bf16[144,128]{1,0:T(8,128)(2,1)S(1)}, bf16[144,128]{1,0:T(8,128)(2,1)S(1)}, bf16[144,128]{1,0:T(8,128)(2,1)S(1)}) custom-call(f32[32,512]{1,0:T(8,128)S(1)} %get-tuple-element.39.codes_ref, f32[128,128]{1,0:T(8,128)S(1)} %get-tuple-element.32.slot_ref, ...), custom_call_target="tpu_custom_call" | custom-call | flops 1000000000 | bytes 1000000 | tf_op jit(solution)/shard_map/pallas_call | solution.py:22
  36.0 3.2 %collective-permute-start.9 = (bf16[144,128]{1,0:T(8,128)(2,1)S(1)}, bf16[144,128]{1,0:T(8,128)(2,1)S(1)}, u32[]{:S(2)}, u32[]{:S(2)}) collective-permute-start(bf16[144,128]{1,0:T(8,128)(2,1)S(1)} %get-tuple-element.46), channel_id=1, source_target_pairs={{0,12},{4,8},{8,4},{12,0},{1,13},{5,9},{9,5},{13,1},{2,14},{6,10},... | collective-permute-start | bytes 110600 | tf_op jit(solution)/shard_map/ppermute | solution.py:442
  39.2 0.1 collective-permute-start.10
  39.3 1.1 %collective-permute-start.11 = (bf16[144,128]{1,0:T(8,128)(2,1)S(1)}, bf16[144,128]{1,0:T(8,128)(2,1)S(1)}, u32[]{:S(2)}, u32[]{:S(2)}) collective-permute-start(bf16[144,128]{1,0:T(8,128)(2,1)S(1)} %get-tuple-element.50), channel_id=1, source_target_pairs={{0,8},{4,12},{8,0},{12,4},{1,9},{5,13},{9,1},{13,5},{2,10},{6,14},... | collective-permute-start | bytes 110600 | tf_op jit(solution)/shard_map/ppermute | solution.py:442
  40.5 0.0 collective-permute-done.7.refs_2_
  40.5 0.0 collective-permute-done.8.refs_3_
  40.5 1.6 %collective-permute-done.9.refs_4_.refs_3_ = bf16[144,128]{1,0:T(8,128)(2,1)S(1)} collective-permute-done((bf16[144,128]{1,0:T(8,128)(2,1)S(1)}, bf16[144,128]{1,0:T(8,128)(2,1)S(1)}, u32[]{:S(2)}, u32[]{:S(2)}) %collective-permute-start.9) | collective-permute-done | bytes 36896 | tf_op jit(solution)/shard_map/ppermute | solution.py:442
  42.1 1.5 %shard_map.96 = (bf16[128,1024]{1,0:T(8,128)(2,1)}, f32[8,128]{1,0:T(8,128)S(1)}) custom-call(bf16[128,1024]{1,0:T(8,128)(2,1)S(1)} %copy-done.2, bf16[1024,1024]{1,0:T(8,128)(2,1)S(1)} %copy-done.1, bf16[128,256]{1,0:T(8,128)(2,1)S(1)} %get-tuple-element.41.refs_0_, bf16[128,256]{1,0:T(8,128)(2,1)S(1)} %collective-permute-done.6.refs_4_.refs_1_, ...), custom_call_target="tpu_custom_call" | custom-call | flops 1000 | bytes 1000 | tf_op jit(solution)/shard_map/pallas_call | solution.py:22
  43.6 0.0 collective-permute-done.10.refs_1_
  43.6 0.6 %collective-permute-done.11.refs_2_ = bf16[144,128]{1,0:T(8,128)(2,1)S(1)} collective-permute-done((bf16[144,128]{1,0:T(8,128)(2,1)S(1)}, bf16[144,128]{1,0:T(8,128)(2,1)S(1)}, u32[]{:S(2)}, u32[]{:S(2)}) %collective-permute-start.11) | collective-permute-done | bytes 36896 | tf_op jit(solution)/shard_map/ppermute | solution.py:442
  44.2 1.1 %shard_map.97 = f32[32,512]{1,0:T(8,128)} custom-call(bf16[32,2048]{1,0:T(8,128)(2,1)S(1)} %copy-done.3, bf16[144,128]{1,0:T(8,128)(2,1)S(1)} %get-tuple-element.48.refs_0_, bf16[144,128]{1,0:T(8,128)(2,1)S(1)} %collective-permute-done.10.refs_1_, bf16[144,128]{1,0:T(8,128)(2,1)S(1)} %collective-permute-done.11.refs_2_, ...), custom_call_target="tpu_custom_call" | custom-call | flops 100000000 | bytes 500000 | tf_op jit(solution)/shard_map/pallas_call | solution.py:22
Async XLA Ops:
  0.6 1.0 %copy-start.5 = (s32[65536]{0:T(1024)S(1)}, s32[65536]{0:T(1024)}, u32[]{:S(2)}) copy-start(s32[65536]{0:T(1024)} %param.10) | copy-start | bytes 786436
  1.6 0.7 %copy-start.6 = (s32[128]{0:T(128)S(1)}, s32[128]{0:T(128)}, u32[]{:S(2)}) copy-start(s32[128]{0:T(128)} %param.11) | copy-start | bytes 1540
  2.2 14.3 %copy-start = (bf16[16384,256]{1,0:T(8,128)(2,1)S(1)}, bf16[16384,256]{1,0:T(8,128)(2,1)}, u32[]{:S(2)}) copy-start(bf16[16384,256]{1,0:T(8,128)(2,1)} %centroids_ref.3) | copy-start | bytes 25165828
  16.5 5.0 %copy-start.1 = (bf16[1024,1024]{1,0:T(8,128)(2,1)S(1)}, bf16[1024,1024]{1,0:T(8,128)(2,1)}, u32[]{:S(2)}) copy-start(bf16[1024,1024]{1,0:T(8,128)(2,1)} %rotation_ref.3) | copy-start | bytes 6291460
  16.5 5.0 %copy-start.2 = (bf16[128,1024]{1,0:T(8,128)(2,1)S(1)}, bf16[128,1024]{1,0:T(8,128)(2,1)}, u32[]{:S(2)}) copy-start(bf16[128,1024]{1,0:T(8,128)(2,1)} %passages_ref.3) | copy-start | bytes 786436
  16.5 5.0 %copy-start.4 = (s32[128,128]{1,0:T(8,128)S(1)}, s32[128,128]{1,0:T(8,128)}, u32[]{:S(2)}) copy-start(s32[128,128]{1,0:T(8,128)} %codes_ref.1) | copy-start | bytes 196612
  16.5 11.4 %copy-start.3 = (bf16[32,2048]{1,0:T(8,128)(2,1)S(1)}, bf16[32,2048]{1,0:T(8,128)(2,1)}, u32[]{:S(2)}) copy-start(bf16[32,2048]{1,0:T(8,128)(2,1)} %codebook_ref.3) | copy-start | bytes 393220
  18.9 10.2 %collective-permute-start = (bf16[4,64,256]{2,1,0:T(8,128)(2,1)S(1)}, bf16[4,64,256]{2,1,0:T(8,128)(2,1)S(1)}, u32[]{:S(2)}, u32[]{:S(2)}) collective-permute-start(bf16[4,64,256]{2,1,0:T(8,128)(2,1)S(1)} %get-tuple-element.30), channel_id=1, source_target_pairs={{0,4},{4,0},{8,12},{12,8},{1,5},{5,1},{9,13},{13,9},{2,6},{6,2},{1... | collective-permute-start | bytes 393224 | tf_op jit(solution)/shard_map/ppermute | solution.py:442
  19.4 9.6 %collective-permute-start.1 = (bf16[4,64,256]{2,1,0:T(8,128)(2,1)S(1)}, bf16[4,64,256]{2,1,0:T(8,128)(2,1)S(1)}, u32[]{:S(2)}, u32[]{:S(2)}) collective-permute-start(bf16[4,64,256]{2,1,0:T(8,128)(2,1)S(1)} %get-tuple-element.31), channel_id=1, source_target_pairs={{0,8},{4,12},{8,0},{12,4},{1,9},{5,13},{9,1},{13,5},{2,10},{6,14},... | collective-permute-start | bytes 393224 | tf_op jit(solution)/shard_map/ppermute | solution.py:442
  22.0 1.9 %collective-permute-start.3 = (bf16[144,256]{1,0:T(8,128)(2,1)S(1)}, bf16[144,256]{1,0:T(8,128)(2,1)S(1)}, u32[]{:S(2)}, u32[]{:S(2)}) collective-permute-start(bf16[144,256]{1,0:T(8,128)(2,1)S(1)} %get-tuple-element.36), channel_id=1, source_target_pairs={{0,1},{1,0},{2,3},{3,2},{4,5},{5,4},{6,7},{7,6},{8,9},{9,8},{10,11... | collective-permute-start | bytes 221192 | tf_op jit(solution)/shard_map/ppermute | solution.py:442
  22.1 5.1 %collective-permute-start.4 = (bf16[144,256]{1,0:T(8,128)(2,1)S(1)}, bf16[144,256]{1,0:T(8,128)(2,1)S(1)}, u32[]{:S(2)}, u32[]{:S(2)}) collective-permute-start(bf16[144,256]{1,0:T(8,128)(2,1)S(1)} %get-tuple-element.37), channel_id=1, source_target_pairs={{0,2},{1,3},{2,0},{3,1},{4,6},{5,7},{6,4},{7,5},{8,10},{9,11},{10,... | collective-permute-start | bytes 221192 | tf_op jit(solution)/shard_map/ppermute | solution.py:442
  22.7 5.2 %collective-permute-start.5 = (bf16[144,256]{1,0:T(8,128)(2,1)S(1)}, bf16[144,256]{1,0:T(8,128)(2,1)S(1)}, u32[]{:S(2)}, u32[]{:S(2)}) collective-permute-start(bf16[144,256]{1,0:T(8,128)(2,1)S(1)} %get-tuple-element.38), channel_id=1, source_target_pairs={{0,3},{1,2},{2,1},{3,0},{4,7},{5,6},{6,5},{7,4},{8,11},{9,10},{10,... | collective-permute-start | bytes 221192 | tf_op jit(solution)/shard_map/ppermute | solution.py:442
  23.9 8.0 %collective-permute-start.2 = (bf16[4,64,256]{2,1,0:T(8,128)(2,1)S(1)}, bf16[4,64,256]{2,1,0:T(8,128)(2,1)S(1)}, u32[]{:S(2)}, u32[]{:S(2)}) collective-permute-start(bf16[4,64,256]{2,1,0:T(8,128)(2,1)S(1)} %get-tuple-element.34), channel_id=1, source_target_pairs={{0,12},{4,8},{8,4},{12,0},{1,13},{5,9},{9,5},{13,1},{2,14},{6,10},... | collective-permute-start | bytes 393224 | tf_op jit(solution)/shard_map/ppermute | solution.py:442
  32.3 2.1 %collective-permute-start.6 = (bf16[128,256]{1,0:T(8,128)(2,1)S(1)}, bf16[128,256]{1,0:T(8,128)(2,1)S(1)}, u32[]{:S(2)}, u32[]{:S(2)}) collective-permute-start(bf16[128,256]{1,0:T(8,128)(2,1)S(1)} %get-tuple-element.42), channel_id=1, source_target_pairs={{0,1},{1,0},{2,3},{3,2},{4,5},{5,4},{6,7},{7,6},{8,9},{9,8},{10,11... | collective-permute-start | bytes 196616 | tf_op jit(solution)/shard_map/ppermute | solution.py:442
  33.0 7.5 %collective-permute-start.7 = (bf16[128,256]{1,0:T(8,128)(2,1)S(1)}, bf16[128,256]{1,0:T(8,128)(2,1)S(1)}, u32[]{:S(2)}, u32[]{:S(2)}) collective-permute-start(bf16[128,256]{1,0:T(8,128)(2,1)S(1)} %get-tuple-element.43), channel_id=1, source_target_pairs={{0,2},{1,3},{2,0},{3,1},{4,6},{5,7},{6,4},{7,5},{8,10},{9,11},{10,... | collective-permute-start | bytes 196616 | tf_op jit(solution)/shard_map/ppermute | solution.py:442
  33.5 6.9 %collective-permute-start.8 = (bf16[128,256]{1,0:T(8,128)(2,1)S(1)}, bf16[128,256]{1,0:T(8,128)(2,1)S(1)}, u32[]{:S(2)}, u32[]{:S(2)}) collective-permute-start(bf16[128,256]{1,0:T(8,128)(2,1)S(1)} %get-tuple-element.44), channel_id=1, source_target_pairs={{0,3},{1,2},{2,1},{3,0},{4,7},{5,6},{6,5},{7,4},{8,11},{9,10},{10,... | collective-permute-start | bytes 196616 | tf_op jit(solution)/shard_map/ppermute | solution.py:442
  36.0 6.1 %collective-permute-start.9 = (bf16[144,128]{1,0:T(8,128)(2,1)S(1)}, bf16[144,128]{1,0:T(8,128)(2,1)S(1)}, u32[]{:S(2)}, u32[]{:S(2)}) collective-permute-start(bf16[144,128]{1,0:T(8,128)(2,1)S(1)} %get-tuple-element.46), channel_id=1, source_target_pairs={{0,12},{4,8},{8,4},{12,0},{1,13},{5,9},{9,5},{13,1},{2,14},{6,10},... | collective-permute-start | bytes 110600 | tf_op jit(solution)/shard_map/ppermute | solution.py:442
  39.2 4.4 %collective-permute-start.10 = (bf16[144,128]{1,0:T(8,128)(2,1)S(1)}, bf16[144,128]{1,0:T(8,128)(2,1)S(1)}, u32[]{:S(2)}, u32[]{:S(2)}) collective-permute-start(bf16[144,128]{1,0:T(8,128)(2,1)S(1)} %get-tuple-element.49), channel_id=1, source_target_pairs={{0,4},{4,0},{8,12},{12,8},{1,5},{5,1},{9,13},{13,9},{2,6},{6,2},{1... | collective-permute-start | bytes 110600 | tf_op jit(solution)/shard_map/ppermute | solution.py:442
  39.3 4.9 %collective-permute-start.11 = (bf16[144,128]{1,0:T(8,128)(2,1)S(1)}, bf16[144,128]{1,0:T(8,128)(2,1)S(1)}, u32[]{:S(2)}, u32[]{:S(2)}) collective-permute-start(bf16[144,128]{1,0:T(8,128)(2,1)S(1)} %get-tuple-element.50), channel_id=1, source_target_pairs={{0,8},{4,12},{8,0},{12,4},{1,9},{5,13},{9,1},{13,5},{2,10},{6,14},... | collective-permute-start | bytes 110600 | tf_op jit(solution)/shard_map/ppermute | solution.py:442

commit v9 on v8

--- a/solution.py
+++ b/solution.py
@@ -299,8 +299,23 @@
 
 
 def early_sums_kernel(limit, codes_ref, slot_ref, centre_ref, *refs):
-    messages, out_ref = refs[:-1], refs[-1]
+    messages, (out_ref, rotated_ref, used_ref, picks_ref) = refs[:-4], refs[-4:]
     rows = slot_ref.shape[0]
+    cap = rotated_ref.shape[0] // len(messages)
+    column = limit + lax.broadcasted_iota(jnp.int32, (rows, cap), 1).astype(F32)
+    picks = []
+    for at, message in enumerate(messages):
+        chosen = (column == slot_ref[:, at : at + 1]).astype(F32)
+        turned = jnp.transpose(chosen)
+        span = slice(at * cap, (at + 1) * cap)
+        used = jnp.sum(turned, axis=1, keepdims=True)
+        used_ref[span, :] = jnp.broadcast_to(used, (cap, 128))
+        rotated_ref[span, :] = jnp.dot(
+            turned.astype(BF16), message[:rows, :], preferred_element_type=F32
+        )
+        own = codes_ref[:, at * rows : (at + 1) * rows].astype(BF16)
+        picks.append(jnp.dot(own, chosen.astype(BF16), preferred_element_type=F32))
+    picks_ref[...] = jnp.concatenate(picks, axis=1)
     residual = []
     for at, message in enumerate(messages):
         centre = centre_ref[at * rows : (at + 1) * rows, :].astype(F32)
@@ -310,23 +325,16 @@
     out_ref[...] = add_words(total, codes_ref[...], jnp.concatenate(residual, axis=0))
 
 
-def late_sums_kernel(limit, codes_ref, slot_ref, piece_ref, early_ref, tally_ref, *refs):
-    messages, outs, total_ref = refs[: piece_ref.shape[0]], refs[piece_ref.shape[0] + 1 : -1], refs[-1]
-    rows = slot_ref.shape[0]
+def late_sums_kernel(piece_ref, early_ref, rotated_ref, used_ref, picks_ref, tally_ref, *refs):
+    outs, total_ref = refs[1:-1], refs[-1]
     subs, cap, width = piece_ref.shape
-    column = limit + lax.broadcasted_iota(jnp.int32, (rows, cap), 1).astype(F32)
-    residual, codes = [], []
-    for at, message in enumerate(messages):
-        chosen = (column == slot_ref[:, at : at + 1]).astype(F32)
-        turned = jnp.transpose(chosen)
-        used = jnp.sum(turned, axis=1, keepdims=True) > 0.0
-        rotated = jnp.dot(turned.astype(BF16), message[:rows, :], preferred_element_type=F32)
-        value = rotated - piece_ref[at].astype(F32)
-        residual.append(jnp.where(used, value, 0.0).astype(BF16))
-        own = codes_ref[:, at * rows : (at + 1) * rows].astype(BF16)
-        codes.append(jnp.dot(own, chosen.astype(BF16), preferred_element_type=F32))
+    residual = []
+    for at in range(subs):
+        span = slice(at * cap, (at + 1) * cap)
+        value = rotated_ref[span, :] - piece_ref[at].astype(F32)
+        residual.append(jnp.where(used_ref[span, :1] > 0.0, value, 0.0).astype(BF16))
     residual = jnp.concatenate(residual, axis=0)
-    total_ref[...] = add_words(early_ref[...], jnp.concatenate(codes, axis=1), residual)
+    total_ref[...] = add_words(early_ref[...], picks_ref[...], residual)
     send_sums(True, total_ref, tally_ref, outs)
 
 
@@ -554,9 +562,14 @@
     )
     centre = part
     if direct:
-        early_sums = call(
+        early_sums, *far = call(
             functools.partial(early_sums_kernel, float((lists - 1) * cap)),
-            shape((words, width), F32),
+            [
+                shape((words, width), F32),
+                shape((subs * cap, width), F32),
+                shape((subs * cap, 128), F32),
+                shape((spaces, subs * cap), F32),
+            ],
             2_000_000_000,
             0,
             codes_t,
@@ -591,16 +604,14 @@
     rebuilt = exchange(rebuilt, "sub") if direct else [all_swap(rebuilt[0], "sub")]
     if direct:
         sums = call(
-            functools.partial(late_sums_kernel, float((lists - 1) * cap)),
+            late_sums_kernel,
             [shape((width // 128 * share + share * spaces // 128, 128), BF16)] * lists,
             1_000_000_000,
             1_000_000,
-            codes_t,
-            slot,
             pieces[-1],
             early_sums,
+            *far,
             tally,
-            *messages,
             rebuilt[1],
             loose=1,
             scratch=[pltpu.VMEM((words, width), F32)],

time: 45.5 us -> 45.3 us (level)
  no operation moved by 1% of the time
where the time goes in v9:
time: 45.3 us; the launch traced here: 45.1 us
  blocking collectives  13.8 us (30%)
  Pallas kernels  13.2 us (29%)
  starting transfers between devices  12.9 us (28%)
  waiting for transfers between devices  2.77 us (6%)
  local copies, waits for them, and re-layouts  1.62 us (4%)
  between operations  0.77 us (2%)
    all_to_all x1, blocking collectives, all_swap(): return lax.all_to_all(value, axis, split_axis=0, concat_axis=0, tiled=True)  13.8 us
    pallas_call x12, Pallas kernels, call(): pl.pallas_call(kernel, out_shape=out_shape, in_specs=[whole() for _ in ar...  13.2 us
    ppermute x12, starting transfers between devices, swap(): return lax.ppermute(value, axis, [(at, at ^ step) for at in range(count)])  12.9 us
    ppermute x12, waiting for transfers between devices, swap(): return lax.ppermute(value, axis, [(at, at ^ step) for at in range(count)])  2.77 us
    unnamed x14, local copies, waits for them, and re-layouts  1.62 us
  transfers between devices with their start and end apart: 12, of which 3 were waited for; matrix products, arithmetic and copies ran while one was open for 0% of the time, Pallas kernels for 20%

profile of v9, /device:TPU:0, one launch (start us, length us, event | category | flops | bytes accessed | tf_op | source)
XLA Modules:
  0.0 45.1 jit_solution(4201808457431594219)
XLA Ops:
  0.6 0.0 copy-start.5
  0.6 0.9 %copy-done.5 = s32[65536]{0:T(1024)S(1)} copy-done((s32[65536]{0:T(1024)S(1)}, s32[65536]{0:T(1024)}, u32[]{:S(2)}) %copy-start.5) | copy-done | bytes 262168
  1.6 0.0 copy-start.6
  1.6 0.7 %copy-done.6 = s32[128]{0:T(128)S(1)} copy-done((s32[128]{0:T(128)S(1)}, s32[128]{0:T(128)}, u32[]{:S(2)}) %copy-start.6) | copy-done | bytes 536
  2.2 0.0 copy-start
  2.2 0.4 shard_map.86
  2.7 13.8 %all_to_all.5 = s32[16,1,128]{2,1,0:T(1,128)S(1)} all-to-all(s32[16,1,128]{2,1,0:T(1,128)S(1)} %bitcast.8), channel_id=1, replica_groups=mesh['groups'=2,'lists'=4,'sub'=4] {'lists','sub'}, dimensions={0} | all-to-all | bytes 16384 | tf_op jit(solution)/shard_map/all_to_all | solution.py:461
  16.5 0.0 copy-done
  16.5 0.0 copy-start.1
  16.5 0.0 copy-start.2
  16.5 0.0 copy-start.4
  16.5 0.0 copy-start.3
  16.5 2.3 %shard_map.87 = (bf16[4,64,256]{2,1,0:T(8,128)(2,1)S(1)}, bf16[4,64,256]{2,1,0:T(8,128)(2,1)S(1)}, s32[16,64]{1,0:T(8,128)S(1)}, f32[64,128]{1,0:T(8,128)S(1)}) custom-call(s32[16,128]{1,0:T(8,128)S(1)} %bitcast.6, bf16[16384,256]{1,0:T(8,128)(2,1)S(1)} %copy-done), custom_call_target="tpu_custom_call" | custom-call | flops 600000000 | bytes 8388608 | tf_op jit(solution)/shard_map/pallas_call | solution.py:22
  18.9 0.6 %collective-permute-start = (bf16[4,64,256]{2,1,0:T(8,128)(2,1)S(1)}, bf16[4,64,256]{2,1,0:T(8,128)(2,1)S(1)}, u32[]{:S(2)}, u32[]{:S(2)}) collective-permute-start(bf16[4,64,256]{2,1,0:T(8,128)(2,1)S(1)} %get-tuple-element.34), channel_id=1, source_target_pairs={{0,4},{4,0},{8,12},{12,8},{1,5},{5,1},{9,13},{13,9},{2,6},{6,2},{1... | collective-permute-start | bytes 393224 | tf_op jit(solution)/shard_map/ppermute | solution.py:450
  19.4 0.6 %collective-permute-start.1 = (bf16[4,64,256]{2,1,0:T(8,128)(2,1)S(1)}, bf16[4,64,256]{2,1,0:T(8,128)(2,1)S(1)}, u32[]{:S(2)}, u32[]{:S(2)}) collective-permute-start(bf16[4,64,256]{2,1,0:T(8,128)(2,1)S(1)} %get-tuple-element.35), channel_id=1, source_target_pairs={{0,8},{4,12},{8,0},{12,4},{1,9},{5,13},{9,1},{13,5},{2,10},{6,14},... | collective-permute-start | bytes 393224 | tf_op jit(solution)/shard_map/ppermute | solution.py:450
  20.0 1.4 %shard_map.88 = (bf16[4,64,256]{2,1,0:T(8,128)(2,1)S(1)}, bf16[4,64,256]{2,1,0:T(8,128)(2,1)S(1)}) custom-call(f32[64,128]{1,0:T(8,128)S(1)} %get-tuple-element.31.spot_ref, bf16[16384,256]{1,0:T(8,128)(2,1)S(1)} %copy-done, s32[16,64]{1,0:T(8,128)S(1)} %get-tuple-element.32.scalar_ref), custom_call_target="tpu_custom_call" | custom-call | tf_op jit(solution)/shard_map/pallas_call | solution.py:22
  21.5 0.0 copy-done.1
  21.5 0.0 copy-done.2
  21.5 0.0 copy-done.4
  21.5 0.5 %shard_map.90 = (bf16[144,256]{1,0:T(8,128)(2,1)S(1)}, bf16[144,256]{1,0:T(8,128)(2,1)S(1)}, bf16[144,256]{1,0:T(8,128)(2,1)S(1)}, bf16[144,256]{1,0:T(8,128)(2,1)S(1)}) custom-call(bf16[128,1024]{1,0:T(8,128)(2,1)S(1)} %copy-done.2, bf16[1024,1024]{1,0:T(8,128)(2,1)S(1)} %copy-done.1, s32[128,128]{1,0:T(8,128)S(1)} %copy-done.4, ...), custom_call_target="tpu_custom_call" | custom-call | tf_op jit(solution)/shard_map/pallas_call | solution.py:22
  22.0 0.1 collective-permute-start.3
  22.1 0.6 %collective-permute-start.4 = (bf16[144,256]{1,0:T(8,128)(2,1)S(1)}, bf16[144,256]{1,0:T(8,128)(2,1)S(1)}, u32[]{:S(2)}, u32[]{:S(2)}) collective-permute-start(bf16[144,256]{1,0:T(8,128)(2,1)S(1)} %get-tuple-element.41), channel_id=1, source_target_pairs={{0,2},{1,3},{2,0},{3,1},{4,6},{5,7},{6,4},{7,5},{8,10},{9,11},{10,... | collective-permute-start | bytes 221192 | tf_op jit(solution)/shard_map/ppermute | solution.py:450
  22.7 1.2 %collective-permute-start.5 = (bf16[144,256]{1,0:T(8,128)(2,1)S(1)}, bf16[144,256]{1,0:T(8,128)(2,1)S(1)}, u32[]{:S(2)}, u32[]{:S(2)}) collective-permute-start(bf16[144,256]{1,0:T(8,128)(2,1)S(1)} %get-tuple-element.42), channel_id=1, source_target_pairs={{0,3},{1,2},{2,1},{3,0},{4,7},{5,6},{6,5},{7,4},{8,11},{9,10},{10,... | collective-permute-start | bytes 221192 | tf_op jit(solution)/shard_map/ppermute | solution.py:450
  23.9 0.0 collective-permute-done.3.refs_1_
  23.9 3.3 %collective-permute-start.2 = (bf16[4,64,256]{2,1,0:T(8,128)(2,1)S(1)}, bf16[4,64,256]{2,1,0:T(8,128)(2,1)S(1)}, u32[]{:S(2)}, u32[]{:S(2)}) collective-permute-start(bf16[4,64,256]{2,1,0:T(8,128)(2,1)S(1)} %get-tuple-element.38), channel_id=1, source_target_pairs={{0,12},{4,8},{8,4},{12,0},{1,13},{5,9},{9,5},{13,1},{2,14},{6,10},... | collective-permute-start | bytes 393224 | tf_op jit(solution)/shard_map/ppermute | solution.py:450
  27.2 0.0 collective-permute-done.4.refs_2_
  27.2 0.7 %collective-permute-done.5.refs_3_ = bf16[144,256]{1,0:T(8,128)(2,1)S(1)} collective-permute-done((bf16[144,256]{1,0:T(8,128)(2,1)S(1)}, bf16[144,256]{1,0:T(8,128)(2,1)S(1)}, u32[]{:S(2)}, u32[]{:S(2)}) %collective-permute-start.5) | collective-permute-done | bytes 73760 | tf_op jit(solution)/shard_map/ppermute | solution.py:450
  27.9 0.0 copy-done.3
  27.9 1.1 %shard_map.91 = (bf16[512,256]{1,0:T(8,128)(2,1)S(1)}, f32[32,512]{1,0:T(8,128)S(1)}, f32[16,512]{1,0:T(8,128)S(1)}) custom-call(bf16[32,2048]{1,0:T(8,128)(2,1)S(1)} %copy-done.3, bf16[144,256]{1,0:T(8,128)(2,1)S(1)} %get-tuple-element.39.refs_0_, bf16[144,256]{1,0:T(8,128)(2,1)S(1)} %collective-permute-done.3.refs_1_, ...), custom_call_target="tpu_custom_call" | custom-call | tf_op jit(solution)/shard_map/pallas_call | solution.py:22
  29.0 0.0 collective-permute-done.refs_1_
  29.0 0.0 collective-permute-done.1.refs_2_
  29.0 0.5 %shard_map.89 = (f32[128,128]{1,0:T(8,128)S(1)}, bf16[512,256]{1,0:T(8,128)(2,1)S(1)}) custom-call(s32[16,128]{1,0:T(8,128)S(1)} %bitcast.7, bf16[4,64,256]{2,1,0:T(8,128)(2,1)S(1)} %get-tuple-element.33.refs_0_.after_ref, bf16[4,64,256]{2,1,0:T(8,128)(2,1)S(1)} %collective-permute-done.refs_1_, bf16[4,64,256]{2,1,0:T(8,128)(2,1)S(1)} %collective-permute-done.1.refs_2_), custom_call_target="tpu_custom_call" | custom-call | flops 3000000000 | tf_op jit(solution)/shard_map/pallas_call | solution.py:22
  29.6 2.6 %shard_map.92 = (f32[256,256]{1,0:T(8,128)S(1)}, f32[256,256]{1,0:T(8,128)S(1)}, f32[256,128]{1,0:T(8,128)S(1)}, f32[32,256]{1,0:T(8,128)S(1)}) custom-call(f32[32,512]{1,0:T(8,128)S(1)} %get-tuple-element.43.codes_ref, f32[128,128]{1,0:T(8,128)S(1)} %get-tuple-element.36.slot_ref, bf16[512,256]{1,0:T(8,128)(2,1)S(1)} %get-tuple-element.37.centre_ref.part_ref, ...), custom_call_target="tpu_custom_call" | custom-call | flops 2000000000 | tf_op jit(solution)/shard_map/pallas_call | solution.py:22
  32.1 0.0 collective-permute-done.2.piece_ref
  32.2 0.3 shard_map.93.centre_ref
  32.5 0.1 shard_map.94
  32.5 0.6 %collective-permute-start.6 = (bf16[128,256]{1,0:T(8,128)(2,1)S(1)}, bf16[128,256]{1,0:T(8,128)(2,1)S(1)}, u32[]{:S(2)}, u32[]{:S(2)}) collective-permute-start(bf16[128,256]{1,0:T(8,128)(2,1)S(1)} %get-tuple-element.47), channel_id=1, source_target_pairs={{0,1},{1,0},{2,3},{3,2},{4,5},{5,4},{6,7},{7,6},{8,9},{9,8},{10,11... | collective-permute-start | bytes 196616 | tf_op jit(solution)/shard_map/ppermute | solution.py:450
  33.2 0.6 %collective-permute-start.7 = (bf16[128,256]{1,0:T(8,128)(2,1)S(1)}, bf16[128,256]{1,0:T(8,128)(2,1)S(1)}, u32[]{:S(2)}, u32[]{:S(2)}) collective-permute-start(bf16[128,256]{1,0:T(8,128)(2,1)S(1)} %get-tuple-element.48), channel_id=1, source_target_pairs={{0,2},{1,3},{2,0},{3,1},{4,6},{5,7},{6,4},{7,5},{8,10},{9,11},{10,... | collective-permute-start | bytes 196616 | tf_op jit(solution)/shard_map/ppermute | solution.py:450
  33.7 0.9 %collective-permute-start.8 = (bf16[128,256]{1,0:T(8,128)(2,1)S(1)}, bf16[128,256]{1,0:T(8,128)(2,1)S(1)}, u32[]{:S(2)}, u32[]{:S(2)}) collective-permute-start(bf16[128,256]{1,0:T(8,128)(2,1)S(1)} %get-tuple-element.49), channel_id=1, source_target_pairs={{0,3},{1,2},{2,1},{3,0},{4,7},{5,6},{6,5},{7,4},{8,11},{9,10},{10,... | collective-permute-start | bytes 196616 | tf_op jit(solution)/shard_map/ppermute | solution.py:450
  34.6 0.0 collective-permute-done.6.refs_0_.refs_1_
  34.6 1.3 %shard_map.95 = (bf16[144,128]{1,0:T(8,128)(2,1)S(1)}, bf16[144,128]{1,0:T(8,128)(2,1)S(1)}, bf16[144,128]{1,0:T(8,128)(2,1)S(1)}, bf16[144,128]{1,0:T(8,128)(2,1)S(1)}) custom-call(bf16[4,64,256]{2,1,0:T(8,128)(2,1)S(1)} %collective-permute-done.2.piece_ref, f32[256,256]{1,0:T(8,128)S(1)} %get-tuple-element.44.after_ref.early_ref, ...), custom_call_target="tpu_custom_call" | custom-call | flops 1000000000 | bytes 1000000 | tf_op jit(solution)/shard_map/pallas_call | solution.py:22
  35.9 3.2 %collective-permute-start.9 = (bf16[144,128]{1,0:T(8,128)(2,1)S(1)}, bf16[144,128]{1,0:T(8,128)(2,1)S(1)}, u32[]{:S(2)}, u32[]{:S(2)}) collective-permute-start(bf16[144,128]{1,0:T(8,128)(2,1)S(1)} %get-tuple-element.54), channel_id=1, source_target_pairs={{0,12},{4,8},{8,4},{12,0},{1,13},{5,9},{9,5},{13,1},{2,14},{6,10},... | collective-permute-start | bytes 110600 | tf_op jit(solution)/shard_map/ppermute | solution.py:450
  39.1 0.0 collective-permute-start.10
  39.2 1.2 %collective-permute-start.11 = (bf16[144,128]{1,0:T(8,128)(2,1)S(1)}, bf16[144,128]{1,0:T(8,128)(2,1)S(1)}, u32[]{:S(2)}, u32[]{:S(2)}) collective-permute-start(bf16[144,128]{1,0:T(8,128)(2,1)S(1)} %get-tuple-element.58), channel_id=1, source_target_pairs={{0,8},{4,12},{8,0},{12,4},{1,9},{5,13},{9,1},{13,5},{2,10},{6,14},... | collective-permute-start | bytes 110600 | tf_op jit(solution)/shard_map/ppermute | solution.py:450
  40.4 0.0 collective-permute-done.7.refs_2_
  40.4 0.0 collective-permute-done.8.refs_3_
  40.4 1.8 %collective-permute-done.9.refs_4_.refs_3_ = bf16[144,128]{1,0:T(8,128)(2,1)S(1)} collective-permute-done((bf16[144,128]{1,0:T(8,128)(2,1)S(1)}, bf16[144,128]{1,0:T(8,128)(2,1)S(1)}, u32[]{:S(2)}, u32[]{:S(2)}) %collective-permute-start.9) | collective-permute-done | bytes 36896 | tf_op jit(solution)/shard_map/ppermute | solution.py:450
  42.2 1.5 %shard_map.96 = (bf16[128,1024]{1,0:T(8,128)(2,1)}, f32[8,128]{1,0:T(8,128)S(1)}) custom-call(bf16[128,1024]{1,0:T(8,128)(2,1)S(1)} %copy-done.2, bf16[1024,1024]{1,0:T(8,128)(2,1)S(1)} %copy-done.1, bf16[128,256]{1,0:T(8,128)(2,1)S(1)} %get-tuple-element.46.refs_0_, bf16[128,256]{1,0:T(8,128)(2,1)S(1)} %collective-permute-done.6.refs_0_.refs_1_, ...), custom_call_target="tpu_custom_call" | custom-call | flops 1000 | bytes 1000 | tf_op jit(solution)/shard_map/pallas_call | solution.py:22
  43.7 0.0 collective-permute-done.10.refs_1_
  43.7 0.3 collective-permute-done.11.refs_2_
  44.0 1.1 %shard_map.97 = f32[32,512]{1,0:T(8,128)} custom-call(bf16[32,2048]{1,0:T(8,128)(2,1)S(1)} %copy-done.3, bf16[144,128]{1,0:T(8,128)(2,1)S(1)} %get-tuple-element.56.refs_0_, bf16[144,128]{1,0:T(8,128)(2,1)S(1)} %collective-permute-done.10.refs_1_, bf16[144,128]{1,0:T(8,128)(2,1)S(1)} %collective-permute-done.11.refs_2_, ...), custom_call_target="tpu_custom_call" | custom-call | flops 100000000 | bytes 500000 | tf_op jit(solution)/shard_map/pallas_call | solution.py:22
Async XLA Ops:
  0.6 1.0 %copy-start.5 = (s32[65536]{0:T(1024)S(1)}, s32[65536]{0:T(1024)}, u32[]{:S(2)}) copy-start(s32[65536]{0:T(1024)} %param.10) | copy-start | bytes 786436
  1.6 0.7 %copy-start.6 = (s32[128]{0:T(128)S(1)}, s32[128]{0:T(128)}, u32[]{:S(2)}) copy-start(s32[128]{0:T(128)} %param.11) | copy-start | bytes 1540
  2.2 14.3 %copy-start = (bf16[16384,256]{1,0:T(8,128)(2,1)S(1)}, bf16[16384,256]{1,0:T(8,128)(2,1)}, u32[]{:S(2)}) copy-start(bf16[16384,256]{1,0:T(8,128)(2,1)} %centroids_ref.3) | copy-start | bytes 25165828
  16.5 5.0 %copy-start.1 = (bf16[1024,1024]{1,0:T(8,128)(2,1)S(1)}, bf16[1024,1024]{1,0:T(8,128)(2,1)}, u32[]{:S(2)}) copy-start(bf16[1024,1024]{1,0:T(8,128)(2,1)} %rotation_ref.3) | copy-start | bytes 6291460
  16.5 5.0 %copy-start.2 = (bf16[128,1024]{1,0:T(8,128)(2,1)S(1)}, bf16[128,1024]{1,0:T(8,128)(2,1)}, u32[]{:S(2)}) copy-start(bf16[128,1024]{1,0:T(8,128)(2,1)} %passages_ref.3) | copy-start | bytes 786436
  16.5 5.0 %copy-start.4 = (s32[128,128]{1,0:T(8,128)S(1)}, s32[128,128]{1,0:T(8,128)}, u32[]{:S(2)}) copy-start(s32[128,128]{1,0:T(8,128)} %codes_ref.1) | copy-start | bytes 196612
  16.5 11.4 %copy-start.3 = (bf16[32,2048]{1,0:T(8,128)(2,1)S(1)}, bf16[32,2048]{1,0:T(8,128)(2,1)}, u32[]{:S(2)}) copy-start(bf16[32,2048]{1,0:T(8,128)(2,1)} %codebook_ref.3) | copy-start | bytes 393220
  18.9 10.2 %collective-permute-start = (bf16[4,64,256]{2,1,0:T(8,128)(2,1)S(1)}, bf16[4,64,256]{2,1,0:T(8,128)(2,1)S(1)}, u32[]{:S(2)}, u32[]{:S(2)}) collective-permute-start(bf16[4,64,256]{2,1,0:T(8,128)(2,1)S(1)} %get-tuple-element.34), channel_id=1, source_target_pairs={{0,4},{4,0},{8,12},{12,8},{1,5},{5,1},{9,13},{13,9},{2,6},{6,2},{1... | collective-permute-start | bytes 393224 | tf_op jit(solution)/shard_map/ppermute | solution.py:450
  19.4 9.6 %collective-permute-start.1 = (bf16[4,64,256]{2,1,0:T(8,128)(2,1)S(1)}, bf16[4,64,256]{2,1,0:T(8,128)(2,1)S(1)}, u32[]{:S(2)}, u32[]{:S(2)}) collective-permute-start(bf16[4,64,256]{2,1,0:T(8,128)(2,1)S(1)} %get-tuple-element.35), channel_id=1, source_target_pairs={{0,8},{4,12},{8,0},{12,4},{1,9},{5,13},{9,1},{13,5},{2,10},{6,14},... | collective-permute-start | bytes 393224 | tf_op jit(solution)/shard_map/ppermute | solution.py:450
  22.0 1.9 %collective-permute-start.3 = (bf16[144,256]{1,0:T(8,128)(2,1)S(1)}, bf16[144,256]{1,0:T(8,128)(2,1)S(1)}, u32[]{:S(2)}, u32[]{:S(2)}) collective-permute-start(bf16[144,256]{1,0:T(8,128)(2,1)S(1)} %get-tuple-element.40), channel_id=1, source_target_pairs={{0,1},{1,0},{2,3},{3,2},{4,5},{5,4},{6,7},{7,6},{8,9},{9,8},{10,11... | collective-permute-start | bytes 221192 | tf_op jit(solution)/shard_map/ppermute | solution.py:450
  22.1 5.1 %collective-permute-start.4 = (bf16[144,256]{1,0:T(8,128)(2,1)S(1)}, bf16[144,256]{1,0:T(8,128)(2,1)S(1)}, u32[]{:S(2)}, u32[]{:S(2)}) collective-permute-start(bf16[144,256]{1,0:T(8,128)(2,1)S(1)} %get-tuple-element.41), channel_id=1, source_target_pairs={{0,2},{1,3},{2,0},{3,1},{4,6},{5,7},{6,4},{7,5},{8,10},{9,11},{10,... | collective-permute-start | bytes 221192 | tf_op jit(solution)/shard_map/ppermute | solution.py:450
  22.7 5.2 %collective-permute-start.5 = (bf16[144,256]{1,0:T(8,128)(2,1)S(1)}, bf16[144,256]{1,0:T(8,128)(2,1)S(1)}, u32[]{:S(2)}, u32[]{:S(2)}) collective-permute-start(bf16[144,256]{1,0:T(8,128)(2,1)S(1)} %get-tuple-element.42), channel_id=1, source_target_pairs={{0,3},{1,2},{2,1},{3,0},{4,7},{5,6},{6,5},{7,4},{8,11},{9,10},{10,... | collective-permute-start | bytes 221192 | tf_op jit(solution)/shard_map/ppermute | solution.py:450
  23.9 8.2 %collective-permute-start.2 = (bf16[4,64,256]{2,1,0:T(8,128)(2,1)S(1)}, bf16[4,64,256]{2,1,0:T(8,128)(2,1)S(1)}, u32[]{:S(2)}, u32[]{:S(2)}) collective-permute-start(bf16[4,64,256]{2,1,0:T(8,128)(2,1)S(1)} %get-tuple-element.38), channel_id=1, source_target_pairs={{0,12},{4,8},{8,4},{12,0},{1,13},{5,9},{9,5},{13,1},{2,14},{6,10},... | collective-permute-start | bytes 393224 | tf_op jit(solution)/shard_map/ppermute | solution.py:450
  32.5 2.1 %collective-permute-start.6 = (bf16[128,256]{1,0:T(8,128)(2,1)S(1)}, bf16[128,256]{1,0:T(8,128)(2,1)S(1)}, u32[]{:S(2)}, u32[]{:S(2)}) collective-permute-start(bf16[128,256]{1,0:T(8,128)(2,1)S(1)} %get-tuple-element.47), channel_id=1, source_target_pairs={{0,1},{1,0},{2,3},{3,2},{4,5},{5,4},{6,7},{7,6},{8,9},{9,8},{10,11... | collective-permute-start | bytes 196616 | tf_op jit(solution)/shard_map/ppermute | solution.py:450
  33.2 7.2 %collective-permute-start.7 = (bf16[128,256]{1,0:T(8,128)(2,1)S(1)}, bf16[128,256]{1,0:T(8,128)(2,1)S(1)}, u32[]{:S(2)}, u32[]{:S(2)}) collective-permute-start(bf16[128,256]{1,0:T(8,128)(2,1)S(1)} %get-tuple-element.48), channel_id=1, source_target_pairs={{0,2},{1,3},{2,0},{3,1},{4,6},{5,7},{6,4},{7,5},{8,10},{9,11},{10,... | collective-permute-start | bytes 196616 | tf_op jit(solution)/shard_map/ppermute | solution.py:450
  33.7 6.7 %collective-permute-start.8 = (bf16[128,256]{1,0:T(8,128)(2,1)S(1)}, bf16[128,256]{1,0:T(8,128)(2,1)S(1)}, u32[]{:S(2)}, u32[]{:S(2)}) collective-permute-start(bf16[128,256]{1,0:T(8,128)(2,1)S(1)} %get-tuple-element.49), channel_id=1, source_target_pairs={{0,3},{1,2},{2,1},{3,0},{4,7},{5,6},{6,5},{7,4},{8,11},{9,10},{10,... | collective-permute-start | bytes 196616 | tf_op jit(solution)/shard_map/ppermute | solution.py:450
  35.9 6.2 %collective-permute-start.9 = (bf16[144,128]{1,0:T(8,128)(2,1)S(1)}, bf16[144,128]{1,0:T(8,128)(2,1)S(1)}, u32[]{:S(2)}, u32[]{:S(2)}) collective-permute-start(bf16[144,128]{1,0:T(8,128)(2,1)S(1)} %get-tuple-element.54), channel_id=1, source_target_pairs={{0,12},{4,8},{8,4},{12,0},{1,13},{5,9},{9,5},{13,1},{2,14},{6,10},... | collective-permute-start | bytes 110600 | tf_op jit(solution)/shard_map/ppermute | solution.py:450
  39.1 4.5 %collective-permute-start.10 = (bf16[144,128]{1,0:T(8,128)(2,1)S(1)}, bf16[144,128]{1,0:T(8,128)(2,1)S(1)}, u32[]{:S(2)}, u32[]{:S(2)}) collective-permute-start(bf16[144,128]{1,0:T(8,128)(2,1)S(1)} %get-tuple-element.57), channel_id=1, source_target_pairs={{0,4},{4,0},{8,12},{12,8},{1,5},{5,1},{9,13},{13,9},{2,6},{6,2},{1... | collective-permute-start | bytes 110600 | tf_op jit(solution)/shard_map/ppermute | solution.py:450
  39.2 4.9 %collective-permute-start.11 = (bf16[144,128]{1,0:T(8,128)(2,1)S(1)}, bf16[144,128]{1,0:T(8,128)(2,1)S(1)}, u32[]{:S(2)}, u32[]{:S(2)}) collective-permute-start(bf16[144,128]{1,0:T(8,128)(2,1)S(1)} %get-tuple-element.58), channel_id=1, source_target_pairs={{0,8},{4,12},{8,0},{12,4},{1,9},{5,13},{9,1},{13,5},{2,10},{6,14},... | collective-permute-start | bytes 110600 | tf_op jit(solution)/shard_map/ppermute | solution.py:450
